TPU v7x, 256 devices: a whole 4x4x8 slice. The times are simulated.
256 devices in a mesh: ctx: 32 (over z, y), tp: 8 (over x, core).
Axes of the slice: x: 4, y: 4, z: 8, core: 2. Of those that a mesh axis runs over, the one named last changes fastest.
Arguments:
- projected: bfloat16 [3, 8192, 4096], P(None, 'ctx', 'tp'), may hold values from -6 to 6
- short_taps: float32 [3, 7, 4096], P(None, None, 'tp'), may hold values from -2 to 2
- pole_decay: float32 [8, 4096], P(None, 'tp'), as said below
- residues: float32 [8, 4096], P(None, 'tp'), may hold values from -2 to 2
- doc_lengths: int32 [16], replicated, may hold values from 1 to 4096, 8192 in all
- cotangent: bfloat16 [8192, 4096], P('ctx', 'tp'), may hold values from -6 to 6
Outputs:
- gated_out: bfloat16 [8192, 4096], P('ctx', 'tp')
- grad_projected: bfloat16 [3, 8192, 4096], P(None, 'ctx', 'tp')
- grad_taps: float32 [3, 7, 4096], P(None, None, 'tp')
- grad_residues: float32 [8, 4096], P(None, 'tp')
Inputs may be any that keep to these rules, and one draw needn't show every extreme that they name: `pole_decay`: each entry lies strictly between 0 and 1. `doc_lengths`: the lengths sum to 8192.
All inputs are finite; a program needn't handle non-finite values.
Results may differ from a plain program's by a relative error of at most 0.023.
Values may be sent and summed in bfloat16 or wider, within the bound.
No kernel may reach another device: no remote copies, remote signals or barrier semaphores. Data moves between devices by JAX's collectives and lax.ppermute only.
A program may use at most 128 MiB of HBM per device.

v0:
```python
import math

import jax
import jax.numpy as jnp
from jax import lax
from jax.sharding import PartitionSpec as P


def from_behind(block, axis, distance):
    devices = range(lax.axis_size(axis))
    route = [(i - distance, i) for i in devices if i - distance in devices]
    return lax.ppermute(block, axis, route)


def doc_of(positions, doc_lengths):
    end_rows = jnp.cumsum(doc_lengths)
    counted = jnp.sum((positions[:, None] >= end_rows[None, :]).astype(jnp.int32), axis=1)
    return jnp.where(positions < 0, -1, counted)


def featurize(extended, short_taps, ext_docs):
    tap_span = short_taps.shape[1] - 1
    row_count = extended.shape[1] - tap_span
    own_docs = ext_docs[tap_span:]
    running = jnp.zeros((extended.shape[0], row_count, extended.shape[2]), jnp.float32)
    for tap_lag in range(tap_span + 1):
        same_doc = (
            ext_docs[tap_span - tap_lag : tap_span - tap_lag + row_count] == own_docs
        ).astype(jnp.float32)
        moved = extended[:, tap_span - tap_lag : tap_span - tap_lag + row_count, :].astype(
            jnp.float32
        )
        running = running + short_taps[:, tap_lag, None, :] * moved * same_doc[None, :, None]
    return running


def unfeaturize(extended_grads, short_taps, ext_docs):
    tap_span = short_taps.shape[1] - 1
    row_count = extended_grads.shape[1] - tap_span
    own_docs = ext_docs[:row_count]
    running = jnp.zeros((extended_grads.shape[0], row_count, extended_grads.shape[2]), jnp.float32)
    for tap_lag in range(tap_span + 1):
        same_doc = (ext_docs[tap_lag : tap_lag + row_count] == own_docs).astype(jnp.float32)
        running = (
            running
            + short_taps[:, tap_lag, None, :]
            * extended_grads[:, tap_lag : tap_lag + row_count, :]
            * same_doc[None, :, None]
        )
    return running


def tap_grads(grad_feats, extended, ext_docs):
    tap_span = extended.shape[1] - grad_feats.shape[1]
    row_count = grad_feats.shape[1]
    own_docs = ext_docs[tap_span:]
    pieces = []
    for tap_lag in range(tap_span + 1):
        same_doc = (
            ext_docs[tap_span - tap_lag : tap_span - tap_lag + row_count] == own_docs
        ).astype(jnp.float32)
        moved = extended[:, tap_span - tap_lag : tap_span - tap_lag + row_count, :].astype(
            jnp.float32
        )
        pieces.append(jnp.sum(grad_feats * moved * same_doc[None, :, None], axis=1))
    return jnp.stack(pieces, axis=1)


def compose(earlier, later):
    return (earlier[0] * later[0], earlier[1] * later[0] + later[1])


def stretch_summary(carried, pole_decay, doc_ids, doc_before, block_rows):
    row_count, chan_count = carried.shape
    mode_count = pole_decay.shape[0]
    stretch_count = row_count // block_rows
    offsets = jnp.arange(block_rows, dtype=jnp.float32)
    rising = pole_decay[None] ** offsets[:, None, None]
    falling = pole_decay[None] ** (-offsets[:, None, None])
    weighted = (
        carried.reshape(stretch_count, block_rows, 1, chan_count).astype(jnp.float32)
        * falling[None]
    )
    stretch_docs = doc_ids.reshape(stretch_count, block_rows)
    shifted = jnp.concatenate([jnp.reshape(doc_before, (1,)), doc_ids[:-1]])
    before = shifted[::block_rows]
    lower_mask = offsets[:, None] >= offsets[None, :]
    doc_mask = jnp.logical_and(
        lower_mask[None], stretch_docs[:, :, None] == stretch_docs[:, None, :]
    ).astype(jnp.float32)
    inner_sums = jnp.einsum(
        "jts,jsx->jtx",
        doc_mask,
        weighted.reshape(stretch_count, block_rows, mode_count * chan_count),
        precision=lax.Precision.HIGHEST,
    )
    inner_sums = inner_sums.reshape(stretch_count, block_rows, mode_count, chan_count)
    keep_mask = (stretch_docs == before[:, None]).astype(jnp.float32)
    end_states = pole_decay ** (block_rows - 1) * inner_sums[:, -1]
    pass_factors = pole_decay**block_rows * keep_mask[:, -1, None, None]
    factors, states = lax.associative_scan(compose, (pass_factors, end_states), axis=0)
    return (inner_sums, keep_mask, rising, factors, states)


def finish(summary, pole_decay, carry_in):
    inner_sums, keep_mask, rising, factors, states = summary
    prior_state = jnp.concatenate(
        [carry_in[None], states[:-1] + factors[:-1] * carry_in[None]], axis=0
    )
    mode_terms = rising[None] * (
        inner_sums + pole_decay * keep_mask[:, :, None, None] * prior_state[:, None]
    )
    return mode_terms.reshape(-1, mode_terms.shape[2], mode_terms.shape[3])


def per_device(projected, short_taps, pole_decay, residues, doc_lengths, cotangent):
    row_count = projected.shape[1]
    chan_count = projected.shape[2]
    tap_span = short_taps.shape[1] - 1
    shards = lax.axis_size("ctx")
    total_rows = row_count * shards
    start_row = lax.axis_index("ctx") * row_count
    left_rim = from_behind(projected[:, row_count - tap_span :, :], "ctx", 1)
    extended = jnp.concatenate([left_rim, projected], axis=1)
    lead_docs = doc_of(
        start_row - tap_span + jnp.arange(row_count + tap_span, dtype=jnp.int32), doc_lengths
    )
    tail_docs = doc_of(start_row + jnp.arange(row_count + tap_span, dtype=jnp.int32), doc_lengths)
    features = featurize(extended, short_taps, lead_docs)
    carried = (features[1] * features[2]).astype(jnp.bfloat16)
    shrink = jnp.sqrt(1.0 - pole_decay * pole_decay)
    mode_coef = residues * shrink
    grad_scale = 1.0 / math.sqrt(total_rows)
    cot_float = cotangent.astype(jnp.float32)
    grad_long = (cot_float * features[0]).astype(jnp.bfloat16)
    owned_cols = chan_count // shards
    lead_col = lax.axis_index("ctx") * owned_cols
    own_decay = lax.dynamic_slice_in_dim(pole_decay, lead_col, owned_cols, 1)
    own_coef = lax.dynamic_slice_in_dim(mode_coef, lead_col, owned_cols, 1)
    own_shrink = lax.dynamic_slice_in_dim(shrink, lead_col, owned_cols, 1)
    all_docs = doc_of(jnp.arange(total_rows, dtype=jnp.int32), doc_lengths)
    block_rows = min(128, total_rows)
    owned = lax.all_to_all(carried, "ctx", split_axis=1, concat_axis=0, tiled=True)
    no_doc = jnp.int32(-1)
    carry_zero = jnp.zeros(own_decay.shape, jnp.float32)
    mode_terms = finish(
        stretch_summary(owned, own_decay, all_docs, no_doc, block_rows), own_decay, carry_zero
    )
    owned_out = jnp.sum(mode_terms * own_coef[None], axis=1).astype(jnp.bfloat16)
    long_out = lax.all_to_all(owned_out, "ctx", split_axis=0, concat_axis=1, tiled=True)
    owned_grad = lax.all_to_all(grad_long, "ctx", split_axis=1, concat_axis=0, tiled=True)
    back_terms = finish(
        stretch_summary(owned_grad[::-1], own_decay, all_docs[::-1], no_doc, block_rows),
        own_decay,
        carry_zero,
    )
    owned_back = jnp.sum(back_terms * own_coef[None], axis=1)[::-1].astype(jnp.bfloat16)
    res_part = (
        own_shrink
        * jnp.einsum(
            "nmc,nc->mc",
            back_terms,
            owned[::-1].astype(jnp.float32),
            precision=lax.Precision.HIGHEST,
        )
        * grad_scale
    )
    grad_carried = lax.all_to_all(owned_back, "ctx", split_axis=0, concat_axis=1, tiled=True)
    grad_res = lax.all_gather(res_part, "ctx", axis=1, tiled=True)
    gated_out = (features[0] * long_out.astype(jnp.float32)).astype(jnp.bfloat16)
    grad_q = cot_float * long_out.astype(jnp.float32)
    carried_float = grad_carried.astype(jnp.float32)
    grad_feats = jnp.stack([grad_q, carried_float * features[2], carried_float * features[1]])
    right_rim = from_behind(grad_feats[:, :tap_span, :].astype(jnp.bfloat16), "ctx", -1).astype(
        jnp.float32
    )
    grad_proj = unfeaturize(
        jnp.concatenate([grad_feats, right_rim], axis=1), short_taps, tail_docs
    ).astype(jnp.bfloat16)
    tap_part = tap_grads(grad_feats, extended, lead_docs) * grad_scale
    grad_tap = lax.psum(tap_part.astype(jnp.bfloat16), "ctx").astype(jnp.float32)
    return (gated_out, grad_proj, grad_tap, grad_res)


def solution(mesh):
    placed = (
        P(None, "ctx", "tp"),
        P(None, None, "tp"),
        P(None, "tp"),
        P(None, "tp"),
        P(),
        P("ctx", "tp"),
    )
    return jax.shard_map(
        per_device,
        mesh=mesh,
        in_specs=placed,
        out_specs=(P("ctx", "tp"), P(None, "ctx", "tp"), P(None, None, "tp"), P(None, "tp")),
        check_vma=False,
    )
```

profile of v0, /device:TPU:2, one launch (start us, length us, event | category | flops | bytes accessed | tf_op | source)
XLA Modules:
  0.0 505.4 jit_solution(7023584393655365384)
XLA Ops:
  1.7 3.5 collective-permute-start
  7.7 1.4 fusion.80
  9.8 1.4 subtract_sqrt_fusion
  12.5 1.2 fusion.85
  15.9 3.8 fusion.25
  20.6 11.3 %all-to-all-start = ((bf16[256,32,16]{0,2,1:T(8,128)(2,1)}), bf16[256,32,16]{0,2,1:T(8,128)(2,1)S(1)}, u32[]{:S(2)}, u32[]{:S(2)}) async-start(bf16[256,32,16]{0,2,1:T(8,128)(2,1)} %bitcast.3), calls=%async_computation | async-start | bytes 524288 | tf_op jit(solution)/shard_map/all_to_all | solution.py:143
  33.0 11.5 %all-to-all-done = bf16[256,32,16]{0,2,1:T(8,128)(2,1)S(1)} async-done(((bf16[256,32,16]{0,2,1:T(8,128)(2,1)}), bf16[256,32,16]{0,2,1:T(8,128)(2,1)S(1)}, u32[]{:S(2)}, u32[]{:S(2)}) %all-to-all-start) | async-done | bytes 262176 | tf_op jit(solution)/shard_map/all_to_all | solution.py:143
  44.5 4.8 all-to-all-start.2
  49.4 1.2 slice.550
  50.6 1.2 slice.554
  51.8 1.2 slice.589
  53.0 1.2 slice.611
  54.3 1.2 slice.615
  55.5 1.2 slice.650
  56.7 2.3 mul.731
  59.0 5.0 mul.864
  65.8 21.3 %rev.13 = bf16[8192,16]{0,1:T(8,128)(2,1)} reverse(bf16[8192,16]{0,1:T(8,128)(2,1)S(1)} %bitcast.165), dimensions={0} | reverse | bytes 524288 | tf_op jit(solution)/shard_map/rev | solution.py:153
  88.1 3.4 bitcast_multiply_fusion.1
  91.4 4.5 fusion.8
  96.0 2.0 copy-done
  98.0 3.1 slice.732
  101.1 3.7 copy.139
  104.7 6.3 %fusion.11 = f32[64,128,128]{1,2,0:T(8,128)S(1)} fusion(f32[64,128,128]{1,2,0:T(8,128)} %get-tuple-element.63, s32[64,128]{1,0:T(8,128)S(1)} %bitcast.164, pred[128,128]{1,0:T(8,128)(4,1)S(1)} %iota_compare_fusion.1), kind=kOutput, calls=%fused_computation.16 | convolution fusion | flops 1612709888 | bytes 8437760 | tf_op jit(solution)/shard_map/jts,jsx->jtx/dot_general | solution.py:91
  111.1 2.1 copy-done.1
  113.1 3.1 slice.693
  116.2 4.1 copy.138
  132.3 1.2 slice.590
  149.5 1.2 slice.651
  150.7 6.8 %copy.123 = f32[64,128,128]{1,0,2:T(8,128)} copy(f32[64,128,128]{1,2,0:T(8,128)} %copy-done) | data formatting | bytes 8388608 | tf_op jit(solution)/shard_map/jts,jsx->jtx/dot_general | solution.py:91
  158.2 3.1 pad.164
  161.9 3.2 pad.153
  165.0 1.6 pad_maximum_fusion.3
  166.6 3.1 pad.152
  171.0 1.5 fusion.74
  173.2 3.2 pad.167
  177.9 3.2 pad.155
  181.1 1.5 fusion.73
  187.1 1.5 fusion.72
  190.3 3.7 pad.460
  195.7 3.3 pad.159
  199.7 5.2 %pad.461 = f32[64,8,16]{0,2,1:T(8,128)} pad(f32[32,8,16]{0,2,1:T(8,128)} %add.343, f32[]{:T(128)} %constant.39.clone.1), padding=1_0_1x0_0_0x0_0_0 | pad | bytes 49156
  204.8 1.5 fusion.71
  206.4 1.1 pad.257
  222.2 1.1 pad.462
  225.0 1.1 pad.463
  228.5 2.6 mul.824
  231.2 5.0 mul.868
  236.2 5.0 reshape.227
  241.2 5.1 %rev.15 = bf16[8192,16]{0,1:T(8,128)(2,1)S(1)} reverse(bf16[8192,16]{0,1:T(8,128)(2,1)S(1)} %bitcast.166), dimensions={0} | reverse | bytes 524288 | tf_op jit(solution)/shard_map/rev | solution.py:163
  246.4 5.6 %add_multiply_fusion = f32[8192,8,16]{0,2,1:T(8,128)S(1)} fusion(f32[8192,8,16]{0,2,1:T(8,128)} %mul.864, f32[8192,8,16]{0,2,1:T(8,128)} %reshape.227, f32[8192,8,16]{0,2,1:T(8,128)} %mul.868, f32[8192]{0:T(1024)S(1)} %copy-done.37, f32[8,16]{1,0:T(8,128)S(1)} %copy-done.36), kind=kLoop, calls=%fused_computation.12 | loop fusion | flops 4194304 | bytes 16810496 | tf_op jit(solution)/shard_map/mul | solution.py:110
  252.0 6.2 %fusion = f32[16,1,8]{2,1,0:T(1,128)S(1)} fusion(f32[8192,8,16]{0,2,1:T(8,128)S(1)} %add_multiply_fusion, bf16[8192,16,1]{0,1,2:T(8,128)(2,1)S(1)} %bitcast.171), kind=kOutput, calls=%fused_computation.2 | convolution fusion | flops 12582912 | bytes 4456960 | tf_op jit(solution)/shard_map/nmc,nc->mc/dot_general | solution.py:160
  259.1 10.3 %fusion.4 = (bf16[64,128,16]{1,0,2:T(8,128)(2,1)S(1)}, bf16[64,128,16]{1,0,2:T(8,128)(2,1)S(1)}) fusion(f32[64,128,8,16]{1,3,2,0:T(8,128)} %bitcast.143, f32[64,8,16]{0,2,1:T(8,128)S(1)} %concatenate.102, f32[64,128]{1,0:T(8,128)S(1)} %copy-done.12, f32[8,16]{1,0:T(8,128)S(1)} %get-tuple-element.101, f32[8,16]{1,0:T(8,128)S(1)} %copy-done.36, ...), kind=kLoop, calls=%fused_computation.7 | loop fusion | flops 12320768 | bytes 9110528 | tf_op jit(solution)/shard_map/reduce_sum | solution.py:157
  269.6 5.1 %rev.14 = bf16[8192,16]{0,1:T(8,128)(2,1)S(1)} reverse(bf16[8192,16]{0,1:T(8,128)(2,1)S(1)} %bitcast.167), dimensions={0} | reverse | bytes 524288 | tf_op jit(solution)/shard_map/rev | solution.py:157
  275.4 9.9 %all-to-all-start.3 = ((bf16[32,256,16]{1,2,0:T(8,128)(2,1)}), bf16[32,256,16]{1,2,0:T(8,128)(2,1)S(1)}, u32[]{:S(2)}, u32[]{:S(2)}) async-start(bf16[32,256,16]{1,2,0:T(8,128)(2,1)} %bitcast.123), calls=%async_computation.3 | async-start | bytes 524288 | tf_op jit(solution)/shard_map/all_to_all | solution.py:168
  286.3 10.9 %all-to-all-done.3 = bf16[32,256,16]{1,2,0:T(8,128)(2,1)S(1)} async-done(((bf16[32,256,16]{1,2,0:T(8,128)(2,1)}), bf16[32,256,16]{1,2,0:T(8,128)(2,1)S(1)}, u32[]{:S(2)}, u32[]{:S(2)}) %all-to-all-start.3) | async-done | bytes 262176 | tf_op jit(solution)/shard_map/all_to_all | solution.py:168
  297.2 4.6 all-to-all-start.1
  302.4 43.8 %all-gather = f32[32,16,8]{1,2,0:T(8,128)S(1)} all-gather(f32[1,16,8]{1,2,0:T(8,128)S(1)} %get-tuple-element.100), channel_id=1, replica_groups=mesh['ctx'=32,'tp'=8] {'ctx'}, dimensions={0}, use_global_device_ids=true | all-gather | bytes 16896 | tf_op jit(solution)/shard_map/all_gather | solution.py:169
  347.2 1.8 fusion.63
  350.2 2.1 fusion.41
  352.4 1.4 collective-permute-start.1
  353.8 1.8 fusion.44
  355.8 141.6 %psum.7 = bf16[3,7,512]{2,0,1:T(4,128)(2,1)S(1)} all-reduce(bf16[3,7,512]{2,0,1:T(4,128)(2,1)S(1)} %multiply_convert_fusion.1), channel_id=1, replica_groups=mesh['ctx'=32,'tp'=8] {'ctx'}, use_global_device_ids=true, to_apply=%region_13.14 | all-reduce | flops 10752 | bytes 43008 | tf_op jit(solution)/shard_map/psum | solution.py:181
  499.7 4.3 fusion.47
  504.0 1.2 copy.126
  (353 shorter events, 79.6 us)
Async XLA Ops:
  0.6 14.9 %copy-start.6 = (bf16[3,256,512]{2,1,0:T(8,128)(2,1)S(1)}, bf16[3,256,512]{2,1,0:T(8,128)(2,1)}, u32[]{:S(2)}) copy-start(bf16[3,256,512]{2,1,0:T(8,128)(2,1)} %param.6) | copy-start | bytes 2359300
  1.7 14.1 %collective-permute-start = (bf16[3,6,512]{1,2,0:T(8,128)(2,1)S(1)}, bf16[3,6,512]{1,2,0:T(8,128)(2,1)S(1)}, u32[]{:S(2)}, u32[]{:S(2)}) collective-permute-start(bf16[3,6,512]{1,2,0:T(8,128)(2,1)S(1)} %copy.108), channel_id=1, source_target_pairs={{0,8},{8,16},{16,24},{24,32},{32,40},{40,48},{48,56},{56,64},{64,7... | collective-permute-start | bytes 55304 | tf_op jit(solution)/shard_map/ppermute | solution.py:12
  6.4 9.5 %copy-start.7 = (s32[8192]{0:T(1024)}, s32[8192]{0:T(1024)S(1)}, u32[]{:S(2)}) copy-start(s32[8192]{0:T(1024)S(1)} %rev.12) | copy-start | bytes 98308
  7.0 12.7 %copy-start.11 = (f32[64,128]{1,0:T(8,128)}, f32[64,128]{1,0:T(8,128)S(1)}, u32[]{:S(2)}) copy-start(f32[64,128]{1,0:T(8,128)S(1)} %compare_convert_fusion) | copy-start | bytes 98308
  9.0 5.5 %copy-start.34 = (f32[8,16]{1,0:T(8,128)}, f32[8,16]{1,0:T(8,128)S(1)}, u32[]{:S(2)}) copy-start(f32[8,16]{1,0:T(8,128)S(1)} %get-tuple-element.31) | copy-start | bytes 1540
  9.8 46.9 %copy-start.9 = (f32[128,8,16]{0,2,1:T(8,128)}, f32[128,8,16]{0,2,1:T(8,128)S(1)}, u32[]{:S(2)}) copy-start(f32[128,8,16]{0,2,1:T(8,128)S(1)} %iota_power_fusion) | copy-start | bytes 196612
  12.5 7.2 %copy-start.55 = (f32[256]{0:T(256)}, f32[256]{0:T(256)S(1)}, u32[]{:S(2)}) copy-start(f32[256]{0:T(256)S(1)} %get-tuple-element.112) | copy-start | bytes 3076
  12.5 7.2 %copy-start.57 = (f32[256]{0:T(256)}, f32[256]{0:T(256)S(1)}, u32[]{:S(2)}) copy-start(f32[256]{0:T(256)S(1)} %get-tuple-element.116) | copy-start | bytes 3076
  12.5 7.2 %copy-start.59 = (f32[256]{0:T(256)}, f32[256]{0:T(256)S(1)}, u32[]{:S(2)}) copy-start(f32[256]{0:T(256)S(1)} %get-tuple-element.117) | copy-start | bytes 3076
  12.5 7.2 %copy-start.61 = (f32[256]{0:T(256)}, f32[256]{0:T(256)S(1)}, u32[]{:S(2)}) copy-start(f32[256]{0:T(256)S(1)} %get-tuple-element.113) | copy-start | bytes 3076
  14.6 1.3 copy-start.63
  14.6 1.3 copy-start.65
  14.7 5.0 copy-start.13
  14.7 5.0 copy-start.38
  14.8 5.0 copy-start.40
  14.8 5.0 copy-start.42
  14.8 5.0 copy-start.44
  14.8 5.0 copy-start.46
  14.8 5.0 copy-start.48
  15.8 4.8 copy-start.2
  15.9 4.7 copy-start.50
  19.8 12.2 %copy-start.25 = (bf16[256,512]{1,0:T(8,128)(2,1)S(1)}, bf16[256,512]{1,0:T(8,128)(2,1)}, u32[]{:S(2)}) copy-start(bf16[256,512]{1,0:T(8,128)(2,1)} %param.11) | copy-start | bytes 786436
  19.8 12.3 %copy-start.54 = (f32[8,16]{1,0:T(8,128)S(1)}, f32[8,16]{1,0:T(8,128)}, u32[]{:S(2)}) copy-start(f32[8,16]{1,0:T(8,128)} %multiply_multiply_fusion.2) | copy-start | bytes 1540
  19.8 12.3 %copy-start.69 = (f32[64]{0:T(128)S(1)}, f32[64]{0:T(128)}, u32[]{:S(2)}) copy-start(f32[64]{0:T(128)} %slice_reduce_fusion) | copy-start | bytes 772
  19.8 12.3 %copy-start.70 = (f32[64]{0:T(128)S(1)}, f32[64]{0:T(128)}, u32[]{:S(2)}) copy-start(f32[64]{0:T(128)} %slice_reduce_fusion.1) | copy-start | bytes 772
  20.6 28.7 %copy-start.35 = (f32[8,16]{1,0:T(8,128)S(1)}, f32[8,16]{1,0:T(8,128)}, u32[]{:S(2)}) copy-start(f32[8,16]{1,0:T(8,128)} %copy-done.34) | copy-start | bytes 1540
  20.6 23.9 %all-to-all-start = ((bf16[256,32,16]{0,2,1:T(8,128)(2,1)}), bf16[256,32,16]{0,2,1:T(8,128)(2,1)S(1)}, u32[]{:S(2)}, u32[]{:S(2)}) async-start(bf16[256,32,16]{0,2,1:T(8,128)(2,1)} %bitcast.3), calls=%async_computation | async-start | bytes 524288 | tf_op jit(solution)/shard_map/all_to_all | solution.py:143
  32.1 26.9 %copy-start.4 = (bf16[256,512]{0,1:T(8,128)(2,1)}, bf16[256,512]{0,1:T(8,128)(2,1)S(1)}, u32[]{:S(2)}) copy-start(bf16[256,512]{0,1:T(8,128)(2,1)S(1)} %copy.116) | copy-start | bytes 786436
  44.5 20.4 %all-to-all-start.2 = ((bf16[256,32,16]{0,2,1:T(8,128)(2,1)}), bf16[256,32,16]{0,2,1:T(8,128)(2,1)}, u32[]{:S(2)}, u32[]{:S(2)}) async-start(bf16[256,32,16]{0,2,1:T(8,128)(2,1)} %bitcast.13), calls=%async_computation.2 | async-start | bytes 524288 | tf_op jit(solution)/shard_map/all_to_all | solution.py:151
  88.1 3.4 copy-start.8
  95.9 2.0 copy-start
  111.0 2.1 copy-start.1
  116.2 4.1 copy-start.53
  116.2 5.4 %copy-start.28 = (f32[32,8,16]{0,2,1:T(8,128)S(1)}, f32[32,8,16]{0,2,1:T(8,128)}, u32[]{:S(2)}) copy-start(f32[32,8,16]{0,2,1:T(8,128)} %slice.550) | copy-start | bytes 49156
  116.2 5.4 %copy-start.29 = (f32[32,8,16]{0,2,1:T(8,128)S(1)}, f32[32,8,16]{0,2,1:T(8,128)}, u32[]{:S(2)}) copy-start(f32[32,8,16]{0,2,1:T(8,128)} %slice.554) | copy-start | bytes 49156
  124.9 9.8 %copy-start.26 = (f32[32,8,16]{0,2,1:T(8,128)S(1)}, f32[32,8,16]{0,2,1:T(8,128)}, u32[]{:S(2)}) copy-start(f32[32,8,16]{0,2,1:T(8,128)} %slice.611) | copy-start | bytes 49156
  124.9 9.8 %copy-start.27 = (f32[32,8,16]{0,2,1:T(8,128)S(1)}, f32[32,8,16]{0,2,1:T(8,128)}, u32[]{:S(2)}) copy-start(f32[32,8,16]{0,2,1:T(8,128)} %slice.615) | copy-start | bytes 49156
  150.7 6.8 %copy-start.20 = (f32[1,8,16]{0,2,1:T(8,128)S(1)}, f32[1,8,16]{0,2,1:T(8,128)}, u32[]{:S(2)}) copy-start(f32[1,8,16]{0,2,1:T(8,128)} %get-tuple-element.47) | copy-start | bytes 1540
  150.7 6.8 %copy-start.21 = (f32[1,8,16]{0,2,1:T(8,128)S(1)}, f32[1,8,16]{0,2,1:T(8,128)}, u32[]{:S(2)}) copy-start(f32[1,8,16]{0,2,1:T(8,128)} %get-tuple-element.48) | copy-start | bytes 1540
  150.7 10.6 %copy-start.24 = (f32[2,8,16]{0,2,1:T(8,128)S(1)}, f32[2,8,16]{0,2,1:T(8,128)}, u32[]{:S(2)}) copy-start(f32[2,8,16]{0,2,1:T(8,128)} %pad_add_fusion.2) | copy-start | bytes 3076
  150.7 14.4 %copy-start.19 = (f32[1,8,16]{0,2,1:T(8,128)S(1)}, f32[1,8,16]{0,2,1:T(8,128)}, u32[]{:S(2)}) copy-start(f32[1,8,16]{0,2,1:T(8,128)} %get-tuple-element.45) | copy-start | bytes 1540
  188.6 21.9 %copy-start.17 = (f32[1,8,16]{0,2,1:T(8,128)S(1)}, f32[1,8,16]{0,2,1:T(8,128)}, u32[]{:S(2)}) copy-start(f32[1,8,16]{0,2,1:T(8,128)} %get-tuple-element.75) | copy-start | bytes 1540
  188.6 21.9 %copy-start.18 = (f32[1,8,16]{0,2,1:T(8,128)S(1)}, f32[1,8,16]{0,2,1:T(8,128)}, u32[]{:S(2)}) copy-start(f32[1,8,16]{0,2,1:T(8,128)} %get-tuple-element.76) | copy-start | bytes 1540
  190.3 20.9 %copy-start.22 = (f32[2,8,16]{0,2,1:T(8,128)S(1)}, f32[2,8,16]{0,2,1:T(8,128)}, u32[]{:S(2)}) copy-start(f32[2,8,16]{0,2,1:T(8,128)} %pad_add_fusion) | copy-start | bytes 3076
  190.3 21.4 %copy-start.23 = (f32[2,8,16]{0,2,1:T(8,128)S(1)}, f32[2,8,16]{0,2,1:T(8,128)}, u32[]{:S(2)}) copy-start(f32[2,8,16]{0,2,1:T(8,128)} %pad_add_fusion.1) | copy-start | bytes 3076
  190.3 22.0 %copy-start.15 = (f32[1,8,16]{0,2,1:T(8,128)S(1)}, f32[1,8,16]{0,2,1:T(8,128)}, u32[]{:S(2)}) copy-start(f32[1,8,16]{0,2,1:T(8,128)} %get-tuple-element.73) | copy-start | bytes 1540
  190.3 22.0 %copy-start.16 = (f32[1,8,16]{0,2,1:T(8,128)S(1)}, f32[1,8,16]{0,2,1:T(8,128)}, u32[]{:S(2)}) copy-start(f32[1,8,16]{0,2,1:T(8,128)} %get-tuple-element.74) | copy-start | bytes 1540
  213.9 6.5 %copy-start.32 = (f32[15,8,16]{0,2,1:T(8,128)S(1)}, f32[15,8,16]{0,2,1:T(8,128)}, u32[]{:S(2)}) copy-start(f32[15,8,16]{0,2,1:T(8,128)} %slice.647) | copy-start | bytes 23044
  214.0 6.4 %copy-start.33 = (f32[15,8,16]{0,2,1:T(8,128)S(1)}, f32[15,8,16]{0,2,1:T(8,128)}, u32[]{:S(2)}) copy-start(f32[15,8,16]{0,2,1:T(8,128)} %slice.648) | copy-start | bytes 23044
  218.2 7.8 %copy-start.30 = (f32[31,8,16]{0,2,1:T(8,128)S(1)}, f32[31,8,16]{0,2,1:T(8,128)}, u32[]{:S(2)}) copy-start(f32[31,8,16]{0,2,1:T(8,128)} %slice.650) | copy-start | bytes 47620
  218.2 7.8 %copy-start.31 = (f32[31,8,16]{0,2,1:T(8,128)S(1)}, f32[31,8,16]{0,2,1:T(8,128)}, u32[]{:S(2)}) copy-start(f32[31,8,16]{0,2,1:T(8,128)} %slice.651) | copy-start | bytes 47620
  236.2 10.2 %copy-start.36 = (f32[8,16]{1,0:T(8,128)S(1)}, f32[8,16]{1,0:T(8,128)}, u32[]{:S(2)}) copy-start(f32[8,16]{1,0:T(8,128)} %copy-done.34) | copy-start | bytes 1540
  236.2 10.2 %copy-start.37 = (f32[8192]{0:T(1024)S(1)}, f32[8192]{0:T(1024)}, u32[]{:S(2)}) copy-start(f32[8192]{0:T(1024)} %fusion.75) | copy-start | bytes 98308
  252.0 7.1 %copy-start.10 = (f32[128,8,16]{0,2,1:T(8,128)S(1)}, f32[128,8,16]{0,2,1:T(8,128)}, u32[]{:S(2)}) copy-start(f32[128,8,16]{0,2,1:T(8,128)} %copy-done.9) | copy-start | bytes 196612
  252.0 7.1 %copy-start.12 = (f32[64,128]{1,0:T(8,128)S(1)}, f32[64,128]{1,0:T(8,128)}, u32[]{:S(2)}) copy-start(f32[64,128]{1,0:T(8,128)} %copy-done.11) | copy-start | bytes 98308
  252.0 7.1 %copy-start.14 = (f32[64,128]{1,0:T(8,128)S(1)}, f32[64,128]{1,0:T(8,128)}, u32[]{:S(2)}) copy-start(f32[64,128]{1,0:T(8,128)} %copy-done.13) | copy-start | bytes 98308
  269.6 32.2 %copy-start.52 = (s32[262]{0:T(512)S(1)}, s32[262]{0:T(512)}, u32[]{:S(2)}) copy-start(s32[262]{0:T(512)} %get-tuple-element.120) | copy-start | bytes 3148
  275.4 21.7 %all-to-all-start.3 = ((bf16[32,256,16]{1,2,0:T(8,128)(2,1)}), bf16[32,256,16]{1,2,0:T(8,128)(2,1)S(1)}, u32[]{:S(2)}, u32[]{:S(2)}) async-start(bf16[32,256,16]{1,2,0:T(8,128)(2,1)} %bitcast.123), calls=%async_computation.3 | async-start | bytes 524288 | tf_op jit(solution)/shard_map/all_to_all | solution.py:168
  297.2 50.0 %all-to-all-start.1 = ((bf16[32,256,16]{1,2,0:T(8,128)(2,1)}), bf16[32,256,16]{1,2,0:T(8,128)(2,1)}, u32[]{:S(2)}, u32[]{:S(2)}) async-start(bf16[32,256,16]{1,2,0:T(8,128)(2,1)} %copy.115), calls=%async_computation.1 | async-start | bytes 524288 | tf_op jit(solution)/shard_map/all_to_all | solution.py:150
  350.2 3.7 copy-start.56
  350.2 3.7 copy-start.58
  350.2 3.7 copy-start.60
  352.4 145.6 %copy-start.5 = (bf16[256,512]{0,1:T(8,128)(2,1)S(1)}, bf16[256,512]{0,1:T(8,128)(2,1)}, u32[]{:S(2)}) copy-start(bf16[256,512]{0,1:T(8,128)(2,1)} %get-tuple-element.36) | copy-start | bytes 786436
  352.4 146.5 %collective-permute-start.1 = (bf16[3,6,512]{1,2,0:T(8,128)(2,1)S(1)}, bf16[3,6,512]{1,2,0:T(8,128)(2,1)S(1)}, u32[]{:S(2)}, u32[]{:S(2)}) collective-permute-start(bf16[3,6,512]{1,2,0:T(8,128)(2,1)S(1)} %slice.986), channel_id=1, source_target_pairs={{8,0},{16,8},{24,16},{32,24},{40,32},{48,40},{56,48},{64,56},{72,6... | collective-permute-start | bytes 55304 | tf_op jit(solution)/shard_map/ppermute | solution.py:12
  (13 other events, 11.0 us)
where the time goes:
time: 512 us; the launch traced here: 505 us
  blocking collectives  185 us (36%)
  local copies, waits for them, and re-layouts  173 us (34%)
  other arithmetic  68.9 us (13%)
  starting transfers between devices  35.5 us (7%)
  waiting for transfers between devices  22.4 us (4%)
  matrix products  17 us (3%)
    psum x1, blocking collectives, per_device(): lax.psum(tap_part.astype(jnp.bfloat16), 'ctx').astype(jnp.float32)  142 us
    all_gather x1, blocking collectives, per_device(): grad_res = lax.all_gather(res_part, 'ctx', axis=1, tiled=True)  43.8 us
    pad x32, local copies, waits for them, and re-layouts, stretch_summary(): lax.associative_scan(compose, (pass_factors, end_states), axis=0)  36.4 us
    slice x56, local copies, waits for them, and re-layouts, stretch_summary(): lax.associative_scan(compose, (pass_factors, end_states), axis=0)  30.7 us
    unnamed x167, local copies, waits for them, and re-layouts  28.8 us
    rev x1, local copies, waits for them, and re-layouts, per_device(): owned_grad[::-1]  21.3 us
    all_to_all x1, waiting for transfers between devices, per_device(): lax.all_to_all(carried, 'ctx', split_axis=1, concat_axis=0, tiled=True)  11.5 us
    all_to_all x1, starting transfers between devices, per_device(): lax.all_to_all(carried, 'ctx', split_axis=1, concat_axis=0, tiled=True)  11.3 us
  transfers between devices with their start and end apart: 6, of which 2 were waited for; matrix products, arithmetic and copies ran while one was open for 6% of the time, Pallas kernels for 0%

commit v1 on v0

v1 whole, which is shorter than its diff:
```python
import functools
import math

import jax
import jax.numpy as jnp
from jax import lax
from jax.experimental import pallas as pl
from jax.experimental.pallas import tpu as pltpu
from jax.sharding import PartitionSpec as P

F32 = jnp.float32
BF16 = jnp.bfloat16
SUB = 8
LANES = 128
HALO = 16


def shift(block, distance, cyclic=False):
    count = lax.axis_size("ctx")
    route = [(i, i + distance) for i in range(count) if 0 <= i + distance < count]
    return lax.ppermute(block, "ctx", route)


def row(ref, *index):
    *lead, at = index
    return jnp.broadcast_to(ref[(*lead, pl.ds(at, 1), slice(None))], (SUB, LANES))


def doc_ends(lens_ref, docs):
    ends, total = [], jnp.int32(0)
    for d in range(docs):
        total = total + lens_ref[d]
        ends.append(total)
    return ends


def fill_keep(keep_ref, ends, start, steps, span):
    spread = lax.broadcasted_iota(jnp.int32, (SUB, LANES), 0) * steps + start
    for r in range(-span, steps + span + 1):
        token = spread + r
        starts = token == 0
        for end in ends:
            starts = jnp.logical_or(starts, token == end)
        keep_ref[r + span] = jnp.where(starts, 0.0, 1.0)


def fill_same(same_ref, keep_ref, steps, span):
    for r in range(steps + span):
        running = keep_ref[r + span]
        same_ref[0, r] = running
        for j in range(2, span + 1):
            running = running * keep_ref[r + span - j + 1]
            same_ref[j - 1, r] = running


def fill_order(order_ref, rows, steps, span):
    shape = order_ref.shape
    at = lax.broadcasted_iota(jnp.int32, shape, 0)
    col = lax.broadcasted_iota(jnp.int32, shape, 1)
    token = (at & (SUB - 1)) * steps + (at >> 3) - span
    held = jnp.where(col < rows, col, jnp.where(col < rows + HALO, col - rows - HALO, col - HALO))
    order_ref[...] = jnp.where(token == held, 1.0, 0.0).astype(BF16)


def fill_chunks(chunk_ref, order_ref, ext_ref, proj_ref, cot_ref, left_ref, right_ref):
    rows = proj_ref.shape[1]
    for i in range(4):
        at = pl.ds(i * LANES, LANES)
        ext_ref[pl.ds(0, rows), at] = proj_ref[i] if i < 3 else cot_ref[...]
        if i < 3:
            ext_ref[pl.ds(rows, HALO), at] = left_ref[i]
        ext_ref[pl.ds(rows + HALO, HALO), at] = right_ref[i]
    chunk_ref[...] = jnp.dot(order_ref[...], ext_ref[...], preferred_element_type=F32)


def states_kernel(
    steps, span, modes, docs, lens_ref, proj_ref, cot_ref, left_ref, right_ref, taps_ref, pole_ref,
    feat_ref, chunk_state_ref, edge_ref,
    keep_ref, same_ref, order_ref, ext_ref, chunk_ref,
):
    rows = proj_ref.shape[1]
    start = lax.axis_index("ctx") * rows

    @pl.when(pl.program_id(0) == 0)
    def _():
        fill_keep(keep_ref, doc_ends(lens_ref, docs), start, steps, span)
        fill_same(same_ref, keep_ref, steps, span)
        fill_order(order_ref, rows, steps, span)
        ext_ref[...] = jnp.zeros_like(ext_ref)

    fill_chunks(chunk_ref, order_ref, ext_ref, proj_ref, cot_ref, left_ref, right_ref)

    def chunk(i, r):
        return chunk_ref[pl.ds((r + span) * SUB, SUB), pl.ds(i * LANES, LANES)]

    for i in range(3):
        taps = [row(taps_ref, i, j) for j in range(span + 1)]
        for r in range(steps + span):
            value = taps[0] * chunk(i, r)
            for j in range(1, span + 1):
                value = value + taps[j] * (same_ref[j - 1, r] * chunk(i, r - j))
            feat_ref[i, pl.ds(r * SUB, SUB), :] = value

    def feat(i, r):
        return feat_ref[i, pl.ds(r * SUB, SUB), :]

    poles = [row(pole_ref, m) for m in range(modes)]
    for way in range(2):
        state = [jnp.zeros((SUB, LANES), F32)] * modes
        through = jnp.ones((SUB, LANES), F32)
        order = range(steps) if way == 0 else range(steps + span - 1, span - 1, -1)
        for r in order:
            if way == 0:
                keep, source = keep_ref[r + span], feat(1, r) * feat(2, r)
            else:
                keep, source = keep_ref[r + 1 + span], feat(0, r) * chunk(3, r)
            through = through * keep
            state = [(poles[m] * keep) * state[m] + source for m in range(modes)]
        for m in range(modes):
            chunk_state_ref[way, m] = state[m]
            full, open_ = poles[m], through
            for _ in range(int(math.log2(steps))):
                full = full * full
            total = state[m]
            for hop in (1, 2, 4):
                move = hop if way == 0 else SUB - hop
                total = total + (full * open_) * pltpu.roll(total, move, 0)
                open_ = open_ * pltpu.roll(open_, move, 0)
                full = full * full
            edge = SUB - 1 if way == 0 else 0
            edge_ref[way, pl.ds(m, 1), :] = total[edge : edge + 1]


def finish_kernel(
    steps, span, modes, docs, lens_ref, proj_ref, cot_ref, left_ref, right_ref, taps_ref, pole_ref, res_ref,
    feat_ref, chunk_state_ref, states_ref,
    gated_ref, grad_proj_ref, sums_ref,
    keep_ref, same_ref, order_ref, ext_ref, chunk_ref, back_ref, incoming_ref, coef_ref, grad_ref, out_ref,
):
    rows = proj_ref.shape[1]
    me = lax.axis_index("ctx")
    shards = states_ref.shape[0]
    start = me * rows
    tile = pl.program_id(0)
    tiles = states_ref.shape[2] // LANES

    @pl.when(tile == 0)
    def _():
        ends = doc_ends(lens_ref, docs)
        fill_keep(keep_ref, ends, start, steps, span)
        fill_same(same_ref, keep_ref, steps, span)
        fill_order(order_ref, rows, steps, span)
        ext_ref[...] = jnp.zeros_like(ext_ref)
        at = lax.broadcasted_iota(jnp.int32, back_ref.shape, 0)
        col = lax.broadcasted_iota(jnp.int32, back_ref.shape, 1)
        back_ref[...] = jnp.where(at == (col & (SUB - 1)) * steps + (col >> 3), 1.0, 0.0).astype(BF16)

        last_start, next_start = jnp.int32(0), jnp.int32(shards * rows)
        resume = start + rows + span
        for end in ends:
            last_start = jnp.where(end <= start - 1, jnp.maximum(last_start, end), last_start)
            next_start = jnp.where(end > resume, jnp.minimum(next_start, end), next_start)
        first = last_start // rows
        last = jnp.minimum(shards - 1, lax.div(next_start - span - 1, rows))
        full = pole_ref[...]
        for _ in range(int(math.log2(rows))):
            full = full * full
        zero = jnp.zeros(full.shape, F32)
        incoming = lax.fori_loop(first, me, lambda j, s: full * s + states_ref[j], zero)
        back = lax.fori_loop(me + 1, last + 1, lambda j, s: full * s + states_ref[last + me + 1 - j], zero)
        for n in range(tiles):
            incoming_ref[n, 0] = incoming[:, n * LANES : (n + 1) * LANES]
            incoming_ref[n, 1] = back[:, n * LANES : (n + 1) * LANES]

    fill_chunks(chunk_ref, order_ref, ext_ref, proj_ref, cot_ref, left_ref, right_ref)

    def chunk(i, r):
        return chunk_ref[pl.ds((r + span) * SUB, SUB), pl.ds(i * LANES, LANES)]

    def feat(i, r):
        return feat_ref[i, pl.ds(r * SUB, SUB), :]

    lane_at = pl.ds(pl.multiple_of(tile * LANES, LANES), LANES)
    pole_rows = pole_ref[:, lane_at]
    shrink = jnp.sqrt(1.0 - pole_rows * pole_rows)
    coef_ref[0] = pole_rows
    coef_ref[1] = res_ref[...] * shrink
    coef_ref[2] = shrink
    poles = [row(coef_ref, 0, m) for m in range(modes)]
    sub = lax.broadcasted_iota(jnp.int32, (SUB, LANES), 0)
    scale = 1.0 / math.sqrt(shards * rows)
    taps_count = span + 1

    sums_ref[...] = jnp.zeros_like(sums_ref)

    for way in range(2):
        through = jnp.ones((SUB, LANES), F32)
        for r in range(steps):
            through = through * keep_ref[r + span if way == 0 else r + 2 * span + 1]
        head = 0 if way == 0 else SUB - 1
        state = []
        for m in range(modes):
            full = poles[m]
            for _ in range(int(math.log2(steps))):
                full = full * full
            entry = row(incoming_ref, tile, way, m)
            open_ = through
            total = chunk_state_ref[way, m]
            total = jnp.where(sub == head, total + (full * open_) * entry, total)
            for hop in (1, 2, 4):
                move = hop if way == 0 else SUB - hop
                inside = sub >= hop if way == 0 else sub < SUB - hop
                total = total + jnp.where(inside, (full * open_) * pltpu.roll(total, move, 0), 0.0)
                open_ = open_ * jnp.where(inside, pltpu.roll(open_, move, 0), 1.0)
                full = full * full
            state.append(jnp.where(sub == head, entry, pltpu.roll(total, 1 if way == 0 else SUB - 1, 0)))
        coefs = [row(coef_ref, 1, m) for m in range(modes)]
        if way == 0:
            for r in range(steps + span):
                keep = keep_ref[r + span]
                source = feat(1, r) * feat(2, r)
                state = [(poles[m] * keep) * state[m] + source for m in range(modes)]
                value = coefs[0] * state[0]
                for m in range(1, modes):
                    value = value + coefs[m] * state[m]
                grad_ref[0, r] = chunk(3, r) * value
                if r < steps:
                    out_ref[pl.ds(r * SUB, SUB), pl.ds(3 * LANES, LANES)] = feat(0, r) * value
        else:
            res_sums = [jnp.zeros((SUB, LANES), F32)] * modes
            for r in range(steps + span - 1, -1, -1):
                keep = keep_ref[r + 1 + span]
                source = chunk(3, r) * feat(0, r)
                state = [(poles[m] * keep) * state[m] + source for m in range(modes)]
                value = coefs[0] * state[0]
                for m in range(1, modes):
                    value = value + coefs[m] * state[m]
                grad_ref[1, r] = value * feat(2, r)
                grad_ref[2, r] = value * feat(1, r)
                if r < steps:
                    carried = feat(1, r) * feat(2, r)
                    res_sums = [res_sums[m] + carried * state[m] for m in range(modes)]
            for m in range(modes):
                total = jnp.sum(res_sums[m], axis=0, keepdims=True)
                sums_ref[pl.ds(3 * taps_count + m, 1), :] = total * coef_ref[2, pl.ds(m, 1), :] * scale

    for i in range(3):
        taps = [row(taps_ref, i, j) for j in range(taps_count)]
        tap_sums = [jnp.zeros((SUB, LANES), F32)] * taps_count
        grads = [jnp.zeros((SUB, LANES), F32)] * taps_count
        for r in range(steps + span):
            here = grad_ref[i, r]
            for j in range(taps_count):
                if r - j >= steps:
                    continue
                masked = here if j == 0 else same_ref[j - 1, r] * here
                if r < steps:
                    tap_sums[j] = tap_sums[j] + masked * chunk(i, r - j)
                if r - j >= 0:
                    grads[j] = grads[j] + taps[j] * masked
            done = r - span
            if done >= 0:
                out_ref[pl.ds(done * SUB, SUB), pl.ds(i * LANES, LANES)] = grads[span]
            grads = [jnp.zeros((SUB, LANES), F32)] + grads[:span]
        for j in range(taps_count):
            total = jnp.sum(tap_sums[j], axis=0, keepdims=True)
            sums_ref[pl.ds(i * taps_count + j, 1), :] = total * scale

    natural = jnp.dot(back_ref[...], out_ref[...].astype(BF16), preferred_element_type=F32).astype(BF16)
    gated_ref[...] = natural[:, 3 * LANES :]
    for i in range(3):
        grad_proj_ref[i] = natural[:, i * LANES : (i + 1) * LANES]


def per_device(projected, short_taps, pole_decay, residues, doc_lengths, cotangent):
    rows, chans = projected.shape[1:]
    span = short_taps.shape[1] - 1
    modes = pole_decay.shape[0]
    docs = doc_lengths.shape[0]
    shards = lax.axis_size("ctx")
    me = lax.axis_index("ctx")
    steps = rows // SUB
    tiles = chans // LANES
    ext_rows = -(-(rows + 2 * HALO) // LANES) * LANES
    sum_rows = 32

    left = shift(projected[:, rows - HALO :], 1)
    right = shift(jnp.concatenate([projected[:, :HALO], cotangent[None, :HALO]]), -1)

    smem = pl.BlockSpec(memory_space=pltpu.SMEM)

    def lanes(*lead):
        return pl.BlockSpec((*lead, LANES), lambda n: (*(0 for _ in lead), n))

    def whole(*shape):
        return pl.BlockSpec(shape, lambda n: tuple(0 for _ in shape))

    shared = [
        smem, lanes(3, rows), lanes(rows), lanes(3, HALO), lanes(4, HALO), lanes(3, span + 1),
    ]
    scratch = [
        pltpu.VMEM((steps + 2 * span + 1, SUB, LANES), F32),
        pltpu.VMEM((span, steps + span, SUB, LANES), F32),
        pltpu.VMEM(((steps + 2 * span) * SUB, ext_rows), BF16),
        pltpu.VMEM((ext_rows, 4 * LANES), BF16),
        pltpu.VMEM(((steps + 2 * span) * SUB, 4 * LANES), F32),
    ]
    params = pltpu.CompilerParams(vmem_limit_bytes=40 << 20)
    feat_spec = lanes(3, (steps + span) * SUB)
    chunk_state_spec = lanes(2, modes, SUB)

    feats, chunk_states, edges = pl.pallas_call(
        functools.partial(states_kernel, steps, span, modes, docs),
        grid=(tiles,),
        out_shape=(
            jax.ShapeDtypeStruct((3, (steps + span) * SUB, chans), F32),
            jax.ShapeDtypeStruct((2, modes, SUB, chans), F32),
            jax.ShapeDtypeStruct((2, modes, chans), F32),
        ),
        in_specs=shared + [lanes(modes)],
        out_specs=(feat_spec, chunk_state_spec, lanes(2, modes)),
        scratch_shapes=scratch,
        compiler_params=params,
        name="states",
    )(doc_lengths, projected, cotangent, left, right, short_taps, pole_decay)

    later = (jnp.arange(shards, dtype=jnp.int32) > me)[:, None, None]
    outgoing = jnp.where(later, edges[:1], edges[1:]).astype(BF16)
    states = lax.all_to_all(outgoing, "ctx", split_axis=0, concat_axis=0, tiled=True).astype(F32)

    gated, grad_proj, sums = pl.pallas_call(
        functools.partial(finish_kernel, steps, span, modes, docs),
        grid=(tiles,),
        out_shape=(
            jax.ShapeDtypeStruct((rows, chans), BF16),
            jax.ShapeDtypeStruct((3, rows, chans), BF16),
            jax.ShapeDtypeStruct((sum_rows, chans), F32),
        ),
        in_specs=shared
        + [whole(modes, chans), lanes(modes), feat_spec, chunk_state_spec, whole(shards, modes, chans)],
        out_specs=(lanes(rows), lanes(3, rows), lanes(sum_rows)),
        scratch_shapes=scratch
        + [
            pltpu.VMEM((rows, rows), BF16),
            pltpu.VMEM((tiles, 2, modes, LANES), F32),
            pltpu.VMEM((3, modes, LANES), F32),
            pltpu.VMEM((3, steps + span, SUB, LANES), F32),
            pltpu.VMEM((rows, 4 * LANES), F32),
        ],
        compiler_params=params,
        name="finish",
    )(doc_lengths, projected, cotangent, left, right, short_taps, pole_decay, residues, feats, chunk_states, states)

    near = 4
    far = shards // near

    def around(block, hop):
        return lax.ppermute(
            block, "ctx", [(i, i // near * near + (i + hop) % near) for i in range(shards)]
        )

    part = sums.astype(BF16)
    one, two, three = (around(part, hop).astype(F32) for hop in (1, 2, 3))
    part = ((part.astype(F32) + two) + (one + three)).astype(BF16)
    groups = [[f * near + n for f in range(far)] for n in range(near)]
    spread = lax.optimization_barrier(jnp.broadcast_to(part[None], (far, sum_rows, chans)))
    gathered = lax.all_to_all(spread, "ctx", 0, 0, tiled=True, axis_index_groups=groups)
    total = jnp.sum(gathered.astype(F32), axis=0)
    tap_rows = 3 * (span + 1)
    grad_tap = total[:tap_rows].reshape(3, span + 1, chans)
    grad_res = total[tap_rows : tap_rows + modes]
    return (gated, grad_proj, grad_tap, grad_res)


def solution(mesh):
    placed = (
        P(None, "ctx", "tp"),
        P(None, None, "tp"),
        P(None, "tp"),
        P(None, "tp"),
        P(),
        P("ctx", "tp"),
    )
    return jax.shard_map(
        per_device,
        mesh=mesh,
        in_specs=placed,
        out_specs=(P("ctx", "tp"), P(None, "ctx", "tp"), P(None, None, "tp"), P(None, "tp")),
        check_vma=False,
    )
```

time: 512 us -> 76.4 us (0.15); the launches traced: 505 us -> 75.9 us
  local copies, waits for them, and re-layouts: 173 us -> 7.1 us
  blocking collectives: 185 us -> 37.7 us
  other arithmetic: 68.9 us -> 0.23 us
  starting transfers between devices: 35.5 us -> 8.76 us
  matrix products: 17 us -> 0 us
  waiting for transfers between devices: 22.4 us -> 7.58 us
  Pallas kernels: 0 us -> 13.8 us
    psum x1 -> x0, blocking collectives: 142 us -> none  [per_device(): lax.psum(tap_part.astype(jnp.bfloat16), 'ctx').astype(jnp.float32)]
    slice x71 -> x3, local copies, waits for them, and re-layouts: 45.3 us -> 1.46 us  [the longest x1 0.85 us: per_device(): projected[:, :HALO]]
    all_gather x1 -> x0, blocking collectives: 43.8 us -> none  [per_device(): grad_res = lax.all_gather(res_part, 'ctx', axis=1, tiled=True)]
    all_to_all x0 -> x2, blocking collectives: none -> 37.7 us  [the longest x1 24.8 us: per_device(): lax.all_to_all(outgoing, 'ctx', split_axis=0, concat_axis=0, tiled=True)]
    pad x32 -> x0, local copies, waits for them, and re-layouts: 36.4 us -> none  [stretch_summary(): lax.associative_scan(compose, (pass_factors, end_states), axis=0)]
    rev x4 -> x0, local copies, waits for them, and re-layouts: 31.6 us -> none  [the longest x1 21.3 us: per_device(): owned_grad[::-1]]
    all_to_all x4 -> x0, starting transfers between devices: 30.6 us -> none  [the longest x1 11.3 us: per_device(): lax.all_to_all(carried, 'ctx', split_axis=1, concat_axis=0, tiled=True)]
    unnamed x167 -> x14, local copies, waits for them, and re-layouts: 28.8 us -> 4.26 us
  transfers between devices with their start and end apart: 6 -> 5, of which waited for: 2 -> 4; matrix products, arithmetic and copies ran while one was open for 6% -> 1% of each run, Pallas kernels for 0% -> 0%
where the time goes in v1:
time: 76.4 us; the launch traced here: 75.9 us
  blocking collectives  37.7 us (49%)
  Pallas kernels  13.8 us (18%)
  starting transfers between devices  8.76 us (11%)
  waiting for transfers between devices  7.58 us (10%)
  local copies, waits for them, and re-layouts  7.1 us (9%)
  between operations  0.77 us (1%)
    all_to_all x1, blocking collectives, per_device(): lax.all_to_all(outgoing, 'ctx', split_axis=0, concat_axis=0, tiled=True)  24.8 us
    all_to_all x1, blocking collectives, per_device(): lax.all_to_all(spread, 'ctx', 0, 0, tiled=True, axis_index_groups=groups)  12.9 us
    pallas_call x1, Pallas kernels, per_device(): pl.pallas_call(functools.partial(finish_kernel, steps, span, modes, docs)...  8.48 us
    pallas_call x1, Pallas kernels, per_device(): pl.pallas_call(functools.partial(states_kernel, steps, span, modes, docs)...  5.29 us
    ppermute x2, waiting for transfers between devices, shift(): return lax.ppermute(block, 'ctx', route)  4.83 us
    ppermute x2, starting transfers between devices, shift(): return lax.ppermute(block, 'ctx', route)  4.76 us
    unnamed x14, local copies, waits for them, and re-layouts  4.26 us
    ppermute x3, starting transfers between devices, around(): lax.ppermute(block, 'ctx', [(i, i // near * near + (i + hop) % near) for...  4 us
  transfers between devices with their start and end apart: 5, of which 4 were waited for; matrix products, arithmetic and copies ran while one was open for 1% of the time, Pallas kernels for 0%

profile of v1, /device:TPU:2, one launch (start us, length us, event | category | flops | bytes accessed | tf_op | source)
XLA Modules:
  0.0 75.9 jit_solution(13841210781606092452)
XLA Ops:
  0.6 0.0 copy-start.3
  0.6 0.0 copy-start.5
  0.7 0.8 %fusion = (bf16[3,16,512]{2,1,0:T(8,128)(2,1)S(1)}, bf16[3,16,512]{2,1,0:T(8,128)(2,1)S(1)}) fusion(bf16[3,256,512]{2,1,0:T(8,128)(2,1)} %proj_ref.3), kind=kLoop, calls=%fused_computation.8 | loop fusion | bytes 196608 | tf_op jit(solution)/shard_map/slice | solution.py:288
  1.5 3.5 %collective-permute-start = (bf16[3,16,512]{2,1,0:T(8,128)(2,1)S(1)}, bf16[3,16,512]{2,1,0:T(8,128)(2,1)S(1)}, u32[]{:S(2)}, u32[]{:S(2)}) collective-permute-start(bf16[3,16,512]{2,1,0:T(8,128)(2,1)S(1)} %get-tuple-element.17), channel_id=1, source_target_pairs={{0,8},{8,16},{16,24},{24,32},{32,40},{40,48},{48,56},{56,64},{64,7... | collective-permute-start | bytes 147464 | tf_op jit(solution)/shard_map/ppermute | solution.py:21
  5.0 0.7 slice_bitcast_fusion.2
  5.7 1.3 %collective-permute-start.1 = (bf16[4,16,512]{2,1,0:T(8,128)(2,1)S(1)}, bf16[4,16,512]{2,1,0:T(8,128)(2,1)S(1)}, u32[]{:S(2)}, u32[]{:S(2)}) collective-permute-start(bf16[4,16,512]{2,1,0:T(8,128)(2,1)S(1)} %pad_maximum_fusion), channel_id=1, source_target_pairs={{8,0},{16,8},{24,16},{32,24},{40,32},{48,40},{56,48},{64,56},{72,6... | collective-permute-start | bytes 196616 | tf_op jit(solution)/shard_map/ppermute | solution.py:21
  7.0 0.0 collective-permute-done.left_ref
  7.0 4.8 %collective-permute-done.1.right_ref = bf16[4,16,512]{2,1,0:T(8,128)(2,1)S(1)} collective-permute-done((bf16[4,16,512]{2,1,0:T(8,128)(2,1)S(1)}, bf16[4,16,512]{2,1,0:T(8,128)(2,1)S(1)}, u32[]{:S(2)}, u32[]{:S(2)}) %collective-permute-start.1) | collective-permute-done | bytes 65568 | tf_op jit(solution)/shard_map/ppermute | solution.py:21
  11.9 0.0 copy-start
  11.9 1.1 %copy-done = bf16[3,256,512]{2,1,0:T(8,128)(2,1)S(1)} copy-done((bf16[3,256,512]{2,1,0:T(8,128)(2,1)S(1)}, bf16[3,256,512]{2,1,0:T(8,128)(2,1)}, u32[]{:S(2)}) %copy-start) | copy-done | bytes 786456
  13.0 0.0 copy-start.1
  13.0 0.9 %copy-done.1 = bf16[256,512]{1,0:T(8,128)(2,1)S(1)} copy-done((bf16[256,512]{1,0:T(8,128)(2,1)S(1)}, bf16[256,512]{1,0:T(8,128)(2,1)}, u32[]{:S(2)}) %copy-start.1) | copy-done | bytes 262168
  14.0 0.0 copy-start.2
  14.0 0.8 %copy-done.2 = f32[3,7,512]{2,1,0:T(8,128)S(1)} copy-done((f32[3,7,512]{2,1,0:T(8,128)S(1)}, f32[3,7,512]{2,1,0:T(8,128)}, u32[]{:S(2)}) %copy-start.2) | copy-done | bytes 43032
  14.8 0.0 copy-start.4
  14.8 0.7 copy-done.4
  15.5 0.0 copy-start.6
  15.5 0.7 copy-done.6
  16.1 5.3 %states.1 = (f32[3,304,512]{2,1,0:T(8,128)S(1)}, f32[2,8,8,512]{3,2,1,0:T(8,128)S(1)}, f32[2,8,512]{2,1,0:T(8,128)S(1)}) custom-call(s32[16]{0:T(128)S(1)} %copy-done.6, bf16[3,256,512]{2,1,0:T(8,128)(2,1)S(1)} %copy-done, bf16[256,512]{1,0:T(8,128)(2,1)S(1)} %copy-done.1, bf16[3,16,512]{2,1,0:T(8,128)(2,1)S(1)} %collective-permute-done.left_ref, ...), custom_call_target="tpu_custom_call" | custom-call | tf_op jit(solution)/shard_map/states/pallas_call | solution.py:312
  21.4 0.1 select_convert_fusion
  21.6 24.8 %all_to_all.10 = bf16[32,8,512]{2,1,0:T(8,128)(2,1)S(1)} all-to-all(bf16[32,8,512]{2,1,0:T(8,128)(2,1)S(1)} %select_convert_fusion), channel_id=1, replica_groups=mesh['ctx'=32,'tp'=8] {'ctx'}, dimensions={0} | all-to-all | bytes 524288 | tf_op jit(solution)/shard_map/all_to_all | solution.py:329
  46.4 0.1 convert_element_type.28.states_ref
  46.4 0.0 copy-done.3
  46.4 0.0 copy-done.5
  46.4 8.5 %finish.1 = (bf16[256,512]{1,0:T(8,128)(2,1)}, bf16[3,256,512]{2,1,0:T(8,128)(2,1)}, f32[32,512]{1,0:T(8,128)S(1)}) custom-call(s32[16]{0:T(128)S(1)} %copy-done.6, bf16[3,256,512]{2,1,0:T(8,128)(2,1)S(1)} %copy-done, bf16[256,512]{1,0:T(8,128)(2,1)S(1)} %copy-done.1, bf16[3,16,512]{2,1,0:T(8,128)(2,1)S(1)} %collective-permute-done.left_ref, ...), custom_call_target="tpu_custom_call" | custom-call | tf_op jit(solution)/shard_map/finish/pallas_call | solution.py:331
  54.9 0.1 collective-permute-start.3
  55.0 2.7 %collective-permute-start.2 = (bf16[32,512]{1,0:T(8,128)(2,1)S(1)}, bf16[32,512]{1,0:T(8,128)(2,1)S(1)}, u32[]{:S(2)}, u32[]{:S(2)}) collective-permute-start(bf16[32,512]{1,0:T(8,128)(2,1)S(1)} %convert_element_type.29), channel_id=1, source_target_pairs={{0,16},{8,24},{16,0},{24,8},{32,48},{40,56},{48,32},{56,40},{64,80... | collective-permute-start | bytes 98312 | tf_op jit(solution)/shard_map/ppermute | solution.py:358
  57.8 1.2 %collective-permute-start.4 = (bf16[32,512]{1,0:T(8,128)(2,1)S(1)}, bf16[32,512]{1,0:T(8,128)(2,1)S(1)}, u32[]{:S(2)}, u32[]{:S(2)}) collective-permute-start(bf16[32,512]{1,0:T(8,128)(2,1)S(1)} %convert_element_type.29), channel_id=1, source_target_pairs={{0,24},{8,0},{16,8},{24,16},{32,56},{40,32},{48,40},{56,48},{64,88... | collective-permute-start | bytes 98312 | tf_op jit(solution)/shard_map/ppermute | solution.py:358
  58.9 1.2 %collective-permute-done.3 = bf16[32,512]{1,0:T(8,128)(2,1)S(1)} collective-permute-done((bf16[32,512]{1,0:T(8,128)(2,1)S(1)}, bf16[32,512]{1,0:T(8,128)(2,1)S(1)}, u32[]{:S(2)}, u32[]{:S(2)}) %collective-permute-start.3) | collective-permute-done | bytes 32800 | tf_op jit(solution)/shard_map/ppermute | solution.py:358
  60.1 0.4 collective-permute-done.2
  60.5 1.2 %collective-permute-done.4 = bf16[32,512]{1,0:T(8,128)(2,1)S(1)} collective-permute-done((bf16[32,512]{1,0:T(8,128)(2,1)S(1)}, bf16[32,512]{1,0:T(8,128)(2,1)S(1)}, u32[]{:S(2)}, u32[]{:S(2)}) %collective-permute-start.4) | collective-permute-done | bytes 32800 | tf_op jit(solution)/shard_map/ppermute | solution.py:358
  61.7 12.9 %all_to_all.11 = bf16[8,32,512]{2,1,0:T(8,128)(2,1)S(1)} all-to-all(bf16[8,32,512]{2,1,0:T(8,128)(2,1)S(1)} %broadcast_in_dim.44), channel_id=1, replica_groups={{0,32,64,96,128,160,192,224},{8,40,72,104,136,168,200,232},{16,48,80,11..., dimensions={0} | all-to-all | bytes 524288 | tf_op jit(solution)/shard_map/all_to_all | solution.py:367
  74.6 0.6 slice.29
  75.3 0.6 reshape.16
  (8 shorter events, 0.1 us)
Async XLA Ops:
  0.6 45.8 %copy-start.3 = (f32[3,7,512]{2,1,0:T(8,128)S(1)}, f32[3,7,512]{2,1,0:T(8,128)}, u32[]{:S(2)}) copy-start(f32[3,7,512]{2,1,0:T(8,128)} %taps_ref.3) | copy-start | bytes 129028
  0.6 45.8 %copy-start.5 = (f32[8,512]{1,0:T(8,128)S(1)}, f32[8,512]{1,0:T(8,128)}, u32[]{:S(2)}) copy-start(f32[8,512]{1,0:T(8,128)} %res_ref.1) | copy-start | bytes 49156
  1.5 5.5 %collective-permute-start = (bf16[3,16,512]{2,1,0:T(8,128)(2,1)S(1)}, bf16[3,16,512]{2,1,0:T(8,128)(2,1)S(1)}, u32[]{:S(2)}, u32[]{:S(2)}) collective-permute-start(bf16[3,16,512]{2,1,0:T(8,128)(2,1)S(1)} %get-tuple-element.17), channel_id=1, source_target_pairs={{0,8},{8,16},{16,24},{24,32},{32,40},{40,48},{48,56},{56,64},{64,7... | collective-permute-start | bytes 147464 | tf_op jit(solution)/shard_map/ppermute | solution.py:21
  5.7 6.2 %collective-permute-start.1 = (bf16[4,16,512]{2,1,0:T(8,128)(2,1)S(1)}, bf16[4,16,512]{2,1,0:T(8,128)(2,1)S(1)}, u32[]{:S(2)}, u32[]{:S(2)}) collective-permute-start(bf16[4,16,512]{2,1,0:T(8,128)(2,1)S(1)} %pad_maximum_fusion), channel_id=1, source_target_pairs={{8,0},{16,8},{24,16},{32,24},{40,32},{48,40},{56,48},{64,56},{72,6... | collective-permute-start | bytes 196616 | tf_op jit(solution)/shard_map/ppermute | solution.py:21
  11.9 1.1 %copy-start = (bf16[3,256,512]{2,1,0:T(8,128)(2,1)S(1)}, bf16[3,256,512]{2,1,0:T(8,128)(2,1)}, u32[]{:S(2)}) copy-start(bf16[3,256,512]{2,1,0:T(8,128)(2,1)} %proj_ref.3) | copy-start | bytes 2359300
  13.0 0.9 %copy-start.1 = (bf16[256,512]{1,0:T(8,128)(2,1)S(1)}, bf16[256,512]{1,0:T(8,128)(2,1)}, u32[]{:S(2)}) copy-start(bf16[256,512]{1,0:T(8,128)(2,1)} %cot_ref.3) | copy-start | bytes 786436
  14.0 0.8 %copy-start.2 = (f32[3,7,512]{2,1,0:T(8,128)S(1)}, f32[3,7,512]{2,1,0:T(8,128)}, u32[]{:S(2)}) copy-start(f32[3,7,512]{2,1,0:T(8,128)} %taps_ref.3) | copy-start | bytes 129028
  14.8 0.7 copy-start.4
  15.5 0.7 copy-start.6
  54.9 5.2 %collective-permute-start.3 = (bf16[32,512]{1,0:T(8,128)(2,1)S(1)}, bf16[32,512]{1,0:T(8,128)(2,1)S(1)}, u32[]{:S(2)}, u32[]{:S(2)}) collective-permute-start(bf16[32,512]{1,0:T(8,128)(2,1)S(1)} %convert_element_type.29), channel_id=1, source_target_pairs={{0,8},{8,16},{16,24},{24,0},{32,40},{40,48},{48,56},{56,32},{64,72... | collective-permute-start | bytes 98312 | tf_op jit(solution)/shard_map/ppermute | solution.py:358
  55.0 5.5 %collective-permute-start.2 = (bf16[32,512]{1,0:T(8,128)(2,1)S(1)}, bf16[32,512]{1,0:T(8,128)(2,1)S(1)}, u32[]{:S(2)}, u32[]{:S(2)}) collective-permute-start(bf16[32,512]{1,0:T(8,128)(2,1)S(1)} %convert_element_type.29), channel_id=1, source_target_pairs={{0,16},{8,24},{16,0},{24,8},{32,48},{40,56},{48,32},{56,40},{64,80... | collective-permute-start | bytes 98312 | tf_op jit(solution)/shard_map/ppermute | solution.py:358
  57.8 3.9 %collective-permute-start.4 = (bf16[32,512]{1,0:T(8,128)(2,1)S(1)}, bf16[32,512]{1,0:T(8,128)(2,1)S(1)}, u32[]{:S(2)}, u32[]{:S(2)}) collective-permute-start(bf16[32,512]{1,0:T(8,128)(2,1)S(1)} %convert_element_type.29), channel_id=1, source_target_pairs={{0,24},{8,0},{16,8},{24,16},{32,56},{40,32},{48,40},{56,48},{64,88... | collective-permute-start | bytes 98312 | tf_op jit(solution)/shard_map/ppermute | solution.py:358

commit v2 on v0

v2 whole, which is shorter than its diff:
```python
import functools
import math

import jax
import jax.numpy as jnp
from jax import lax
from jax.experimental import pallas as pl
from jax.experimental.pallas import tpu as pltpu
from jax.sharding import PartitionSpec as P

F32 = jnp.float32
BF16 = jnp.bfloat16
SUB = 8
LANES = 128
HALO = 16
SUM_ROWS = 32


def shift(block, distance):
    count = lax.axis_size("ctx")
    route = [(i, i + distance) for i in range(count) if 0 <= i + distance < count]
    return lax.ppermute(block, "ctx", route)


def spread(line):
    return jnp.broadcast_to(line, (SUB, LANES))


def power(base, exponent):
    for _ in range(int(math.log2(exponent))):
        base = base * base
    return base


def total_of(terms):
    terms = list(terms)
    while len(terms) > 1:
        terms = [a + b for a, b in zip(terms[::2], terms[1::2])] + terms[len(terms) & ~1 :]
    return terms[0]


def doc_ends(lens_ref):
    ends, total = [], jnp.int32(0)
    for d in range(lens_ref.shape[0]):
        total = total + lens_ref[d]
        ends.append(total)
    return ends


def keep_at(token, ends):
    starts = token == 0
    for end in ends:
        starts = jnp.logical_or(starts, token == end)
    return jnp.where(starts, 0.0, 1.0)


def fill_keep(keep_ref, ends, start, steps, span):
    token = lax.broadcasted_iota(jnp.int32, (SUB, LANES), 0) * steps + start
    for r in range(-span, steps + span + 1):
        keep_ref[r + span] = keep_at(token + r, ends)


def fill_same(same_ref, keep_ref, steps, span):
    for r in range(steps + span):
        running = keep_ref[r + span]
        same_ref[0, r] = running
        for j in range(2, span + 1):
            running = running * keep_ref[r + span - j + 1]
            same_ref[j - 1, r] = running


def fill_cum(cum_ref, keep_ref, steps, span):
    running = jnp.ones((SUB, LANES), F32)
    for r in range(steps + span):
        running = running * keep_ref[r + span]
        cum_ref[0, r] = running
    running = jnp.ones((SUB, LANES), F32)
    for r in range(steps + span - 1, -1, -1):
        running = running * keep_ref[r + 1 + span]
        cum_ref[1, r] = running


def fill_pick(pick_ref, ends, start, rows, span):
    shards = pick_ref.shape[1]
    last_start, next_start = jnp.int32(0), jnp.int32(shards * rows)
    for end in ends:
        last_start = jnp.where(end < start, jnp.maximum(last_start, end), last_start)
        next_start = jnp.where(end > start + rows + span, jnp.minimum(next_start, end), next_start)
    owner = lax.broadcasted_iota(jnp.int32, (shards, LANES), 0) * rows
    pick_ref[0] = jnp.where(owner + rows > last_start, 1.0, 0.0)
    pick_ref[1] = jnp.where(owner + span < next_start, 1.0, 0.0)


def fill_order(order_ref, rows, steps, span):
    shape = order_ref.shape
    at = lax.broadcasted_iota(jnp.int32, shape, 0)
    col = lax.broadcasted_iota(jnp.int32, shape, 1)
    token = (at & (SUB - 1)) * steps + (at >> 3) - span
    held = jnp.where(col < rows, col, jnp.where(col < rows + HALO, col - rows - HALO, col - HALO))
    order_ref[...] = jnp.where(token == held, 1.0, 0.0).astype(BF16)


def fill_rim_masks(mask_ref, ends, start, rows, span):
    last_start, next_start = jnp.int32(0), jnp.int32(1 << 30)
    for end in ends:
        last_start = jnp.where(end < start + rows, jnp.maximum(last_start, end), last_start)
        next_start = jnp.where(end > start + span, jnp.minimum(next_start, end), next_start)
    sub = lax.broadcasted_iota(jnp.int32, (SUB, LANES), 0)
    for side in range(2):
        token = start + sub + side * rows
        running = jnp.ones((SUB, LANES), F32)
        for j in range(span):
            running = running * keep_at(token - j, ends)
            mask_ref[side, j] = running
        seen = token >= last_start if side == 0 else token < next_start
        mask_ref[side, span] = jnp.where(jnp.logical_and(sub < span, seen), 1.0, 0.0)


def at_step(r):
    return pl.ds(r * SUB, SUB)


def lanes_of(i):
    return pl.ds(i * LANES, LANES)


def load_kernel(
    steps, span,
    lens_hbm, proj_hbm, cot_hbm, taps_hbm, pole_hbm, res_hbm,
    left_ref, right_ref, proj_ref, cot_ref, taps_ref, pole_ref, res_ref, keep_ref, rim_mask_ref, pick_ref, order_ref,
    lens_ref, edge_sem, small_sem, tile_sem,
):
    tiles, _, rows, _ = proj_ref.shape
    lens_copy = pltpu.make_async_copy(lens_hbm, lens_ref, small_sem.at[0])
    copies = [
        pltpu.make_async_copy(proj_hbm.at[:, pl.ds(rows - HALO, HALO), :], left_ref, edge_sem.at[0]),
        pltpu.make_async_copy(proj_hbm.at[:, pl.ds(0, HALO), :], right_ref.at[pl.ds(0, 3)], edge_sem.at[1]),
        pltpu.make_async_copy(cot_hbm.at[pl.ds(0, HALO), :], right_ref.at[3], edge_sem.at[2]),
        pltpu.make_async_copy(taps_hbm, taps_ref, small_sem.at[1]),
        pltpu.make_async_copy(pole_hbm, pole_ref, small_sem.at[2]),
        pltpu.make_async_copy(res_hbm, res_ref, small_sem.at[3]),
    ]
    for n in range(tiles):
        at = lanes_of(n)
        copies.append(pltpu.make_async_copy(proj_hbm.at[:, :, at], proj_ref.at[n], tile_sem.at[n, 0]))
        copies.append(pltpu.make_async_copy(cot_hbm.at[:, at], cot_ref.at[n], tile_sem.at[n, 1]))
    lens_copy.start()
    for copy in copies:
        copy.start()
    fill_order(order_ref, rows, steps, span)
    lens_copy.wait()
    start = lax.axis_index("ctx") * rows
    ends = doc_ends(lens_ref)
    fill_keep(keep_ref, ends, start, steps, span)
    fill_rim_masks(rim_mask_ref, ends, start, rows, span)
    fill_pick(pick_ref, ends, start, rows, span)
    for copy in copies:
        copy.wait()


def fill_ext(ext_ref, n, proj_ref, cot_ref, left_ref, right_ref, streams):
    rows = proj_ref.shape[2]
    lane_at = pl.ds(pl.multiple_of(n * LANES, LANES), LANES)
    for place, i in enumerate(streams):
        at = lanes_of(place)
        ext_ref[pl.ds(0, rows), at] = proj_ref[n, i] if i < 3 else cot_ref[n]
        if i < 3:
            ext_ref[pl.ds(rows, HALO), at] = left_ref[i, :, lane_at]
        ext_ref[pl.ds(rows + HALO, HALO), at] = right_ref[i, :, lane_at]


def edges_kernel(
    steps, span, modes,
    proj_ref, cot_ref, taps_ref, pole_ref, keep_ref, order_ref,
    edge_ref, rim_ref,
    same_ref, mask_ref, ext_ref, chunk_ref, feat_ref,
):
    tiles, _, rows, _ = proj_ref.shape
    fill_same(same_ref, keep_ref, steps, span)
    sub = lax.broadcasted_iota(jnp.int32, (SUB, LANES), 0)
    running = jnp.ones((SUB, LANES), F32)
    for r in range(steps - 1, -1, -1):
        mask_ref[0, r] = running if r >= span else jnp.where(sub == 0, 0.0, running)
        running = running * keep_ref[r + span]
    through = [running]
    running = jnp.ones((SUB, LANES), F32)
    for r in range(span, steps + span):
        mask_ref[1, r - span] = running if r < steps else jnp.where(sub == SUB - 1, 0.0, running)
        running = running * keep_ref[r + 1 + span]
    through.append(running)

    def tile_step(n, carry):
        for i in range(4):
            ext_ref[:, lanes_of(i)] = proj_ref[n, i] if i < 3 else cot_ref[n]
        chunk_ref[...] = jnp.dot(order_ref[:, pl.ds(0, rows)], ext_ref[...], preferred_element_type=F32)
        rim_ref[n, 0] = proj_ref[n, 1, pl.ds(0, HALO), :].astype(F32)[:SUB]
        rim_ref[n, 1] = proj_ref[n, 2, pl.ds(0, HALO), :].astype(F32)[:SUB]
        rim_ref[n, 2] = proj_ref[n, 0, pl.ds(rows - HALO, HALO), :].astype(F32)[HALO - SUB :]

        def chunk(i, r):
            return chunk_ref[at_step(r + span), lanes_of(i)]

        lane_at = pl.ds(pl.multiple_of(n * LANES, LANES), LANES)
        for i in range(3):
            taps = [spread(taps_ref[i, pl.ds(j, 1), lane_at]) for j in range(span + 1)]
            first = span if i == 0 else 0
            for r in range(first, first + steps):
                value = taps[0] * chunk(i, r)
                for j in range(1, span + 1):
                    value = value + taps[j] * (same_ref[j - 1, r] * chunk(i, r - j))
                if i == 0:
                    value = value * chunk(3, r) * mask_ref[1, r - first]
                elif i == 2:
                    value = value * feat_ref[1, r] * mask_ref[0, r]
                feat_ref[i, r - first] = value

        poles = [spread(pole_ref[pl.ds(m, 1), lane_at]) for m in range(modes)]
        for way in range(2):
            state = [jnp.zeros((SUB, LANES), F32)] * modes
            for r in range(steps) if way == 0 else range(steps - 1, -1, -1):
                source = feat_ref[2 if way == 0 else 0, r]
                state = [poles[m] * state[m] + source for m in range(modes)]
            open_ = through[way]
            factors = [power(poles[m], steps) for m in range(modes)]
            for hop in (1, 2, 4):
                move = hop if way == 0 else SUB - hop
                for m in range(modes):
                    state[m] = state[m] + (factors[m] * open_) * pltpu.roll(state[m], move, 0)
                    factors[m] = factors[m] * factors[m]
                open_ = open_ * pltpu.roll(open_, move, 0)
            last = SUB - 1 if way == 0 else 0
            for m in range(modes):
                edge_ref[way, pl.ds(m, 1), lane_at] = state[m][last : last + 1]
        return carry

    lax.fori_loop(0, tiles, tile_step, 0)


def rims_kernel(
    rows, span, modes,
    edge_ref, rim_ref, taps_ref, pole_ref, mask_ref, left_ref, right_ref,
    send_ref,
    ext_ref, line_ref, out_ref,
):
    tiles = rim_ref.shape[0]
    for n in range(tiles):
        at = lanes_of(n)
        ext_ref[0, pl.ds(0, SUB)] = left_ref[1, :, at].astype(F32)[HALO - SUB :]
        ext_ref[0, pl.ds(SUB, SUB)] = rim_ref[n, 0]
        ext_ref[1, pl.ds(0, SUB)] = left_ref[2, :, at].astype(F32)[HALO - SUB :]
        ext_ref[1, pl.ds(SUB, SUB)] = rim_ref[n, 1]
        ext_ref[2, pl.ds(0, SUB)] = rim_ref[n, 2]
        ext_ref[2, pl.ds(SUB, SUB)] = right_ref[0, :, at].astype(F32)[:SUB]
        made = []
        for e, i, side in ((0, 1, 0), (1, 2, 0), (2, 0, 1)):
            value = spread(taps_ref[i, pl.ds(0, 1), at]) * ext_ref[e, pl.ds(SUB, SUB)]
            for j in range(1, span + 1):
                value = value + spread(taps_ref[i, pl.ds(j, 1), at]) * (
                    mask_ref[side, j - 1] * ext_ref[e, pl.ds(SUB - j, SUB)]
                )
            made.append(value)
        line_ref[n, 0] = made[0] * made[1] * mask_ref[0, span]
        line_ref[n, 1] = made[2] * right_ref[3, :, at].astype(F32)[:SUB] * mask_ref[1, span]
        pole = pole_ref[:, at]
        scale, bit, left_over = jnp.ones((modes, LANES), F32), pole, rows - span
        while left_over:
            if left_over & 1:
                scale = scale * bit
            bit = bit * bit
            left_over >>= 1
        for way in range(2):
            running = jnp.zeros((modes, LANES), F32)
            for t in range(span) if way == 0 else range(span - 1, -1, -1):
                running = running * pole + spread(line_ref[n, way, pl.ds(t, 1), :])
            out_ref[way, :, at] = edge_ref[way, :, at] + scale * running
    half = out_ref.shape[2] // 2
    ahead, behind = (
        jnp.concatenate([out_ref[way, :, pl.ds(0, half)], out_ref[way, :, pl.ds(half, half)]], axis=0).astype(BF16)
        for way in range(2)
    )
    me = lax.axis_index("ctx")

    def fill(value):
        def one(d, carry):
            send_ref[d] = value
            return carry

        return one

    lax.fori_loop(0, me, fill(behind), 0)
    lax.fori_loop(me, send_ref.shape[0], fill(ahead), 0)


def local_kernel(
    steps, span, modes,
    proj_ref, cot_ref, left_ref, right_ref, taps_ref, pole_ref, res_ref, keep_ref, order_ref,
    feat_ref, sums_ref, pack_hbm, query_hbm,
    same_ref, ext_ref, chunk_ref, coef_ref, pack_ref, query_ref, out_sem,
):
    tiles, _, rows, _ = proj_ref.shape
    full_steps = steps + span
    fill_same(same_ref, keep_ref, steps, span)
    ext_ref[...] = jnp.zeros_like(ext_ref)
    sub = lax.broadcasted_iota(jnp.int32, (SUB, LANES), 0)

    def run(first, count):
        running = keep_ref[first + span]
        for r in range(first + 1, first + count):
            running = running * keep_ref[r + span]
        return running

    through = [run(0, steps), run(span + 1, steps)]
    onward = run(steps, span + 1)

    def tile_results(n):
        return (
            pltpu.make_async_copy(pack_ref.at[n], pack_hbm.at[n], out_sem.at[n, 0]),
            pltpu.make_async_copy(query_ref.at[n], query_hbm.at[n], out_sem.at[n, 1]),
        )

    def tile_step(n, carry):
        lane_at = pl.ds(pl.multiple_of(n * LANES, LANES), LANES)
        fill_ext(ext_ref, n, proj_ref, cot_ref, left_ref, right_ref, range(4))
        chunk_ref[...] = jnp.dot(order_ref[...], ext_ref[...], preferred_element_type=F32)

        def chunk(i, r):
            return chunk_ref[at_step(r + span), lanes_of(i)]

        for i in range(3):
            taps = [spread(taps_ref[i, pl.ds(j, 1), lane_at]) for j in range(span + 1)]
            for r in range(full_steps):
                value = taps[0] * chunk(i, r)
                for j in range(1, span + 1):
                    value = value + taps[j] * (same_ref[j - 1, r] * chunk(i, r - j))
                if i == 0:
                    query_ref[n, r] = value
                else:
                    feat_ref[n, i - 1, r] = value

        pole_rows = pole_ref[:, lane_at]
        coef_ref[...] = res_ref[:, lane_at] * jnp.sqrt(1.0 - pole_rows * pole_rows)
        poles = [spread(pole_ref[pl.ds(m, 1), lane_at]) for m in range(modes)]
        coefs = [spread(coef_ref[pl.ds(m, 1), :]) for m in range(modes)]
        ends = []
        res_sums = [jnp.zeros((SUB, LANES), F32)] * modes
        for way in range(2):
            state = [jnp.zeros((SUB, LANES), F32)] * modes
            for r in range(full_steps) if way == 0 else range(full_steps - 1, -1, -1):
                if way == 0:
                    keep, source = keep_ref[r + span], feat_ref[n, 0, r] * feat_ref[n, 1, r]
                else:
                    keep, source = keep_ref[r + 1 + span], chunk(3, r) * query_ref[n, r]
                state = [(poles[m] * keep) * state[m] + source for m in range(modes)]
                pack_ref[n, way * full_steps + r] = total_of(coefs[m] * state[m] for m in range(modes))
                if way == 0 and r == steps - 1 or way == 1 and r == span:
                    ends.append(state)
                if way == 1 and r < steps:
                    carried = feat_ref[n, 0, r] * feat_ref[n, 1, r]
                    res_sums = [res_sums[m] + carried * state[m] for m in range(modes)]

        for way in range(2):
            head = 0 if way == 0 else SUB - 1
            back = 1 if way == 0 else SUB - 1
            for m in range(modes):
                state = ends[way][m]
                factor = power(poles[m], steps)
                open_ = through[way]
                unit = factor * open_
                for hop in (1, 2, 4):
                    move = hop if way == 0 else SUB - hop
                    inside = sub >= hop if way == 0 else sub < SUB - hop
                    far = jnp.where(inside, pltpu.roll(state, move, 0), 0.0)
                    state = state + (factor * open_) * far
                    unit = unit * jnp.where(inside, pltpu.roll(unit, move, 0), 1.0)
                    open_ = open_ * jnp.where(inside, pltpu.roll(open_, move, 0), 1.0)
                    factor = factor * factor
                state = jnp.where(sub == head, 0.0, pltpu.roll(state, back, 0))
                unit = jnp.where(sub == head, 1.0, pltpu.roll(unit, back, 0))
                at = 2 * full_steps + way * 2 * modes + m
                pack_ref[n, at] = coefs[m] * state
                pack_ref[n, at + modes] = coefs[m] * unit
                if way == 1:
                    reach = poles[m]
                    for _ in range(span):
                        reach = reach * poles[m]
                    seen = reach * onward * ends[0][m]
                    total = jnp.sum(res_sums[m] + seen * state, axis=0, keepdims=True)
                    sums_ref[0, pl.ds(m, 1), lane_at] = total
                    sums_ref[1, pl.ds(m, 1), lane_at] = jnp.sum(seen * unit, axis=0, keepdims=True)
        for copy in tile_results(n):
            copy.start()
        return carry

    lax.fori_loop(0, tiles, tile_step, 0)
    for n in range(tiles):
        for copy in tile_results(n):
            copy.wait()


def fill_coming(coming_ref, states_ref, pick_ref, pole_ref, rows):
    shards = states_ref.shape[0]
    me = lax.axis_index("ctx")
    modes, chans = pole_ref.shape
    full = power(pole_ref[...], rows)
    half = chans // 2
    full = jnp.concatenate([full[:, :half], full[:, half:]], axis=0)

    def seen(way, j):
        return jnp.broadcast_to(pick_ref[way, pl.ds(j, 1), pl.ds(0, 1)], full.shape)

    def forward(j, state):
        return full * state + seen(0, j) * states_ref[j].astype(F32)

    def backward(n, state):
        j = shards - 1 - n
        return full * state + seen(1, j) * states_ref[j].astype(F32)

    zero = jnp.zeros(full.shape, F32)
    coming = lax.fori_loop(0, me, forward, zero)
    back = lax.fori_loop(0, shards - 1 - me, backward, zero)
    for way, state in enumerate((coming, back)):
        for n in range(chans // LANES):
            top, left = divmod(n * LANES, half)
            coming_ref[n, way] = state[top * modes : (top + 1) * modes, left : left + LANES]


def combine(way, n, steps, span, modes, pole_ref, pack_ref, coming_ref, cum_ref, lane_at):
    full_steps = steps + span
    poles = [spread(pole_ref[pl.ds(m, 1), lane_at]) for m in range(modes)]
    at = 2 * full_steps + way * 2 * modes
    state = [
        pack_ref[n, at + m] + pack_ref[n, at + modes + m] * spread(coming_ref[n, way, pl.ds(m, 1), :])
        for m in range(modes)
    ]
    for r in range(full_steps) if way == 0 else range(full_steps - 1, -1, -1):
        state = [poles[m] * state[m] for m in range(modes)]
        yield r, pack_ref[n, way * full_steps + r] + cum_ref[way, r] * total_of(state)


def sums_kernel(
    rows, steps, span, modes,
    proj_ref, cot_ref, left_ref, right_ref, pole_ref, keep_ref, order_ref, pick_ref, states_ref, feat_ref, res_ref,
    pack_hbm,
    out_ref,
    pack_ref, same_ref, cum_ref, ext_ref, chunk_ref, coming_ref, grad_ref, sums_ref, tile_sem,
):
    tiles = feat_ref.shape[0]
    shards = states_ref.shape[0]

    def load(n):
        return pltpu.make_async_copy(pack_hbm.at[n], pack_ref.at[n], tile_sem.at[n])

    for n in range(tiles):
        load(n).start()
    fill_same(same_ref, keep_ref, steps, span)
    fill_cum(cum_ref, keep_ref, steps, span)
    ext_ref[...] = jnp.zeros_like(ext_ref)
    sums_ref[...] = jnp.zeros_like(sums_ref)
    fill_coming(coming_ref, states_ref, pick_ref, pole_ref, rows)
    scale = 1.0 / math.sqrt(shards * rows)
    for n in range(tiles):
        at = lanes_of(n)
        pole = pole_ref[:, at]
        total = res_ref[0, :, at] + res_ref[1, :, at] * coming_ref[n, 1]
        sums_ref[pl.ds(3 * SUB, modes), at] = total * jnp.sqrt(1.0 - pole * pole) * scale

    def tile_step(n, carry):
        lane_at = pl.ds(pl.multiple_of(n * LANES, LANES), LANES)
        fill_ext(ext_ref, n, proj_ref, cot_ref, left_ref, right_ref, range(4))
        chunk_ref[...] = jnp.dot(order_ref[...], ext_ref[...], preferred_element_type=F32)
        load(n).wait()
        for way in range(2):
            for r, value in combine(way, n, steps, span, modes, pole_ref, pack_ref, coming_ref, cum_ref, lane_at):
                if r >= steps:
                    continue
                if way == 0:
                    grad_ref[0, r] = chunk_ref[at_step(r + span), lanes_of(3)] * value
                else:
                    grad_ref[1, r] = value * feat_ref[n, 1, r]
                    grad_ref[2, r] = value * feat_ref[n, 0, r]
        for i in range(3):
            tap_sums = [jnp.zeros((SUB, LANES), F32)] * (span + 1)
            for r in range(steps):
                here = grad_ref[i, r]
                for j in range(span + 1):
                    masked = here if j == 0 else same_ref[j - 1, r] * here
                    tap_sums[j] = tap_sums[j] + masked * chunk_ref[at_step(r - j + span), lanes_of(i)]
            for j in range(span + 1):
                sums_ref[pl.ds(i * SUB + j, 1), lane_at] = jnp.sum(tap_sums[j], axis=0, keepdims=True) * scale
        return carry

    lax.fori_loop(0, tiles, tile_step, 0)
    out_ref[...] = sums_ref[...].astype(BF16)


def outputs_kernel(
    rows, steps, span, modes,
    proj_ref, cot_ref, left_ref, right_ref, taps_ref, pole_ref, keep_ref, order_ref, pick_ref, states_ref, feat_ref,
    pack_hbm, query_hbm,
    gated_ref, grad_proj_ref,
    pack_ref, query_ref, same_ref, cum_ref, ext_ref, chunk_ref, coming_ref, grad_ref, back_ref, out_ref, tile_sem,
):
    tiles = feat_ref.shape[0]

    def loads(n):
        return (
            pltpu.make_async_copy(pack_hbm.at[n], pack_ref.at[n], tile_sem.at[n, 0]),
            pltpu.make_async_copy(query_hbm.at[n], query_ref.at[n], tile_sem.at[n, 1]),
        )

    for n in range(tiles):
        for copy in loads(n):
            copy.start()
    fill_same(same_ref, keep_ref, steps, span)
    fill_cum(cum_ref, keep_ref, steps, span)
    ext_ref[...] = jnp.zeros_like(ext_ref)
    at = lax.broadcasted_iota(jnp.int32, back_ref.shape, 0)
    col = lax.broadcasted_iota(jnp.int32, back_ref.shape, 1)
    back_ref[...] = jnp.where(at == (col & (SUB - 1)) * steps + (col >> 3), 1.0, 0.0).astype(BF16)
    fill_coming(coming_ref, states_ref, pick_ref, pole_ref, rows)

    def tile_step(n, carry):
        lane_at = pl.ds(pl.multiple_of(n * LANES, LANES), LANES)
        fill_ext(ext_ref, n, proj_ref, cot_ref, left_ref, right_ref, (3,))
        chunk_ref[...] = jnp.dot(order_ref[...], ext_ref[...], preferred_element_type=F32)
        for copy in loads(n):
            copy.wait()
        for way in range(2):
            for r, value in combine(way, n, steps, span, modes, pole_ref, pack_ref, coming_ref, cum_ref, lane_at):
                if way == 0:
                    grad_ref[0, r] = chunk_ref[at_step(r + span), :] * value
                    if r < steps:
                        out_ref[at_step(r), lanes_of(3)] = query_ref[n, r] * value
                else:
                    grad_ref[1, r] = value * feat_ref[n, 1, r]
                    grad_ref[2, r] = value * feat_ref[n, 0, r]
        for i in range(3):
            taps = [spread(taps_ref[i, pl.ds(j, 1), lane_at]) for j in range(span + 1)]
            for r in range(steps):
                value = taps[0] * grad_ref[i, r]
                for j in range(1, span + 1):
                    value = value + taps[j] * (same_ref[j - 1, r + j] * grad_ref[i, r + j])
                out_ref[at_step(r), lanes_of(i)] = value
        natural = jnp.dot(back_ref[...], out_ref[...].astype(BF16), preferred_element_type=F32).astype(BF16)
        gated_ref[:, lane_at] = natural[:, 3 * LANES :]
        for i in range(3):
            grad_proj_ref[i, :, lane_at] = natural[:, i * LANES : (i + 1) * LANES]
        return carry

    lax.fori_loop(0, tiles, tile_step, 0)


def final_kernel(parts_ref, tap_ref, res_ref):
    total = total_of(parts_ref[g].astype(F32) for g in range(parts_ref.shape[0]))
    for i in range(3):
        tap_ref[i] = total[i * SUB : i * SUB + tap_ref.shape[1]]
    res_ref[...] = total[3 * SUB :]


def per_device(projected, short_taps, pole_decay, residues, doc_lengths, cotangent):
    rows, chans = projected.shape[1:]
    taps = short_taps.shape[1]
    span = taps - 1
    modes = pole_decay.shape[0]
    docs = doc_lengths.shape[0]
    shards = lax.axis_size("ctx")
    steps = rows // SUB
    tiles = chans // LANES
    full_steps = steps + span
    chunk_rows = (full_steps + span) * SUB
    ext_rows = -(-(rows + 2 * HALO) // LANES) * LANES
    pack_shape = (tiles, 2 * full_steps + 4 * modes, SUB, LANES)
    query_shape = (tiles, full_steps, SUB, LANES)

    vmem = pl.BlockSpec(memory_space=pltpu.VMEM)
    hbm = pl.BlockSpec(memory_space=pltpu.HBM)
    free = jax.ShapeDtypeStruct
    dma = pltpu.SemaphoreType.DMA

    def in_hbm(*arrays):
        return [pltpu.with_memory_space_constraint(a, pltpu.HBM) for a in arrays]

    def in_vmem(*arrays):
        return [pltpu.with_memory_space_constraint(a, pltpu.VMEM) for a in arrays]

    def call(kernel, name, out_shape, in_specs, scratch, limit, flops):
        return pl.pallas_call(
            kernel,
            out_shape=tuple(space(shape, kind) for shape, kind, space in out_shape),
            in_specs=in_specs,
            out_specs=tuple(hbm if o[2] is pltpu.HBM else vmem for o in out_shape),
            scratch_shapes=scratch,
            compiler_params=pltpu.CompilerParams(vmem_limit_bytes=limit << 20),
            cost_estimate=pl.CostEstimate(flops=flops, bytes_accessed=4 << 20, transcendentals=0),
            name=name,
        )

    same_scratch = pltpu.VMEM((span, full_steps, SUB, LANES), F32)
    cum_scratch = pltpu.VMEM((2, full_steps, SUB, LANES), F32)
    coming_scratch = pltpu.VMEM((tiles, 2, modes, LANES), F32)

    left, right, proj, cot, taps_near, poles, weights, keeps, rim_masks, picks, order = call(
        functools.partial(load_kernel, steps, span),
        "load",
        [
            ((3, HALO, chans), BF16, free),
            ((4, HALO, chans), BF16, free),
            ((tiles, 3, rows, LANES), BF16, pltpu.VMEM),
            ((tiles, rows, LANES), BF16, pltpu.VMEM),
            ((3, taps, chans), F32, pltpu.VMEM),
            ((modes, chans), F32, pltpu.VMEM),
            ((modes, chans), F32, pltpu.VMEM),
            ((full_steps + span + 1, SUB, LANES), F32, pltpu.VMEM),
            ((2, taps, SUB, LANES), F32, pltpu.VMEM),
            ((2, shards, LANES), F32, pltpu.VMEM),
            ((chunk_rows, ext_rows), BF16, pltpu.VMEM),
        ],
        [hbm] * 6,
        [pltpu.SMEM((docs,), jnp.int32), dma((3,)), dma((4,)), dma((tiles, 2))],
        8,
        1_000_000,
    )(*in_hbm(doc_lengths, projected, cotangent, short_taps, pole_decay, residues))
    left = shift(left, 1)
    right = shift(right, -1)

    edges, rims = call(
        functools.partial(edges_kernel, steps, span, modes),
        "edges",
        [((2, modes, chans), F32, pltpu.VMEM), ((tiles, 3, SUB, LANES), F32, pltpu.VMEM)],
        [vmem] * 6,
        [
            same_scratch,
            pltpu.VMEM((2, steps, SUB, LANES), F32),
            pltpu.VMEM((rows, 4 * LANES), BF16),
            pltpu.VMEM((chunk_rows, 4 * LANES), F32),
            pltpu.VMEM((3, steps, SUB, LANES), F32),
        ],
        12,
        40_000_000,
    )(*in_vmem(proj, cot, taps_near, poles, keeps, order))

    (outgoing,) = call(
        functools.partial(rims_kernel, rows, span, modes),
        "rims",
        [((shards, 2 * modes, chans // 2), BF16, free)],
        [vmem] * 7,
        [
            pltpu.VMEM((3, 2 * SUB, LANES), F32),
            pltpu.VMEM((tiles, 2, SUB, LANES), F32),
            pltpu.VMEM((2, modes, chans), F32),
        ],
        8,
        1_000_000,
    )(*in_vmem(edges, rims, taps_near, poles, rim_masks), left, right)

    states = lax.all_to_all(outgoing, "ctx", split_axis=0, concat_axis=0, tiled=True)

    feats, res_sums, pack, query = call(
        functools.partial(local_kernel, steps, span, modes),
        "local",
        [
            ((tiles, 2, full_steps, SUB, LANES), F32, pltpu.VMEM),
            ((2, modes, chans), F32, pltpu.VMEM),
            (pack_shape, F32, pltpu.HBM),
            (query_shape, F32, pltpu.HBM),
        ],
        [vmem] * 9,
        [
            same_scratch,
            pltpu.VMEM((ext_rows, 4 * LANES), BF16),
            pltpu.VMEM((chunk_rows, 4 * LANES), F32),
            pltpu.VMEM((modes, LANES), F32),
            pltpu.VMEM(pack_shape, F32),
            pltpu.VMEM(query_shape, F32),
            dma((tiles, 2)),
        ],
        16,
        60_000_000,
    )(*in_vmem(proj, cot), left, right, *in_vmem(taps_near, poles, weights, keeps, order))

    (sums,) = call(
        functools.partial(sums_kernel, rows, steps, span, modes),
        "sums",
        [((SUM_ROWS, chans), BF16, free)],
        [vmem] * 11 + [hbm],
        [
            pltpu.VMEM(pack_shape, F32),
            same_scratch,
            cum_scratch,
            pltpu.VMEM((ext_rows, 4 * LANES), BF16),
            pltpu.VMEM((chunk_rows, 4 * LANES), F32),
            coming_scratch,
            pltpu.VMEM((3, steps, SUB, LANES), F32),
            pltpu.VMEM((SUM_ROWS, chans), F32),
            dma((tiles,)),
        ],
        12,
        30_000_000,
    )(
        *in_vmem(proj, cot),
        left,
        right,
        *in_vmem(poles, keeps, order, picks),
        states,
        *in_vmem(feats, res_sums),
        *in_hbm(pack),
    )

    near = 4
    far = shards // near

    def around(block, hop):
        return lax.ppermute(
            block, "ctx", [(i, i // near * near + (i + hop) % near) for i in range(shards)]
        )

    one, two, three = (around(sums, hop).astype(F32) for hop in (1, 2, 3))
    part = ((sums.astype(F32) + two) + (one + three)).astype(BF16)
    groups = [[f * near + n for f in range(far)] for n in range(near)]
    spread_part = lax.optimization_barrier(jnp.broadcast_to(part[None], (far, SUM_ROWS, chans)))
    gathered = lax.all_to_all(spread_part, "ctx", 0, 0, tiled=True, axis_index_groups=groups)
    grad_tap, grad_res = call(
        final_kernel,
        "final",
        [((3, taps, chans), F32, free), ((modes, chans), F32, free)],
        [vmem],
        [],
        8,
        100_000,
    )(gathered)

    gated, grad_proj = call(
        functools.partial(outputs_kernel, rows, steps, span, modes),
        "outputs",
        [((rows, chans), BF16, free), ((3, rows, chans), BF16, free)],
        [vmem] * 11 + [hbm] * 2,
        [
            pltpu.VMEM(pack_shape, F32),
            pltpu.VMEM(query_shape, F32),
            same_scratch,
            cum_scratch,
            pltpu.VMEM((ext_rows, LANES), BF16),
            pltpu.VMEM((chunk_rows, LANES), F32),
            coming_scratch,
            pltpu.VMEM((3, full_steps, SUB, LANES), F32),
            pltpu.VMEM((rows, rows), BF16),
            pltpu.VMEM((rows, 4 * LANES), F32),
            dma((tiles, 2)),
        ],
        16,
        40_000_000,
    )(
        *in_vmem(proj, cot),
        left,
        right,
        *in_vmem(taps_near, poles, keeps, order, picks),
        states,
        *in_vmem(feats),
        *in_hbm(pack, query),
    )
    return (gated, grad_proj, grad_tap, grad_res)


def solution(mesh):
    placed = (
        P(None, "ctx", "tp"),
        P(None, None, "tp"),
        P(None, "tp"),
        P(None, "tp"),
        P(),
        P("ctx", "tp"),
    )
    return jax.shard_map(
        per_device,
        mesh=mesh,
        in_specs=placed,
        out_specs=(P("ctx", "tp"), P(None, "ctx", "tp"), P(None, None, "tp"), P(None, "tp")),
        check_vma=False,
    )
```

time: 512 us -> 65.8 us (0.13); the launches traced: 505 us -> 65.4 us
  blocking collectives: 185 us -> 0 us
  local copies, waits for them, and re-layouts: 173 us -> 0.72 us
  other arithmetic: 68.9 us -> 0.02 us
  Pallas kernels: 0 us -> 23 us
  matrix products: 17 us -> 0 us
  starting transfers between devices: 35.5 us -> 26.7 us
  waiting for transfers between devices: 22.4 us -> 14.3 us
    psum x1 -> x0, blocking collectives: 142 us -> none  [per_device(): lax.psum(tap_part.astype(jnp.bfloat16), 'ctx').astype(jnp.float32)]
    slice x71 -> x0, local copies, waits for them, and re-layouts: 45.3 us -> none  [the longest x56 30.7 us: stretch_summary(): lax.associative_scan(compose, (pass_factors, end_states), axis=0)]
    all_gather x1 -> x0, blocking collectives: 43.8 us -> none  [per_device(): grad_res = lax.all_gather(res_part, 'ctx', axis=1, tiled=True)]
    pad x32 -> x0, local copies, waits for them, and re-layouts: 36.4 us -> none  [stretch_summary(): lax.associative_scan(compose, (pass_factors, end_states), axis=0)]
    rev x4 -> x0, local copies, waits for them, and re-layouts: 31.6 us -> none  [the longest x1 21.3 us: per_device(): owned_grad[::-1]]
    unnamed x167 -> x0, local copies, waits for them, and re-layouts: 28.8 us -> none
    pallas_call x0 -> x7, Pallas kernels: none -> 23 us  [the longest x1 6.37 us: per_device(): call(functools.partial(outputs_kernel, rows, steps, span, modes), 'output...]
    add x45 -> x0, other arithmetic: 20.3 us -> none  [the longest x20 10.1 us: compose(): return (earlier[0] * later[0], earlier[1] * later[0] + later[1])]
  transfers between devices with their start and end apart: 6 -> 7, of which waited for: 2 -> 5; matrix products, arithmetic and copies ran while one was open for 6% -> 0% of each run, Pallas kernels for 0% -> 23%
where the time goes in v2:
time: 65.8 us; the launch traced here: 65.4 us
  starting transfers between devices  26.7 us (41%)
  Pallas kernels  23 us (35%)
  waiting for transfers between devices  14.3 us (22%)
  between operations  0.73 us (1%)
  local copies, waits for them, and re-layouts  0.72 us (1%)
    all_to_all x1, starting transfers between devices, per_device(): lax.all_to_all(outgoing, 'ctx', split_axis=0, concat_axis=0, tiled=True)  14 us
    pallas_call x1, Pallas kernels, per_device(): call(functools.partial(outputs_kernel, rows, steps, span, modes), 'output...  6.37 us
    all_to_all x1, waiting for transfers between devices, per_device(): lax.all_to_all(outgoing, 'ctx', split_axis=0, concat_axis=0, tiled=True)  6.14 us
    pallas_call x1, Pallas kernels, per_device(): call(functools.partial(local_kernel, steps, span, modes), 'local', [((til...  5.88 us
    ppermute x2, starting transfers between devices, shift(): return lax.ppermute(block, 'ctx', route)  5.84 us
    pallas_call x1, Pallas kernels, per_device(): call(functools.partial(sums_kernel, rows, steps, span, modes), 'sums', [(...  4.9 us
    ppermute x3, waiting for transfers between devices, around(): lax.ppermute(block, 'ctx', [(i, i // near * near + (i + hop) % near) for...  4.11 us
    all_to_all x1, waiting for transfers between devices, per_device(): lax.all_to_all(spread_part, 'ctx', 0, 0, tiled=True, axis_index_groups=gr...  4.01 us
  transfers between devices with their start and end apart: 7, of which 5 were waited for; matrix products, arithmetic and copies ran while one was open for 0% of the time, Pallas kernels for 23%

profile of v2, /device:TPU:2, one launch (start us, length us, event | category | flops | bytes accessed | tf_op | source)
XLA Modules:
  0.0 65.4 jit_solution(218819983040629618)
XLA Ops:
  0.6 1.5 %load.1 = (bf16[3,16,512]{2,1,0:T(8,128)(2,1)S(1)}, bf16[4,16,512]{2,1,0:T(8,128)(2,1)S(1)}, bf16[4,3,256,128]{3,2,1,0:T(8,128)(2,1)S(1)}, bf16[4,256,128]{2,1,0...) custom-call(s32[16]{0:T(128)} %lens_hbm.1, ...), custom_call_target="tpu_custom_call" | custom-call | flops 1000000 | bytes 4194304 | tf_op jit(solution)/shard_map/load/pallas_call | solution.py:602
  2.1 1.3 %collective-permute-start.1 = (bf16[4,16,512]{2,1,0:T(8,128)(2,1)S(1)}, bf16[4,16,512]{2,1,0:T(8,128)(2,1)S(1)}, u32[]{:S(2)}, u32[]{:S(2)}) collective-permute-start(bf16[4,16,512]{2,1,0:T(8,128)(2,1)S(1)} %get-tuple-element.28), channel_id=1, source_target_pairs={{8,0},{16,8},{24,16},{32,24},{40,32},{48,40},{56,48},{64,56},{72,6... | collective-permute-start | bytes 196616 | tf_op jit(solution)/shard_map/ppermute | solution.py:22
  3.4 4.5 %collective-permute-start = (bf16[3,16,512]{2,1,0:T(8,128)(2,1)S(1)}, bf16[3,16,512]{2,1,0:T(8,128)(2,1)S(1)}, u32[]{:S(2)}, u32[]{:S(2)}) collective-permute-start(bf16[3,16,512]{2,1,0:T(8,128)(2,1)S(1)} %get-tuple-element.27), channel_id=1, source_target_pairs={{0,8},{8,16},{16,24},{24,32},{32,40},{40,48},{48,56},{56,64},{64,7... | collective-permute-start | bytes 147464 | tf_op jit(solution)/shard_map/ppermute | solution.py:22
  8.0 2.7 %edges.1 = (f32[2,8,512]{2,1,0:T(8,128)S(1)}, f32[4,3,8,128]{3,2,1,0:T(8,128)S(1)}) custom-call(bf16[4,3,256,128]{3,2,1,0:T(8,128)(2,1)S(1)} %get-tuple-element.25.proj_ref, bf16[4,256,128]{2,1,0:T(8,128)(2,1)S(1)} %get-tuple-element.26.cot_ref, f32[3,7,512]{2,1,0:T(8,128)S(1)} %get-tuple-element.29.taps_ref, f32[8,512]{1,0:T(8,128)S(1)} %get-tuple-element.30.pole_ref, ...), custom_call_target="tpu_custom_call" | custom-call | flops 40000000 | bytes 4194304 | tf_op jit(solution)/shard_map/edges/pallas_call | solution.py:626
  10.7 0.0 collective-permute-done.left_ref
  10.7 0.0 collective-permute-done.1.right_ref
  10.7 1.0 %rims.1 = bf16[32,16,256]{2,1,0:T(8,128)(2,1)} custom-call(f32[2,8,512]{2,1,0:T(8,128)S(1)} %get-tuple-element.34.edge_ref, f32[4,3,8,128]{3,2,1,0:T(8,128)S(1)} %get-tuple-element.35.rim_ref, f32[3,7,512]{2,1,0:T(8,128)S(1)} %get-tuple-element.29.taps_ref, f32[8,512]{1,0:T(8,128)S(1)} %get-tuple-element.30.pole_ref, ...), custom_call_target="tpu_custom_call" | custom-call | flops 1000000 | bytes 4194304 | tf_op jit(solution)/shard_map/rims/pallas_call | solution.py:642
  11.7 14.0 %all-to-all-start = ((bf16[32,16,256]{2,1,0:T(8,128)(2,1)}), bf16[32,16,256]{2,1,0:T(8,128)(2,1)S(1)}, u32[]{:S(2)}, u32[]{:S(2)}) async-start(bf16[32,16,256]{2,1,0:T(8,128)(2,1)} %rims.1), calls=%async_computation | async-start | bytes 524288 | tf_op jit(solution)/shard_map/all_to_all | solution.py:656
  25.7 5.9 %local.1 = (f32[4,2,38,8,128]{4,3,2,1,0:T(8,128)S(1)}, f32[2,8,512]{2,1,0:T(8,128)S(1)}, f32[4,108,8,128]{3,2,1,0:T(8,128)}, f32[4,38,8,128]{3,2,1,0:T(8,128)}) custom-call(bf16[4,3,256,128]{3,2,1,0:T(8,128)(2,1)S(1)} %get-tuple-element.25.proj_ref, bf16[4,256,128]{2,1,0:T(8,128)(2,1)S(1)} %get-tuple-element.26.cot_ref, ...), custom_call_target="tpu_custom_call" | custom-call | flops 60000000 | bytes 4194304 | tf_op jit(solution)/shard_map/local/pallas_call | solution.py:658
  31.6 6.1 %all-to-all-done.states_ref = bf16[32,16,256]{2,1,0:T(8,128)(2,1)S(1)} async-done(((bf16[32,16,256]{2,1,0:T(8,128)(2,1)}), bf16[32,16,256]{2,1,0:T(8,128)(2,1)S(1)}, u32[]{:S(2)}, u32[]{:S(2)}) %all-to-all-start) | async-done | bytes 262176 | tf_op jit(solution)/shard_map/all_to_all | solution.py:656
  37.8 4.9 %sums.1 = bf16[32,512]{1,0:T(8,128)(2,1)S(1)} custom-call(bf16[4,3,256,128]{3,2,1,0:T(8,128)(2,1)S(1)} %get-tuple-element.25.proj_ref, bf16[4,256,128]{2,1,0:T(8,128)(2,1)S(1)} %get-tuple-element.26.cot_ref, bf16[3,16,512]{2,1,0:T(8,128)(2,1)S(1)} %collective-permute-done.left_ref, bf16[4,16,512]{2,1,0:T(8,128)(2,1)S(1)} %collective-permute-done.1.right_ref, ...), custom_call_target="tpu_custom_call" | custom-call | flops 30000000 | bytes 4194304 | tf_op jit(solution)/shard_map/sums/pallas_call | solution.py:681
  42.7 1.2 %collective-permute-start.4 = (bf16[32,512]{1,0:T(8,128)(2,1)S(1)}, bf16[32,512]{1,0:T(8,128)(2,1)S(1)}, u32[]{:S(2)}, u32[]{:S(2)}) collective-permute-start(bf16[32,512]{1,0:T(8,128)(2,1)S(1)} %sums.1), channel_id=1, source_target_pairs={{0,24},{8,0},{16,8},{24,16},{32,56},{40,32},{48,40},{56,48},{64,88... | collective-permute-start | bytes 98312 | tf_op jit(solution)/shard_map/ppermute | solution.py:713
  43.9 0.9 %collective-permute-start.3 = (bf16[32,512]{1,0:T(8,128)(2,1)S(1)}, bf16[32,512]{1,0:T(8,128)(2,1)S(1)}, u32[]{:S(2)}, u32[]{:S(2)}) collective-permute-start(bf16[32,512]{1,0:T(8,128)(2,1)S(1)} %sums.1), channel_id=1, source_target_pairs={{0,8},{8,16},{16,24},{24,0},{32,40},{40,48},{48,56},{56,32},{64,72... | collective-permute-start | bytes 98312 | tf_op jit(solution)/shard_map/ppermute | solution.py:713
  44.8 1.3 %collective-permute-start.2 = (bf16[32,512]{1,0:T(8,128)(2,1)S(1)}, bf16[32,512]{1,0:T(8,128)(2,1)S(1)}, u32[]{:S(2)}, u32[]{:S(2)}) collective-permute-start(bf16[32,512]{1,0:T(8,128)(2,1)S(1)} %sums.1), channel_id=1, source_target_pairs={{0,16},{8,24},{16,0},{24,8},{32,48},{40,56},{48,32},{56,40},{64,80... | collective-permute-start | bytes 98312 | tf_op jit(solution)/shard_map/ppermute | solution.py:713
  46.1 0.6 collective-permute-done.4
  46.7 2.3 %collective-permute-done.3 = bf16[32,512]{1,0:T(8,128)(2,1)S(1)} collective-permute-done((bf16[32,512]{1,0:T(8,128)(2,1)S(1)}, bf16[32,512]{1,0:T(8,128)(2,1)S(1)}, u32[]{:S(2)}, u32[]{:S(2)}) %collective-permute-start.3) | collective-permute-done | bytes 32800 | tf_op jit(solution)/shard_map/ppermute | solution.py:713
  49.0 1.2 %collective-permute-done.2 = bf16[32,512]{1,0:T(8,128)(2,1)S(1)} collective-permute-done((bf16[32,512]{1,0:T(8,128)(2,1)S(1)}, bf16[32,512]{1,0:T(8,128)(2,1)S(1)}, u32[]{:S(2)}, u32[]{:S(2)}) %collective-permute-start.2) | collective-permute-done | bytes 32800 | tf_op jit(solution)/shard_map/ppermute | solution.py:713
  50.2 0.7 %broadcast_in_dim.2 = bf16[8,32,512]{2,1,0:T(8,128)(2,1)} broadcast(bf16[32,512]{1,0:T(8,128)(2,1)S(1)} %add_convert_fusion), dimensions={1,2} | broadcast | bytes 294912 | tf_op jit(solution)/shard_map/broadcast_in_dim | solution.py:720
  51.0 3.4 %all-to-all-start.1 = ((bf16[8,32,512]{2,1,0:T(8,128)(2,1)}), bf16[8,32,512]{2,1,0:T(8,128)(2,1)S(1)}, u32[]{:S(2)}, u32[]{:S(2)}) async-start(bf16[8,32,512]{2,1,0:T(8,128)(2,1)} %broadcast_in_dim.2), calls=%async_computation.1 | async-start | bytes 524288 | tf_op jit(solution)/shard_map/all_to_all | solution.py:721
  54.4 6.4 %outputs.1 = (bf16[256,512]{1,0:T(8,128)(2,1)}, bf16[3,256,512]{2,1,0:T(8,128)(2,1)}) custom-call(bf16[4,3,256,128]{3,2,1,0:T(8,128)(2,1)S(1)} %get-tuple-element.25.proj_ref, bf16[4,256,128]{2,1,0:T(8,128)(2,1)S(1)} %get-tuple-element.26.cot_ref, bf16[3,16,512]{2,1,0:T(8,128)(2,1)S(1)} %collective-permute-done.left_ref, ...), custom_call_target="tpu_custom_call" | custom-call | flops 40000000 | bytes 4194304 | tf_op jit(solution)/shard_map/outputs/pallas_call | solution.py:732
  60.7 4.0 %all-to-all-done.1.parts_ref = bf16[8,32,512]{2,1,0:T(8,128)(2,1)S(1)} async-done(((bf16[8,32,512]{2,1,0:T(8,128)(2,1)}), bf16[8,32,512]{2,1,0:T(8,128)(2,1)S(1)}, u32[]{:S(2)}, u32[]{:S(2)}) %all-to-all-start.1) | async-done | bytes 262176 | tf_op jit(solution)/shard_map/all_to_all | solution.py:721
  64.8 0.6 final.1
  (1 shorter events, 0.0 us)
Async XLA Ops:
  2.1 8.6 %collective-permute-start.1 = (bf16[4,16,512]{2,1,0:T(8,128)(2,1)S(1)}, bf16[4,16,512]{2,1,0:T(8,128)(2,1)S(1)}, u32[]{:S(2)}, u32[]{:S(2)}) collective-permute-start(bf16[4,16,512]{2,1,0:T(8,128)(2,1)S(1)} %get-tuple-element.28), channel_id=1, source_target_pairs={{8,0},{16,8},{24,16},{32,24},{40,32},{48,40},{56,48},{64,56},{72,6... | collective-permute-start | bytes 196616 | tf_op jit(solution)/shard_map/ppermute | solution.py:22
  3.4 7.3 %collective-permute-start = (bf16[3,16,512]{2,1,0:T(8,128)(2,1)S(1)}, bf16[3,16,512]{2,1,0:T(8,128)(2,1)S(1)}, u32[]{:S(2)}, u32[]{:S(2)}) collective-permute-start(bf16[3,16,512]{2,1,0:T(8,128)(2,1)S(1)} %get-tuple-element.27), channel_id=1, source_target_pairs={{0,8},{8,16},{16,24},{24,32},{32,40},{40,48},{48,56},{56,64},{64,7... | collective-permute-start | bytes 147464 | tf_op jit(solution)/shard_map/ppermute | solution.py:22
  11.7 26.1 %all-to-all-start = ((bf16[32,16,256]{2,1,0:T(8,128)(2,1)}), bf16[32,16,256]{2,1,0:T(8,128)(2,1)S(1)}, u32[]{:S(2)}, u32[]{:S(2)}) async-start(bf16[32,16,256]{2,1,0:T(8,128)(2,1)} %rims.1), calls=%async_computation | async-start | bytes 524288 | tf_op jit(solution)/shard_map/all_to_all | solution.py:656
  42.7 4.0 %collective-permute-start.4 = (bf16[32,512]{1,0:T(8,128)(2,1)S(1)}, bf16[32,512]{1,0:T(8,128)(2,1)S(1)}, u32[]{:S(2)}, u32[]{:S(2)}) collective-permute-start(bf16[32,512]{1,0:T(8,128)(2,1)S(1)} %sums.1), channel_id=1, source_target_pairs={{0,24},{8,0},{16,8},{24,16},{32,56},{40,32},{48,40},{56,48},{64,88... | collective-permute-start | bytes 98312 | tf_op jit(solution)/shard_map/ppermute | solution.py:713
  43.9 5.1 %collective-permute-start.3 = (bf16[32,512]{1,0:T(8,128)(2,1)S(1)}, bf16[32,512]{1,0:T(8,128)(2,1)S(1)}, u32[]{:S(2)}, u32[]{:S(2)}) collective-permute-start(bf16[32,512]{1,0:T(8,128)(2,1)S(1)} %sums.1), channel_id=1, source_target_pairs={{0,8},{8,16},{16,24},{24,0},{32,40},{40,48},{48,56},{56,32},{64,72... | collective-permute-start | bytes 98312 | tf_op jit(solution)/shard_map/ppermute | solution.py:713
  44.8 5.4 %collective-permute-start.2 = (bf16[32,512]{1,0:T(8,128)(2,1)S(1)}, bf16[32,512]{1,0:T(8,128)(2,1)S(1)}, u32[]{:S(2)}, u32[]{:S(2)}) collective-permute-start(bf16[32,512]{1,0:T(8,128)(2,1)S(1)} %sums.1), channel_id=1, source_target_pairs={{0,16},{8,24},{16,0},{24,8},{32,48},{40,56},{48,32},{56,40},{64,80... | collective-permute-start | bytes 98312 | tf_op jit(solution)/shard_map/ppermute | solution.py:713
  51.0 13.8 %all-to-all-start.1 = ((bf16[8,32,512]{2,1,0:T(8,128)(2,1)}), bf16[8,32,512]{2,1,0:T(8,128)(2,1)S(1)}, u32[]{:S(2)}, u32[]{:S(2)}) async-start(bf16[8,32,512]{2,1,0:T(8,128)(2,1)} %broadcast_in_dim.2), calls=%async_computation.1 | async-start | bytes 524288 | tf_op jit(solution)/shard_map/all_to_all | solution.py:721

commit v3 on v2

v3 whole, which is shorter than its diff:
```python
import functools
import math

import jax
import jax.numpy as jnp
from jax import lax
from jax.experimental import pallas as pl
from jax.experimental.pallas import tpu as pltpu
from jax.sharding import PartitionSpec as P

F32 = jnp.float32
BF16 = jnp.bfloat16
SUB = 8
LANES = 128
HALO = 16
SUM_ROWS = 32
MAX_DOC = 4096


def shift(block, distance):
    count = lax.axis_size("ctx")
    route = [(i, i + distance) for i in range(count) if 0 <= i + distance < count]
    return lax.ppermute(block, "ctx", route)


def spread(line):
    return jnp.broadcast_to(line, (SUB, LANES))


def power(base, exponent):
    for _ in range(int(math.log2(exponent))):
        base = base * base
    return base


def total_of(terms):
    terms = list(terms)
    while len(terms) > 1:
        terms = [a + b for a, b in zip(terms[::2], terms[1::2])] + terms[len(terms) & ~1 :]
    return terms[0]


def doc_ends(lens_ref):
    ends, total = [], jnp.int32(0)
    for d in range(lens_ref.shape[0]):
        total = total + lens_ref[d]
        ends.append(total)
    return ends


def keep_at(token, ends):
    starts = token == 0
    for end in ends:
        starts = jnp.logical_or(starts, token == end)
    return jnp.where(starts, 0.0, 1.0)


def fill_keep(keep_ref, ends, start, steps, span):
    token = lax.broadcasted_iota(jnp.int32, (SUB, LANES), 0) * steps + start
    for r in range(-span, steps + span):
        keep_ref[r + span] = keep_at(token + r, ends)


def fill_same(same_ref, keep_ref, span):
    for r in range(same_ref.shape[1]):
        running = keep_ref[r + span]
        same_ref[0, r] = running
        for j in range(2, span + 1):
            running = running * keep_ref[r + span - j + 1]
            same_ref[j - 1, r] = running


def fill_cum(cum_ref, keep_ref, steps, span):
    running = jnp.ones((SUB, LANES), F32)
    for r in range(steps):
        running = running * keep_ref[r + span]
        cum_ref[0, r] = running
    running = jnp.ones((SUB, LANES), F32)
    for r in range(steps - 1, -1, -1):
        running = running * keep_ref[r + 1 + span]
        cum_ref[1, r] = running


def fill_pick(pick_ref, ends, start, rows):
    shards = pick_ref.shape[1]
    last_start, next_start = jnp.int32(0), jnp.int32(shards * rows)
    for end in ends:
        last_start = jnp.where(end < start, jnp.maximum(last_start, end), last_start)
        next_start = jnp.where(end > start + rows, jnp.minimum(next_start, end), next_start)
    owner = lax.broadcasted_iota(jnp.int32, pick_ref.shape[1:], 0) * rows
    pick_ref[0] = jnp.where(owner + rows > last_start, 1.0, 0.0)
    pick_ref[1] = jnp.where(owner < next_start, 1.0, 0.0)


def fill_order(order_ref, steps):
    at = lax.broadcasted_iota(jnp.int32, order_ref.shape, 0)
    col = lax.broadcasted_iota(jnp.int32, order_ref.shape, 1)
    order_ref[...] = jnp.where((at & (SUB - 1)) * steps + (at >> 3) == col, 1.0, 0.0).astype(BF16)


def fill_rim_masks(mask_ref, ends, start, rows, span):
    last_start, next_start = jnp.int32(0), jnp.int32(1 << 30)
    for end in ends:
        last_start = jnp.where(end < start + rows, jnp.maximum(last_start, end), last_start)
        next_start = jnp.where(end > start, jnp.minimum(next_start, end), next_start)
    sub = lax.broadcasted_iota(jnp.int32, (SUB, LANES), 0)
    token = start + sub
    running = jnp.ones((SUB, LANES), F32)
    for j in range(span):
        running = running * keep_at(token - j, ends)
        mask_ref[j] = running
    mask_ref[span] = jnp.where(jnp.logical_and(sub < span, token >= last_start), 1.0, 0.0)
    mask_ref[span + 1] = jnp.where(jnp.logical_and(sub < span, token < next_start), 1.0, 0.0)


def at_step(r):
    return pl.ds(r * SUB, SUB)


def lanes_of(i):
    return pl.ds(i * LANES, LANES)


def load_kernel(
    steps, span,
    lens_hbm, proj_hbm, cot_hbm, taps_hbm, pole_hbm, res_hbm,
    left_ref, proj_ref, cot_ref, taps_ref, pole_ref, res_ref, keep_ref, rim_mask_ref, pick_ref, order_ref,
    lens_ref, small_sem, tile_sem,
):
    tiles, _, rows, _ = proj_ref.shape
    lens_copy = pltpu.make_async_copy(lens_hbm, lens_ref, small_sem.at[0])
    copies = [
        pltpu.make_async_copy(proj_hbm.at[:, pl.ds(rows - HALO, HALO), :], left_ref, small_sem.at[4]),
        pltpu.make_async_copy(taps_hbm, taps_ref, small_sem.at[1]),
        pltpu.make_async_copy(pole_hbm, pole_ref, small_sem.at[2]),
        pltpu.make_async_copy(res_hbm, res_ref, small_sem.at[3]),
    ]
    for n in range(tiles):
        at = lanes_of(n)
        copies.append(pltpu.make_async_copy(proj_hbm.at[:, :, at], proj_ref.at[n], tile_sem.at[n, 0]))
        copies.append(pltpu.make_async_copy(cot_hbm.at[:, at], cot_ref.at[n], tile_sem.at[n, 1]))
    lens_copy.start()
    for copy in copies:
        copy.start()
    fill_order(order_ref, steps)
    lens_copy.wait()
    start = lax.axis_index("ctx") * rows
    ends = doc_ends(lens_ref)
    fill_keep(keep_ref, ends, start, steps, span)
    fill_rim_masks(rim_mask_ref, ends, start, rows, span)
    fill_pick(pick_ref, ends, start, rows)
    for copy in copies:
        copy.wait()


def fir_steps(span, first, last, value_at, same_ref, taps):
    windows = [[value_at(i, first - 1 - j) for j in range(span)] for i in range(len(taps))]
    for r in range(first, last):
        same = [same_ref[j - 1, r] for j in range(1, span + 1)]
        results = []
        for i, stream_taps in enumerate(taps):
            windows[i] = [value_at(i, r)] + windows[i][:span]
            terms = [stream_taps[j] * (same[j - 1] * windows[i][j]) for j in range(1, span + 1)]
            results.append(total_of([stream_taps[0] * windows[i][0]] + terms))
        yield r, results


def fill_chunks(chunk_ref, tokens_ref, n, left_ref, streams, steps, span):
    sub = lax.broadcasted_iota(jnp.int32, (SUB, LANES), 0)
    lane_at = pl.ds(pl.multiple_of(n * LANES, LANES), LANES)
    for place, i in enumerate(streams):
        values = []
        for r in range(0, steps, 2):
            pair = tokens_ref[n, pl.ds(r * SUB, 2 * SUB), lanes_of(i)].astype(F32)
            values += [pair[:SUB], pair[SUB:]]
        for r in range(steps):
            chunk_ref[place, r + span] = values[r]
        for r in range(span if i < 3 else 0):
            halo = spread(left_ref[i, pl.ds(SUB - span + r, 1), lane_at])
            chunk_ref[place, r] = jnp.where(sub == 0, halo, pltpu.roll(values[steps - span + r], 1, 0))


def edges_kernel(
    steps, span, modes,
    proj_ref, cot_ref, taps_ref, pole_ref, keep_ref, order_ref,
    edge_ref, rim_ref, tokens_ref,
    same_ref, mask_ref, ext_ref, chunk_ref, feat_ref,
):
    tiles, _, rows, _ = proj_ref.shape
    fill_same(same_ref, keep_ref, span)
    sub = lax.broadcasted_iota(jnp.int32, (SUB, LANES), 0)
    running = jnp.ones((SUB, LANES), F32)
    ahead = jnp.where(sub == 0, 0.0, 1.0)
    for r in range(steps - 1, -1, -1):
        mask_ref[0, r] = running if r >= span else ahead * running
        running = running * keep_ref[r + span]
    through = [running]
    running = jnp.ones((SUB, LANES), F32)
    for r in range(steps):
        mask_ref[1, r] = running if r >= span else ahead * running
        running = running * keep_ref[r + 1 + span]
    through.append(running)

    def tile_step(n, carry):
        for i in range(4):
            ext_ref[:, lanes_of(i)] = proj_ref[n, i] if i < 3 else cot_ref[n]
        chunk_ref[...] = jnp.dot(order_ref[...], ext_ref[...], preferred_element_type=F32)
        tokens_ref[n] = chunk_ref[...].astype(BF16)
        for i in range(4):
            rim_ref[n, i] = ext_ref[pl.ds(0, HALO), lanes_of(i)].astype(F32)[:SUB]

        def chunk(i, r):
            value = chunk_ref[at_step(r % steps), lanes_of(i)]
            return value if r >= 0 else pltpu.roll(value, 1, 0)

        lane_at = pl.ds(pl.multiple_of(n * LANES, LANES), LANES)
        taps = [[spread(taps_ref[i, pl.ds(j, 1), lane_at]) for j in range(span + 1)] for i in range(3)]
        for r, (query, key, value) in fir_steps(span, 0, steps, chunk, same_ref, taps):
            feat_ref[0, r] = key * value * mask_ref[0, r]
            feat_ref[1, r] = query * chunk(3, r) * mask_ref[1, r]

        poles = [spread(pole_ref[pl.ds(m, 1), lane_at]) for m in range(modes)]
        for way in range(2):
            state = [jnp.zeros((SUB, LANES), F32)] * modes
            for r in range(steps) if way == 0 else range(steps - 1, -1, -1):
                source = feat_ref[way, r]
                state = [poles[m] * state[m] + source for m in range(modes)]
            open_ = through[way]
            factors = [power(poles[m], steps) for m in range(modes)]
            for hop in (1, 2, 4):
                move = hop if way == 0 else SUB - hop
                for m in range(modes):
                    state[m] = state[m] + (factors[m] * open_) * pltpu.roll(state[m], move, 0)
                    factors[m] = factors[m] * factors[m]
                open_ = open_ * pltpu.roll(open_, move, 0)
            last = SUB - 1 if way == 0 else 0
            for m in range(modes):
                edge_ref[way, pl.ds(m, 1), lane_at] = state[m][last : last + 1]
        return carry

    lax.fori_loop(0, tiles, tile_step, 0)


def rims_kernel(
    rows, span, modes,
    edge_ref, rim_ref, taps_ref, pole_ref, mask_ref, left_ref,
    send_ref, left_out_ref,
    ext_ref, line_ref, out_ref,
):
    tiles = rim_ref.shape[0]
    for n in range(tiles):
        at = lanes_of(n)
        made = []
        for i in range(3):
            left_out_ref[i, :, at] = left_ref[i, :, at].astype(F32)[HALO - SUB :]
            ext_ref[i, pl.ds(0, SUB)] = left_out_ref[i, :, at]
            ext_ref[i, pl.ds(SUB, SUB)] = rim_ref[n, i]
            value = spread(taps_ref[i, pl.ds(0, 1), at]) * rim_ref[n, i]
            for j in range(1, span + 1):
                value = value + spread(taps_ref[i, pl.ds(j, 1), at]) * (mask_ref[j - 1] * ext_ref[i, pl.ds(SUB - j, SUB)])
            made.append(value)
        line_ref[n, 0] = made[1] * made[2] * mask_ref[span]
        line_ref[n, 1] = made[0] * rim_ref[n, 3] * mask_ref[span + 1]
        pole = pole_ref[:, at]
        scale, bit, left_over = jnp.ones((modes, LANES), F32), pole, rows - span
        while left_over:
            if left_over & 1:
                scale = scale * bit
            bit = bit * bit
            left_over >>= 1
        for way in range(2):
            running = jnp.zeros((modes, LANES), F32)
            for t in range(span) if way == 0 else range(span - 1, -1, -1):
                running = running * pole + spread(line_ref[n, way, pl.ds(t, 1), :])
            out_ref[way, :, at] = edge_ref[way, :, at] + (scale * running if way == 0 else running)
    half = out_ref.shape[2] // 2
    ahead, behind = (
        jnp.concatenate([out_ref[way, :, pl.ds(0, half)], out_ref[way, :, pl.ds(half, half)]], axis=0).astype(BF16)
        for way in range(2)
    )
    me = lax.axis_index("ctx")

    def fill(value):
        def one(d, carry):
            send_ref[d] = value
            return carry

        return one

    lax.fori_loop(0, me, fill(behind), 0)
    lax.fori_loop(me, send_ref.shape[0], fill(ahead), 0)


def local_kernel(
    steps, span, modes,
    tokens_ref, left_ref, taps_ref, pole_ref, res_ref, keep_ref,
    feat_ref, sums_ref, pack_first_ref, pack_hbm, query_hbm,
    same_ref, chunk_ref, coef_ref, pack_ref, query_ref, out_sem,
):
    tiles = tokens_ref.shape[0]
    fill_same(same_ref, keep_ref, span)
    sub = lax.broadcasted_iota(jnp.int32, (SUB, LANES), 0)

    def run(first, count):
        running = keep_ref[first + span]
        for r in range(first + 1, first + count):
            running = running * keep_ref[r + span]
        return running

    through = [run(0, steps), run(1, steps)]
    onward = keep_ref[steps + span]

    def tile_results(n):
        return (
            pltpu.make_async_copy(pack_ref.at[n], pack_hbm.at[n], out_sem.at[n, 0]),
            pltpu.make_async_copy(query_ref.at[n], query_hbm.at[n], out_sem.at[n, 1]),
        )

    def tile_step(n, carry):
        lane_at = pl.ds(pl.multiple_of(n * LANES, LANES), LANES)
        fill_chunks(chunk_ref, tokens_ref, n, left_ref, range(4), steps, span)

        def chunk(i, r):
            return chunk_ref[i, r + span]

        taps = [[spread(taps_ref[i, pl.ds(j, 1), lane_at]) for j in range(span + 1)] for i in range(3)]
        for r, (query, key, value) in fir_steps(span, 0, steps, chunk, same_ref, taps):
            query_ref[n, r] = query
            feat_ref[n, 0, r] = key
            feat_ref[n, 1, r] = value

        pole_rows = pole_ref[:, lane_at]
        coef_ref[...] = res_ref[:, lane_at] * jnp.sqrt(1.0 - pole_rows * pole_rows)
        poles = [spread(pole_ref[pl.ds(m, 1), lane_at]) for m in range(modes)]
        coefs = [spread(coef_ref[pl.ds(m, 1), :]) for m in range(modes)]
        ends = []
        res_sums = [jnp.zeros((SUB, LANES), F32)] * modes
        for way in range(2):
            state = [jnp.zeros((SUB, LANES), F32)] * modes
            for r in range(steps) if way == 0 else range(steps - 1, -1, -1):
                if way == 0:
                    keep, source = keep_ref[r + span], feat_ref[n, 0, r] * feat_ref[n, 1, r]
                else:
                    keep, source = keep_ref[r + 1 + span], chunk(3, r) * query_ref[n, r]
                state = [(poles[m] * keep) * state[m] + source for m in range(modes)]
                pack_ref[n, way * steps + r] = total_of(coefs[m] * state[m] for m in range(modes))
                if way == 1:
                    carried = feat_ref[n, 0, r] * feat_ref[n, 1, r]
                    res_sums = [res_sums[m] + carried * state[m] for m in range(modes)]
            ends.append(state)

        for way in range(2):
            head = 0 if way == 0 else SUB - 1
            back = 1 if way == 0 else SUB - 1
            for m in range(modes):
                state = ends[way][m]
                factor = power(poles[m], steps)
                open_ = through[way]
                unit = factor * open_
                for hop in (1, 2, 4):
                    move = hop if way == 0 else SUB - hop
                    inside = sub >= hop if way == 0 else sub < SUB - hop
                    far = jnp.where(inside, pltpu.roll(state, move, 0), 0.0)
                    state = state + (factor * open_) * far
                    unit = unit * jnp.where(inside, pltpu.roll(unit, move, 0), 1.0)
                    open_ = open_ * jnp.where(inside, pltpu.roll(open_, move, 0), 1.0)
                    factor = factor * factor
                state = jnp.where(sub == head, 0.0, pltpu.roll(state, back, 0))
                unit = jnp.where(sub == head, 1.0, pltpu.roll(unit, back, 0))
                at = 2 * steps + way * 2 * modes + m
                pack_ref[n, at] = coefs[m] * state
                pack_ref[n, at + modes] = coefs[m] * unit
                if way == 1:
                    seen = poles[m] * onward * ends[0][m]
                    total = jnp.sum(res_sums[m] + seen * state, axis=0, keepdims=True)
                    sums_ref[0, pl.ds(m, 1), lane_at] = total
                    sums_ref[1, pl.ds(m, 1), lane_at] = jnp.sum(seen * unit, axis=0, keepdims=True)
        for copy in tile_results(n):
            copy.start()
        return carry

    lax.fori_loop(0, tiles, tile_step, 0)
    pack_first_ref[...] = pack_ref[0]
    for n in range(tiles):
        for copy in tile_results(n):
            copy.wait()


def fill_coming(coming_ref, states_ref, pick_ref, pole_ref, rows):
    shards = states_ref.shape[0]
    me = lax.axis_index("ctx")
    modes, chans = pole_ref.shape
    full = power(pole_ref[...], rows)
    half = chans // 2
    full = jnp.concatenate([full[:, :half], full[:, half:]], axis=0)
    weight = jnp.ones(full.shape, F32)
    totals = [jnp.zeros(full.shape, F32)] * 2
    for hop in range(1, min(shards - 1, -(-MAX_DOC // rows)) + 1):
        for way, j in enumerate((me - hop, me + hop)):
            inside = jnp.logical_and(j >= 0, j < shards).astype(F32)
            held = jnp.clip(j, 0, shards - 1)
            seen = jnp.broadcast_to(pick_ref[way, pl.ds(held, 1), :], full.shape) * inside
            totals[way] = totals[way] + (weight * seen) * states_ref[held].astype(F32)
        weight = weight * full
    for way, state in enumerate(totals):
        for n in range(chans // LANES):
            top, left = divmod(n * LANES, half)
            coming_ref[n, way] = state[top * modes : (top + 1) * modes, left : left + LANES]


def combine(way, n, steps, modes, pole_ref, pack_ref, coming_ref, cum_ref, lane_at):
    poles = [spread(pole_ref[pl.ds(m, 1), lane_at]) for m in range(modes)]
    at = 2 * steps + way * 2 * modes
    state = [
        pack_ref[n, at + m] + pack_ref[n, at + modes + m] * spread(coming_ref[n, way, pl.ds(m, 1), :])
        for m in range(modes)
    ]
    for r in range(steps) if way == 0 else range(steps - 1, -1, -1):
        state = [poles[m] * state[m] for m in range(modes)]
        yield r, pack_ref[n, way * steps + r] + cum_ref[way, r] * total_of(state)


def sums_kernel(
    rows, steps, span, modes,
    tokens_ref, left_ref, pole_ref, keep_ref, pick_ref, states_ref, feat_ref, res_ref, pack_first_ref, pack_hbm,
    out_ref, rim_ref,
    pack_ref, same_ref, cum_ref, chunk_ref, coming_ref, grad_ref, sums_ref, line_ref, tile_sem,
):
    tiles = feat_ref.shape[0]
    shards = states_ref.shape[0]

    def load(n):
        return pltpu.make_async_copy(pack_hbm.at[n], pack_ref.at[n], tile_sem.at[n])

    for n in range(1, tiles):
        load(n).start()
    pack_ref[0] = pack_first_ref[...]
    fill_same(same_ref, keep_ref, span)
    fill_cum(cum_ref, keep_ref, steps, span)
    sums_ref[...] = jnp.zeros_like(sums_ref)
    line_ref[...] = jnp.zeros_like(line_ref)
    fill_coming(coming_ref, states_ref, pick_ref, pole_ref, rows)
    scale = 1.0 / math.sqrt(shards * rows)

    def tile_step(n, carry):
        lane_at = pl.ds(pl.multiple_of(n * LANES, LANES), LANES)
        fill_chunks(chunk_ref, tokens_ref, n, left_ref, range(4), steps, span)

        @pl.when(n > 0)
        def _():
            load(n).wait()

        for way in range(2):
            for r, value in combine(way, n, steps, modes, pole_ref, pack_ref, coming_ref, cum_ref, lane_at):
                if way == 0:
                    grad_ref[0, r] = chunk_ref[3, r + span] * value
                else:
                    grad_ref[1, r] = value * feat_ref[n, 1, r]
                    grad_ref[2, r] = value * feat_ref[n, 0, r]
        for i in range(3):
            for r in range(span):
                line_ref[i, pl.ds(r, 1), lane_at] = grad_ref[i, r, pl.ds(0, 1), :]
        tap_sums = [[jnp.zeros((SUB, LANES), F32)] * (span + 1)] * 3
        windows = [[chunk_ref[i, span - 1 - j] for j in range(span)] for i in range(3)]
        for r in range(steps):
            same = [same_ref[j - 1, r] for j in range(1, span + 1)]
            for i in range(3):
                here = grad_ref[i, r]
                windows[i] = [chunk_ref[i, r + span]] + windows[i][:span]
                masked = [here] + [same[j] * here for j in range(span)]
                tap_sums[i] = [tap_sums[i][j] + masked[j] * windows[i][j] for j in range(span + 1)]
        for i in range(3):
            for j in range(span + 1):
                sums_ref[pl.ds((i * SUB + j) * SUB, SUB), lane_at] = tap_sums[i][j]
        return carry

    lax.fori_loop(0, tiles, tile_step, 0)
    rim_ref[...] = line_ref[...].astype(BF16)
    shape = (3 * SUB, 3 * SUB * SUB)
    at = lax.broadcasted_iota(jnp.int32, shape, 0)
    col = lax.broadcasted_iota(jnp.int32, shape, 1)
    gather = jnp.where((col >> 3) == at, 1.0, 0.0).astype(BF16)
    high = sums_ref[...].astype(BF16)
    low = (sums_ref[...] - high.astype(F32)).astype(BF16)
    taps = jnp.dot(gather, high, preferred_element_type=F32) + jnp.dot(gather, low, preferred_element_type=F32)
    pole = pole_ref[...]
    back = jnp.concatenate([coming_ref[n, 1] for n in range(tiles)], axis=1)
    res = (res_ref[0] + res_ref[1] * back) * jnp.sqrt(1.0 - pole * pole)
    out_ref[...] = (jnp.concatenate([taps, res], axis=0) * scale).astype(BF16)


def outputs_kernel(
    rows, steps, span, modes,
    tokens_ref, taps_ref, pole_ref, keep_ref, pick_ref, states_ref, feat_ref,
    pack_hbm, query_hbm,
    gated_ref, grad_proj_ref, tail_ref, tail_mask_ref,
    pack_ref, query_ref, same_ref, cum_ref, chunk_ref, coming_ref, grad_ref, back_ref, out_ref, tile_sem,
):
    tiles = feat_ref.shape[0]

    def loads(n):
        return (
            pltpu.make_async_copy(pack_hbm.at[n], pack_ref.at[n], tile_sem.at[n, 0]),
            pltpu.make_async_copy(query_hbm.at[n], query_ref.at[n], tile_sem.at[n, 1]),
        )

    for n in range(tiles):
        for copy in loads(n):
            copy.start()
    fill_same(same_ref, keep_ref, span)
    fill_cum(cum_ref, keep_ref, steps, span)
    at = lax.broadcasted_iota(jnp.int32, back_ref.shape, 0)
    col = lax.broadcasted_iota(jnp.int32, back_ref.shape, 1)
    sub = lax.broadcasted_iota(jnp.int32, (SUB, LANES), 0)
    back_ref[...] = jnp.where(at == (col & (SUB - 1)) * steps + (col >> 3), 1.0, 0.0).astype(BF16)
    fill_coming(coming_ref, states_ref, pick_ref, pole_ref, rows)

    def tile_step(n, carry):
        lane_at = pl.ds(pl.multiple_of(n * LANES, LANES), LANES)
        fill_chunks(chunk_ref, tokens_ref, n, None, (3,), steps, span)
        for copy in loads(n):
            copy.wait()
        for way in range(2):
            for r, value in combine(way, n, steps, modes, pole_ref, pack_ref, coming_ref, cum_ref, lane_at):
                if way == 0:
                    grad_ref[0, r] = chunk_ref[0, r + span] * value
                    out_ref[at_step(r), lanes_of(3)] = query_ref[n, r] * value
                else:
                    grad_ref[1, r] = value * feat_ref[n, 1, r]
                    grad_ref[2, r] = value * feat_ref[n, 0, r]
        for i in range(3):
            for r in range(span):
                grad_ref[i, steps + r] = jnp.where(sub == SUB - 1, 0.0, pltpu.roll(grad_ref[i, r], SUB - 1, 0))
        taps = [[spread(taps_ref[i, pl.ds(j, 1), lane_at]) for j in range(span + 1)] for i in range(3)]
        windows = [[grad_ref[i, r] for r in range(span)] for i in range(3)]
        for r in range(steps):
            same = [same_ref[j - 1, r + j] for j in range(1, span + 1)]
            for i in range(3):
                windows[i] = windows[i][-span:] + [grad_ref[i, r + span]]
                terms = [taps[i][j] * (same[j - 1] * windows[i][j]) for j in range(1, span + 1)]
                out_ref[at_step(r), lanes_of(i)] = total_of([taps[i][0] * windows[i][0]] + terms)
        for i in range(3):
            for r in range(steps - HALO, steps):
                last = out_ref[pl.ds(r * SUB + SUB - 1, 1), lanes_of(i)]
                tail_ref[i, pl.ds(r - steps + HALO, 1), lane_at] = last
        natural = jnp.dot(back_ref[...], out_ref[...].astype(BF16), preferred_element_type=F32).astype(BF16)
        gated_ref[:, lane_at] = natural[:, 3 * LANES :]
        for i in range(3):
            grad_proj_ref[i, :, lane_at] = natural[:, i * LANES : (i + 1) * LANES]
        return carry

    lax.fori_loop(0, tiles, tile_step, 0)
    for j in range(1, span + 1):
        for r in range(span):
            tail_mask_ref[j - 1, pl.ds(r, 1), :] = same_ref[j - 1, steps + r, pl.ds(SUB - 1, 1), :]


def tail_kernel(rows, span, partial_hbm, tail_ref, rim_ref, taps_ref, mask_ref, grad_proj_hbm, line_ref, sem):
    sub = lax.broadcasted_iota(jnp.int32, (SUB, LANES), 0)
    for n in range(rim_ref.shape[2] // LANES):
        at = lanes_of(n)
        for i in range(3):
            behind = rim_ref[i, :, at].astype(F32)[:SUB]
            value = tail_ref[i, pl.ds(HALO - SUB, SUB), at]
            for j in range(1, span + 1):
                added = spread(taps_ref[i, pl.ds(j, 1), at]) * (mask_ref[j - 1] * behind)
                value = value + pltpu.roll(jnp.where(sub < j, added, 0.0), SUB - j, 0)
            whole = jnp.concatenate([tail_ref[i, pl.ds(0, HALO - SUB), at], value], axis=0)
            line_ref[i, :, at] = whole.astype(BF16)
    copy = pltpu.make_async_copy(line_ref, grad_proj_hbm.at[:, pl.ds(rows - HALO, HALO), :], sem)
    copy.start()
    copy.wait()


def spread_kernel(one_ref, two_ref, three_ref, own_ref, out_ref):
    own, one, two, three = (ref[...].astype(F32) for ref in (own_ref, one_ref, two_ref, three_ref))
    total = ((own + two) + (one + three)).astype(BF16)
    for g in range(out_ref.shape[0]):
        out_ref[g] = total


def final_kernel(parts_ref, tap_ref, res_ref):
    total = total_of(parts_ref[g].astype(F32) for g in range(parts_ref.shape[0]))
    for i in range(3):
        tap_ref[i] = total[i * SUB : i * SUB + tap_ref.shape[1]]
    res_ref[...] = total[3 * SUB :]


def per_device(projected, short_taps, pole_decay, residues, doc_lengths, cotangent):
    rows, chans = projected.shape[1:]
    taps = short_taps.shape[1]
    span = taps - 1
    modes = pole_decay.shape[0]
    docs = doc_lengths.shape[0]
    shards = lax.axis_size("ctx")
    steps = rows // SUB
    tiles = chans // LANES
    full_steps = steps + span
    pack_shape = (tiles, 2 * steps + 4 * modes, SUB, LANES)
    query_shape = (tiles, steps, SUB, LANES)

    vmem = pl.BlockSpec(memory_space=pltpu.VMEM)
    hbm = pl.BlockSpec(memory_space=pltpu.HBM)
    free = jax.ShapeDtypeStruct
    dma = pltpu.SemaphoreType.DMA

    def in_hbm(*arrays):
        return [pltpu.with_memory_space_constraint(a, pltpu.HBM) for a in arrays]

    def in_vmem(*arrays):
        return [pltpu.with_memory_space_constraint(a, pltpu.VMEM) for a in arrays]

    def call(kernel, name, out_shape, in_specs, scratch, limit, flops, aliases=None):
        return pl.pallas_call(
            kernel,
            out_shape=tuple(space(shape, kind) for shape, kind, space in out_shape),
            in_specs=in_specs,
            out_specs=tuple(hbm if o[2] is pltpu.HBM else vmem for o in out_shape),
            scratch_shapes=scratch,
            input_output_aliases=aliases or {},
            compiler_params=pltpu.CompilerParams(vmem_limit_bytes=limit << 20),
            cost_estimate=pl.CostEstimate(flops=flops, bytes_accessed=4 << 20, transcendentals=0),
            name=name,
        )

    same_scratch = pltpu.VMEM((span, steps, SUB, LANES), F32)
    cum_scratch = pltpu.VMEM((2, steps, SUB, LANES), F32)
    chunk_scratch = pltpu.VMEM((4, full_steps, SUB, LANES), F32)
    coming_scratch = pltpu.VMEM((tiles, 2, modes, LANES), F32)

    left, proj, cot, taps_near, poles, weights, keeps, rim_masks, picks, order = call(
        functools.partial(load_kernel, steps, span),
        "load",
        [
            ((3, HALO, chans), BF16, free),
            ((tiles, 3, rows, LANES), BF16, pltpu.VMEM),
            ((tiles, rows, LANES), BF16, pltpu.VMEM),
            ((3, taps, chans), F32, pltpu.VMEM),
            ((modes, chans), F32, pltpu.VMEM),
            ((modes, chans), F32, pltpu.VMEM),
            ((full_steps + span, SUB, LANES), F32, pltpu.VMEM),
            ((taps + 1, SUB, LANES), F32, pltpu.VMEM),
            ((2, shards, chans // 2), F32, pltpu.VMEM),
            ((rows, rows), BF16, pltpu.VMEM),
        ],
        [hbm] * 6,
        [pltpu.SMEM((docs,), jnp.int32), dma((5,)), dma((tiles, 2))],
        8,
        1_000_000,
    )(*in_hbm(doc_lengths, projected, cotangent, short_taps, pole_decay, residues))
    left = shift(left, 1)

    edges, rims, tokens = call(
        functools.partial(edges_kernel, steps, span, modes),
        "edges",
        [
            ((2, modes, chans), F32, pltpu.VMEM),
            ((tiles, 4, SUB, LANES), F32, pltpu.VMEM),
            ((tiles, rows, 4 * LANES), BF16, pltpu.VMEM),
        ],
        [vmem] * 6,
        [
            same_scratch,
            pltpu.VMEM((2, steps, SUB, LANES), F32),
            pltpu.VMEM((rows, 4 * LANES), BF16),
            pltpu.VMEM((rows, 4 * LANES), F32),
            pltpu.VMEM((2, steps, SUB, LANES), F32),
        ],
        12,
        40_000_000,
    )(*in_vmem(proj, cot, taps_near, poles, keeps, order))

    outgoing, left = call(
        functools.partial(rims_kernel, rows, span, modes),
        "rims",
        [
            ((shards, 2 * modes, chans // 2), BF16, pltpu.VMEM),
            ((3, SUB, chans), F32, pltpu.VMEM),
        ],
        [vmem] * 6,
        [
            pltpu.VMEM((3, 2 * SUB, LANES), F32),
            pltpu.VMEM((tiles, 2, SUB, LANES), F32),
            pltpu.VMEM((2, modes, chans), F32),
        ],
        8,
        1_000_000,
    )(*in_vmem(edges, rims, taps_near, poles, rim_masks), left)

    states = lax.all_to_all(outgoing, "ctx", split_axis=0, concat_axis=0, tiled=True)

    feats, res_sums, pack_first, pack, query = call(
        functools.partial(local_kernel, steps, span, modes),
        "local",
        [
            ((tiles, 2, steps, SUB, LANES), F32, pltpu.VMEM),
            ((2, modes, chans), F32, pltpu.VMEM),
            (pack_shape[1:], F32, pltpu.VMEM),
            (pack_shape, F32, pltpu.HBM),
            (query_shape, F32, pltpu.HBM),
        ],
        [vmem] * 6,
        [
            same_scratch,
            chunk_scratch,
            pltpu.VMEM((modes, LANES), F32),
            pltpu.VMEM(pack_shape, F32),
            pltpu.VMEM(query_shape, F32),
            dma((tiles, 2)),
        ],
        16,
        60_000_000,
    )(*in_vmem(tokens, left, taps_near, poles, weights, keeps))

    sums, ahead = call(
        functools.partial(sums_kernel, rows, steps, span, modes),
        "sums",
        [((SUM_ROWS, chans), BF16, free), ((3, HALO, chans), BF16, free)],
        [vmem] * 9 + [hbm],
        [
            pltpu.VMEM(pack_shape, F32),
            same_scratch,
            cum_scratch,
            chunk_scratch,
            coming_scratch,
            pltpu.VMEM((3, steps, SUB, LANES), F32),
            pltpu.VMEM((3 * SUB * SUB, chans), F32),
            pltpu.VMEM((3, HALO, chans), F32),
            dma((tiles,)),
        ],
        12,
        30_000_000,
    )(
        *in_vmem(tokens, left, poles, keeps, picks),
        states,
        *in_vmem(feats, res_sums, pack_first),
        *in_hbm(pack),
    )

    behind = shift(ahead, -1)

    near = 4
    far = shards // near

    def around(block, hop):
        return lax.ppermute(
            block, "ctx", [(i, i // near * near + (i + hop) % near) for i in range(shards)]
        )

    (parts,) = call(
        spread_kernel, "spread", [((far, SUM_ROWS, chans), BF16, pltpu.VMEM)], [vmem] * 4, [], 4, 100_000
    )(*(around(sums, hop) for hop in (1, 2, 3)), sums)
    groups = [[f * near + n for f in range(far)] for n in range(near)]
    gathered = lax.all_to_all(parts, "ctx", 0, 0, tiled=True, axis_index_groups=groups)
    grad_tap, grad_res = call(
        final_kernel,
        "final",
        [((3, taps, chans), F32, free), ((modes, chans), F32, free)],
        [vmem],
        [],
        8,
        100_000,
    )(gathered)

    gated, grad_proj, tail, tail_mask = call(
        functools.partial(outputs_kernel, rows, steps, span, modes),
        "outputs",
        [
            ((rows, chans), BF16, free),
            ((3, rows, chans), BF16, free),
            ((3, HALO, chans), F32, pltpu.VMEM),
            ((span, SUB, LANES), F32, pltpu.VMEM),
        ],
        [vmem] * 7 + [hbm] * 2,
        [
            pltpu.VMEM(pack_shape, F32),
            pltpu.VMEM(query_shape, F32),
            pltpu.VMEM((span, full_steps, SUB, LANES), F32),
            cum_scratch,
            pltpu.VMEM((1, full_steps, SUB, LANES), F32),
            coming_scratch,
            pltpu.VMEM((3, full_steps, SUB, LANES), F32),
            pltpu.VMEM((rows, rows), BF16),
            pltpu.VMEM((rows, 4 * LANES), F32),
            dma((tiles, 2)),
        ],
        16,
        40_000_000,
    )(
        *in_vmem(tokens, taps_near, poles, keeps, picks),
        states,
        *in_vmem(feats),
        *in_hbm(pack, query),
    )
    (grad_proj,) = call(
        functools.partial(tail_kernel, rows, span),
        "tail",
        [((3, rows, chans), BF16, pltpu.HBM)],
        [hbm] + [vmem] * 4,
        [pltpu.VMEM((3, HALO, chans), BF16), dma],
        4,
        500_000,
        aliases={0: 0},
    )(*in_hbm(grad_proj), *in_vmem(tail), behind, *in_vmem(taps_near, tail_mask))
    return (gated, grad_proj, grad_tap, grad_res)


def solution(mesh):
    placed = (
        P(None, "ctx", "tp"),
        P(None, None, "tp"),
        P(None, "tp"),
        P(None, "tp"),
        P(),
        P("ctx", "tp"),
    )
    return jax.shard_map(
        per_device,
        mesh=mesh,
        in_specs=placed,
        out_specs=(P("ctx", "tp"), P(None, "ctx", "tp"), P(None, None, "tp"), P(None, "tp")),
        check_vma=False,
    )
```

time: 65.8 us -> 58.6 us (0.89)
  Pallas kernels: 23 us -> 18.8 us
  starting transfers between devices: 26.7 us -> 22.9 us
  waiting for transfers between devices: 14.3 us -> 15.8 us
  local copies, waits for them, and re-layouts: 0.72 us -> 0 us
    pallas_call x1, Pallas kernels: 4.9 us -> 2.62 us  [per_device(): call(functools.partial(sums_kernel, rows, steps, span, modes), 'sums', [(...]
    all_to_all x1, starting transfers between devices: 14 us -> 11.9 us  [per_device(): lax.all_to_all(outgoing, 'ctx', split_axis=0, concat_axis=0, tiled=True)]
    all_to_all x1, waiting for transfers between devices: 6.14 us -> 8.03 us  [per_device(): lax.all_to_all(outgoing, 'ctx', split_axis=0, concat_axis=0, tiled=True)]
    pallas_call x1, Pallas kernels: 5.88 us -> 4.13 us  [per_device(): call(functools.partial(local_kernel, steps, span, modes), 'local', [((til...]
    pallas_call x1, Pallas kernels: 6.37 us -> 4.91 us  [per_device(): call(functools.partial(outputs_kernel, rows, steps, span, modes), 'output...]
    pallas_call x0 -> x2, Pallas kernels: none -> 1.42 us  [the longest x1 0.73 us: per_device(): call(spread_kernel, 'spread', [((far, SUM_ROWS, chans), BF16, pltpu.VMEM)...]
    ppermute x2, starting transfers between devices: 5.84 us -> 4.77 us  [shift(): return lax.ppermute(block, 'ctx', route)]
    broadcast_in_dim x1 -> x0, local copies, waits for them, and re-layouts: 0.72 us -> none  [per_device(): jnp.broadcast_to(part[None], (far, SUM_ROWS, chans))]
  transfers between devices with their start and end apart: 7 -> 7, of which waited for: 5 -> 5; matrix products, arithmetic and copies ran while one was open for 0% -> 0% of each run, Pallas kernels for 23% -> 21%
where the time goes in v3:
time: 58.6 us; the launch traced here: 58.3 us
  starting transfers between devices  22.9 us (39%)
  Pallas kernels  18.8 us (32%)
  waiting for transfers between devices  15.8 us (27%)
  between operations  0.73 us (1%)
    all_to_all x1, starting transfers between devices, per_device(): lax.all_to_all(outgoing, 'ctx', split_axis=0, concat_axis=0, tiled=True)  11.9 us
    all_to_all x1, waiting for transfers between devices, per_device(): lax.all_to_all(outgoing, 'ctx', split_axis=0, concat_axis=0, tiled=True)  8.03 us
    pallas_call x1, Pallas kernels, per_device(): call(functools.partial(outputs_kernel, rows, steps, span, modes), 'output...  4.91 us
    ppermute x2, starting transfers between devices, shift(): return lax.ppermute(block, 'ctx', route)  4.77 us
    ppermute x3, waiting for transfers between devices, around(): lax.ppermute(block, 'ctx', [(i, i // near * near + (i + hop) % near) for...  4.27 us
    pallas_call x1, Pallas kernels, per_device(): call(functools.partial(local_kernel, steps, span, modes), 'local', [((til...  4.13 us
    all_to_all x1, waiting for transfers between devices, per_device(): lax.all_to_all(parts, 'ctx', 0, 0, tiled=True, axis_index_groups=groups)  3.46 us
    all_to_all x1, starting transfers between devices, per_device(): lax.all_to_all(parts, 'ctx', 0, 0, tiled=True, axis_index_groups=groups)  3.41 us
  transfers between devices with their start and end apart: 7, of which 5 were waited for; matrix products, arithmetic and copies ran while one was open for 0% of the time, Pallas kernels for 21%

profile of v3, /device:TPU:2, one launch (start us, length us, event | category | flops | bytes accessed | tf_op | source)
XLA Modules:
  0.0 58.3 jit_solution(9096546059398063326)
XLA Ops:
  0.6 1.4 %load.1 = (bf16[3,16,512]{2,1,0:T(8,128)(2,1)S(1)}, bf16[4,3,256,128]{3,2,1,0:T(8,128)(2,1)S(1)}, bf16[4,256,128]{2,1,0:T(8,128)(2,1)S(1)}, f32[3,7,512]{2,1,0:T...) custom-call(s32[16]{0:T(128)} %lens_hbm.1, ...), custom_call_target="tpu_custom_call" | custom-call | flops 1000000 | bytes 4194304 | tf_op jit(solution)/shard_map/load/pallas_call | solution.py:631
  2.1 3.5 %collective-permute-start = (bf16[3,16,512]{2,1,0:T(8,128)(2,1)S(1)}, bf16[3,16,512]{2,1,0:T(8,128)(2,1)S(1)}, u32[]{:S(2)}, u32[]{:S(2)}) collective-permute-start(bf16[3,16,512]{2,1,0:T(8,128)(2,1)S(1)} %get-tuple-element.43), channel_id=1, source_target_pairs={{0,8},{8,16},{16,24},{24,32},{32,40},{40,48},{48,56},{56,64},{64,7... | collective-permute-start | bytes 147464 | tf_op jit(solution)/shard_map/ppermute | solution.py:23
  5.6 2.7 %edges.1 = (f32[2,8,512]{2,1,0:T(8,128)S(1)}, f32[4,4,8,128]{3,2,1,0:T(8,128)S(1)}, bf16[4,256,512]{2,1,0:T(8,128)(2,1)S(1)}) custom-call(bf16[4,3,256,128]{3,2,1,0:T(8,128)(2,1)S(1)} %get-tuple-element.32.proj_ref, bf16[4,256,128]{2,1,0:T(8,128)(2,1)S(1)} %get-tuple-element.33.cot_ref, f32[3,7,512]{2,1,0:T(8,128)S(1)} %get-tuple-element.34.taps_ref, ...), custom_call_target="tpu_custom_call" | custom-call | flops 40000000 | bytes 4194304 | tf_op jit(solution)/shard_map/edges/pallas_call | solution.py:653
  8.3 0.0 collective-permute-done.left_ref
  8.3 1.0 %rims.1 = (bf16[32,16,256]{2,1,0:T(8,128)(2,1)}, f32[3,8,512]{2,1,0:T(8,128)S(1)}) custom-call(f32[2,8,512]{2,1,0:T(8,128)S(1)} %get-tuple-element.40.edge_ref, f32[4,4,8,128]{3,2,1,0:T(8,128)S(1)} %get-tuple-element.41.rim_ref, f32[3,7,512]{2,1,0:T(8,128)S(1)} %get-tuple-element.34.taps_ref, f32[8,512]{1,0:T(8,128)S(1)} %get-tuple-element.35.pole_ref, ...), custom_call_target="tpu_custom_call" | custom-call | flops 1000000 | bytes 4194304 | tf_op jit(solution)/shard_map/rims/pallas_call | solution.py:673
  9.3 11.9 %all-to-all-start = ((bf16[32,16,256]{2,1,0:T(8,128)(2,1)}), bf16[32,16,256]{2,1,0:T(8,128)(2,1)S(1)}, u32[]{:S(2)}, u32[]{:S(2)}) async-start(bf16[32,16,256]{2,1,0:T(8,128)(2,1)} %get-tuple-element.44), calls=%async_computation | async-start | bytes 524288 | tf_op jit(solution)/shard_map/all_to_all | solution.py:690
  21.2 4.1 %local.1 = (f32[4,2,32,8,128]{4,3,2,1,0:T(8,128)S(1)}, f32[2,8,512]{2,1,0:T(8,128)S(1)}, f32[96,8,128]{2,1,0:T(8,128)S(1)}, f32[4,96,8,128]{3,2,1,0:T(8,128)}, f32[4,32,8,128]{3,2,1,0:T(8,128)}) custom-call(bf16[4,256,512]{2,1,0:T(8,128)(2,1)S(1)} %get-tuple-element.38.tokens_ref, f32[3,8,512]{2,1,0:T(8,128)S(1)} %get-tuple-element.45.left_ref, ...), custom_call_target="tpu_custom_call" | custom-call | flops 60000000 | bytes 4194304 | tf_op jit(solution)/shard_map/local/pallas_call | solution.py:692
  25.4 8.0 %all-to-all-done.states_ref = bf16[32,16,256]{2,1,0:T(8,128)(2,1)S(1)} async-done(((bf16[32,16,256]{2,1,0:T(8,128)(2,1)}), bf16[32,16,256]{2,1,0:T(8,128)(2,1)S(1)}, u32[]{:S(2)}, u32[]{:S(2)}) %all-to-all-start) | async-done | bytes 262176 | tf_op jit(solution)/shard_map/all_to_all | solution.py:690
  33.4 2.6 %sums.1 = (bf16[32,512]{1,0:T(8,128)(2,1)S(1)}, bf16[3,16,512]{2,1,0:T(8,128)(2,1)S(1)}) custom-call(bf16[4,256,512]{2,1,0:T(8,128)(2,1)S(1)} %get-tuple-element.38.tokens_ref, f32[3,8,512]{2,1,0:T(8,128)S(1)} %get-tuple-element.45.left_ref, f32[8,512]{1,0:T(8,128)S(1)} %get-tuple-element.35.pole_ref, f32[44,8,128]{2,1,0:T(8,128)S(1)} %get-tuple-element.36.keep_ref, ...), custom_call_target="tpu_custom_call" | custom-call | flops 30000000 | bytes 4194304 | tf_op jit(solution)/shard_map/sums/pallas_call | solution.py:715
  36.0 1.2 %collective-permute-start.4 = (bf16[32,512]{1,0:T(8,128)(2,1)S(1)}, bf16[32,512]{1,0:T(8,128)(2,1)S(1)}, u32[]{:S(2)}, u32[]{:S(2)}) collective-permute-start(bf16[32,512]{1,0:T(8,128)(2,1)S(1)} %get-tuple-element.57.own_ref), channel_id=1, source_target_pairs={{0,24},{8,0},{16,8},{24,16},{32,56},{40,32},{48,40},{56,48},{64,88... | collective-permute-start | bytes 98312 | tf_op jit(solution)/shard_map/ppermute | solution.py:746
  37.2 0.8 %collective-permute-start.3 = (bf16[32,512]{1,0:T(8,128)(2,1)S(1)}, bf16[32,512]{1,0:T(8,128)(2,1)S(1)}, u32[]{:S(2)}, u32[]{:S(2)}) collective-permute-start(bf16[32,512]{1,0:T(8,128)(2,1)S(1)} %get-tuple-element.57.own_ref), channel_id=1, source_target_pairs={{0,16},{8,24},{16,0},{24,8},{32,48},{40,56},{48,32},{56,40},{64,80... | collective-permute-start | bytes 98312 | tf_op jit(solution)/shard_map/ppermute | solution.py:746
  37.9 0.9 %collective-permute-start.2 = (bf16[32,512]{1,0:T(8,128)(2,1)S(1)}, bf16[32,512]{1,0:T(8,128)(2,1)S(1)}, u32[]{:S(2)}, u32[]{:S(2)}) collective-permute-start(bf16[32,512]{1,0:T(8,128)(2,1)S(1)} %get-tuple-element.57.own_ref), channel_id=1, source_target_pairs={{0,8},{8,16},{16,24},{24,0},{32,40},{40,48},{48,56},{56,32},{64,72... | collective-permute-start | bytes 98312 | tf_op jit(solution)/shard_map/ppermute | solution.py:746
  38.8 1.2 %collective-permute-done.4.three_ref = bf16[32,512]{1,0:T(8,128)(2,1)S(1)} collective-permute-done((bf16[32,512]{1,0:T(8,128)(2,1)S(1)}, bf16[32,512]{1,0:T(8,128)(2,1)S(1)}, u32[]{:S(2)}, u32[]{:S(2)}) %collective-permute-start.4) | collective-permute-done | bytes 32800 | tf_op jit(solution)/shard_map/ppermute | solution.py:746
  40.0 2.6 %collective-permute-done.3.two_ref = bf16[32,512]{1,0:T(8,128)(2,1)S(1)} collective-permute-done((bf16[32,512]{1,0:T(8,128)(2,1)S(1)}, bf16[32,512]{1,0:T(8,128)(2,1)S(1)}, u32[]{:S(2)}, u32[]{:S(2)}) %collective-permute-start.3) | collective-permute-done | bytes 32800 | tf_op jit(solution)/shard_map/ppermute | solution.py:746
  42.6 0.5 collective-permute-done.2.one_ref
  43.1 0.7 %spread.1 = bf16[8,32,512]{2,1,0:T(8,128)(2,1)} custom-call(bf16[32,512]{1,0:T(8,128)(2,1)S(1)} %collective-permute-done.2.one_ref, bf16[32,512]{1,0:T(8,128)(2,1)S(1)} %collective-permute-done.3.two_ref, bf16[32,512]{1,0:T(8,128)(2,1)S(1)} %collective-permute-done.4.three_ref, bf16[32,512]{1,0:T(8,128)(2,1)S(1)} %get-tuple-element.57.own_ref), custom_call_target="tpu_custom_call" | custom-call | flops 100000 | bytes 4194304 | tf_op jit(solution)/shard_map/spread/pallas_call | solution.py:750
  43.8 3.4 %all-to-all-start.1 = ((bf16[8,32,512]{2,1,0:T(8,128)(2,1)}), bf16[8,32,512]{2,1,0:T(8,128)(2,1)S(1)}, u32[]{:S(2)}, u32[]{:S(2)}) async-start(bf16[8,32,512]{2,1,0:T(8,128)(2,1)} %spread.1), calls=%async_computation.1 | async-start | bytes 524288 | tf_op jit(solution)/shard_map/all_to_all | solution.py:754
  47.2 1.3 %collective-permute-start.1 = (bf16[3,16,512]{2,1,0:T(8,128)(2,1)S(1)}, bf16[3,16,512]{2,1,0:T(8,128)(2,1)S(1)}, u32[]{:S(2)}, u32[]{:S(2)}) collective-permute-start(bf16[3,16,512]{2,1,0:T(8,128)(2,1)S(1)} %get-tuple-element.55), channel_id=1, source_target_pairs={{8,0},{16,8},{24,16},{32,24},{40,32},{48,40},{56,48},{64,56},{72,6... | collective-permute-start | bytes 147464 | tf_op jit(solution)/shard_map/ppermute | solution.py:23
  48.5 4.9 %outputs.1 = (bf16[256,512]{1,0:T(8,128)(2,1)}, bf16[3,256,512]{2,1,0:T(8,128)(2,1)}, f32[3,16,512]{2,1,0:T(8,128)S(1)}, f32[6,8,128]{2,1,0:T(8,128)S(1)}) custom-call(bf16[4,256,512]{2,1,0:T(8,128)(2,1)S(1)} %get-tuple-element.38.tokens_ref, f32[3,7,512]{2,1,0:T(8,128)S(1)} %get-tuple-element.34.taps_ref, f32[8,512]{1,0:T(8,128)S(1)} %get-tuple-element.35.pole_ref, ...), custom_call_target="tpu_custom_call" | custom-call | flops 40000000 | bytes 4194304 | tf_op jit(solution)/shard_map/outputs/pallas_call | solution.py:765
  53.4 0.0 collective-permute-done.1.rim_ref
  53.4 0.7 %tail.1 = bf16[3,256,512]{2,1,0:T(8,128)(2,1)} custom-call(bf16[3,256,512]{2,1,0:T(8,128)(2,1)} %get-tuple-element.51.partial_hbm, f32[3,16,512]{2,1,0:T(8,128)S(1)} %get-tuple-element.52.tail_ref, bf16[3,16,512]{2,1,0:T(8,128)(2,1)S(1)} %collective-permute-done.1.rim_ref, ...), custom_call_target="tpu_custom_call", output_to_operand_aliasing={{}: (0, {})} | custom-call | flops 500000 | bytes 4194304 | tf_op jit(solution)/shard_map/tail/pallas_call | solution.py:795
  54.1 3.5 %all-to-all-done.1.parts_ref = bf16[8,32,512]{2,1,0:T(8,128)(2,1)S(1)} async-done(((bf16[8,32,512]{2,1,0:T(8,128)(2,1)}), bf16[8,32,512]{2,1,0:T(8,128)(2,1)S(1)}, u32[]{:S(2)}, u32[]{:S(2)}) %all-to-all-start.1) | async-done | bytes 262176 | tf_op jit(solution)/shard_map/all_to_all | solution.py:754
  57.6 0.6 %final.1 = (f32[3,7,512]{2,1,0:T(8,128)}, f32[8,512]{1,0:T(8,128)}) custom-call(bf16[8,32,512]{2,1,0:T(8,128)(2,1)S(1)} %all-to-all-done.1.parts_ref), custom_call_target="tpu_custom_call" | custom-call | flops 100000 | bytes 4194304 | tf_op jit(solution)/shard_map/final/pallas_call | solution.py:755
Async XLA Ops:
  2.1 6.2 %collective-permute-start = (bf16[3,16,512]{2,1,0:T(8,128)(2,1)S(1)}, bf16[3,16,512]{2,1,0:T(8,128)(2,1)S(1)}, u32[]{:S(2)}, u32[]{:S(2)}) collective-permute-start(bf16[3,16,512]{2,1,0:T(8,128)(2,1)S(1)} %get-tuple-element.43), channel_id=1, source_target_pairs={{0,8},{8,16},{16,24},{24,32},{32,40},{40,48},{48,56},{56,64},{64,7... | collective-permute-start | bytes 147464 | tf_op jit(solution)/shard_map/ppermute | solution.py:23
  9.3 24.1 %all-to-all-start = ((bf16[32,16,256]{2,1,0:T(8,128)(2,1)}), bf16[32,16,256]{2,1,0:T(8,128)(2,1)S(1)}, u32[]{:S(2)}, u32[]{:S(2)}) async-start(bf16[32,16,256]{2,1,0:T(8,128)(2,1)} %get-tuple-element.44), calls=%async_computation | async-start | bytes 524288 | tf_op jit(solution)/shard_map/all_to_all | solution.py:690
  36.0 4.0 %collective-permute-start.4 = (bf16[32,512]{1,0:T(8,128)(2,1)S(1)}, bf16[32,512]{1,0:T(8,128)(2,1)S(1)}, u32[]{:S(2)}, u32[]{:S(2)}) collective-permute-start(bf16[32,512]{1,0:T(8,128)(2,1)S(1)} %get-tuple-element.57.own_ref), channel_id=1, source_target_pairs={{0,24},{8,0},{16,8},{24,16},{32,56},{40,32},{48,40},{56,48},{64,88... | collective-permute-start | bytes 98312 | tf_op jit(solution)/shard_map/ppermute | solution.py:746
  37.2 5.4 %collective-permute-start.3 = (bf16[32,512]{1,0:T(8,128)(2,1)S(1)}, bf16[32,512]{1,0:T(8,128)(2,1)S(1)}, u32[]{:S(2)}, u32[]{:S(2)}) collective-permute-start(bf16[32,512]{1,0:T(8,128)(2,1)S(1)} %get-tuple-element.57.own_ref), channel_id=1, source_target_pairs={{0,16},{8,24},{16,0},{24,8},{32,48},{40,56},{48,32},{56,40},{64,80... | collective-permute-start | bytes 98312 | tf_op jit(solution)/shard_map/ppermute | solution.py:746
  37.9 5.1 %collective-permute-start.2 = (bf16[32,512]{1,0:T(8,128)(2,1)S(1)}, bf16[32,512]{1,0:T(8,128)(2,1)S(1)}, u32[]{:S(2)}, u32[]{:S(2)}) collective-permute-start(bf16[32,512]{1,0:T(8,128)(2,1)S(1)} %get-tuple-element.57.own_ref), channel_id=1, source_target_pairs={{0,8},{8,16},{16,24},{24,0},{32,40},{40,48},{48,56},{56,32},{64,72... | collective-permute-start | bytes 98312 | tf_op jit(solution)/shard_map/ppermute | solution.py:746
  43.8 13.8 %all-to-all-start.1 = ((bf16[8,32,512]{2,1,0:T(8,128)(2,1)}), bf16[8,32,512]{2,1,0:T(8,128)(2,1)S(1)}, u32[]{:S(2)}, u32[]{:S(2)}) async-start(bf16[8,32,512]{2,1,0:T(8,128)(2,1)} %spread.1), calls=%async_computation.1 | async-start | bytes 524288 | tf_op jit(solution)/shard_map/all_to_all | solution.py:754
  47.2 6.2 %collective-permute-start.1 = (bf16[3,16,512]{2,1,0:T(8,128)(2,1)S(1)}, bf16[3,16,512]{2,1,0:T(8,128)(2,1)S(1)}, u32[]{:S(2)}, u32[]{:S(2)}) collective-permute-start(bf16[3,16,512]{2,1,0:T(8,128)(2,1)S(1)} %get-tuple-element.55), channel_id=1, source_target_pairs={{8,0},{16,8},{24,16},{32,24},{40,32},{48,40},{56,48},{64,56},{72,6... | collective-permute-start | bytes 147464 | tf_op jit(solution)/shard_map/ppermute | solution.py:23

commit v4 on v3

--- a/solution.py
+++ b/solution.py
@@ -90,12 +90,6 @@
     owner = lax.broadcasted_iota(jnp.int32, pick_ref.shape[1:], 0) * rows
     pick_ref[0] = jnp.where(owner + rows > last_start, 1.0, 0.0)
     pick_ref[1] = jnp.where(owner < next_start, 1.0, 0.0)
-
-
-def fill_order(order_ref, steps):
-    at = lax.broadcasted_iota(jnp.int32, order_ref.shape, 0)
-    col = lax.broadcasted_iota(jnp.int32, order_ref.shape, 1)
-    order_ref[...] = jnp.where((at & (SUB - 1)) * steps + (at >> 3) == col, 1.0, 0.0).astype(BF16)
 
 
 def fill_rim_masks(mask_ref, ends, start, rows, span):
@@ -124,7 +118,7 @@
 def load_kernel(
     steps, span,
     lens_hbm, proj_hbm, cot_hbm, taps_hbm, pole_hbm, res_hbm,
-    left_ref, proj_ref, cot_ref, taps_ref, pole_ref, res_ref, keep_ref, rim_mask_ref, pick_ref, order_ref,
+    left_ref, proj_ref, cot_ref, taps_ref, pole_ref, res_ref, keep_ref, rim_mask_ref, pick_ref,
     lens_ref, small_sem, tile_sem,
 ):
     tiles, _, rows, _ = proj_ref.shape
@@ -142,7 +136,6 @@
     lens_copy.start()
     for copy in copies:
         copy.start()
-    fill_order(order_ref, steps)
     lens_copy.wait()
     start = lax.axis_index("ctx") * rows
     ends = doc_ends(lens_ref)
@@ -182,9 +175,9 @@
 
 def edges_kernel(
     steps, span, modes,
-    proj_ref, cot_ref, taps_ref, pole_ref, keep_ref, order_ref,
+    proj_ref, cot_ref, taps_ref, pole_ref, keep_ref,
     edge_ref, rim_ref, tokens_ref,
-    same_ref, mask_ref, ext_ref, chunk_ref, feat_ref,
+    same_ref, mask_ref, chunk_ref, feat_ref,
 ):
     tiles, _, rows, _ = proj_ref.shape
     fill_same(same_ref, keep_ref, span)
@@ -203,14 +196,14 @@
 
     def tile_step(n, carry):
         for i in range(4):
-            ext_ref[:, lanes_of(i)] = proj_ref[n, i] if i < 3 else cot_ref[n]
-        chunk_ref[...] = jnp.dot(order_ref[...], ext_ref[...], preferred_element_type=F32)
-        tokens_ref[n] = chunk_ref[...].astype(BF16)
-        for i in range(4):
-            rim_ref[n, i] = ext_ref[pl.ds(0, HALO), lanes_of(i)].astype(F32)[:SUB]
+            natural = (proj_ref[n, i] if i < 3 else cot_ref[n]).astype(F32)
+            rim_ref[n, i] = natural[:SUB]
+            ordered = jnp.swapaxes(natural.reshape(SUB, steps, LANES), 0, 1)
+            chunk_ref[i] = ordered
+            tokens_ref[n, :, lanes_of(i)] = ordered.reshape(rows, LANES).astype(BF16)
 
         def chunk(i, r):
-            value = chunk_ref[at_step(r % steps), lanes_of(i)]
+            value = chunk_ref[i, r % steps]
             return value if r >= 0 else pltpu.roll(value, 1, 0)
 
         lane_at = pl.ds(pl.multiple_of(n * LANES, LANES), LANES)
@@ -238,7 +231,7 @@
                 edge_ref[way, pl.ds(m, 1), lane_at] = state[m][last : last + 1]
         return carry
 
-    lax.fori_loop(0, tiles, tile_step, 0)
+    lax.fori_loop(0, tiles, tile_step, 0, unroll=True)
 
 
 def rims_kernel(
@@ -491,40 +484,52 @@
 
 def outputs_kernel(
     rows, steps, span, modes,
-    tokens_ref, taps_ref, pole_ref, keep_ref, pick_ref, states_ref, feat_ref,
+    tokens_ref, taps_ref, pole_ref, keep_ref, pick_ref, states_ref, feat_ref, pack_first_ref,
     pack_hbm, query_hbm,
-    gated_ref, grad_proj_ref, tail_ref, tail_mask_ref,
-    pack_ref, query_ref, same_ref, cum_ref, chunk_ref, coming_ref, grad_ref, back_ref, out_ref, tile_sem,
+    gated_hbm, grad_proj_hbm, tail_ref, tail_mask_ref,
+    pack_ref, query_ref, same_ref, cum_ref, chunk_ref, coming_ref, grad_ref, out_ref, gated_ref, grad_proj_ref,
+    pack_sem, query_sem, out_sem,
 ):
     tiles = feat_ref.shape[0]
 
-    def loads(n):
+    def load_pack(n):
+        return pltpu.make_async_copy(pack_hbm.at[n], pack_ref.at[n], pack_sem.at[n])
+
+    def load_query(n):
+        return pltpu.make_async_copy(query_hbm.at[n], query_ref.at[n], query_sem.at[n])
+
+    def results(n):
+        at = pl.ds(n * LANES, LANES)
+        if not isinstance(n, int):
+            at = pl.ds(pl.multiple_of(n * LANES, LANES), LANES)
         return (
-            pltpu.make_async_copy(pack_hbm.at[n], pack_ref.at[n], tile_sem.at[n, 0]),
-            pltpu.make_async_copy(query_hbm.at[n], query_ref.at[n], tile_sem.at[n, 1]),
+            pltpu.make_async_copy(gated_ref.at[n], gated_hbm.at[:, at], out_sem.at[n, 0]),
+            pltpu.make_async_copy(grad_proj_ref.at[n], grad_proj_hbm.at[:, :, at], out_sem.at[n, 1]),
         )
 
     for n in range(tiles):
-        for copy in loads(n):
-            copy.start()
+        load_query(n).start()
+        if n > 0:
+            load_pack(n).start()
+    pack_ref[0] = pack_first_ref[...]
     fill_same(same_ref, keep_ref, span)
     fill_cum(cum_ref, keep_ref, steps, span)
-    at = lax.broadcasted_iota(jnp.int32, back_ref.shape, 0)
-    col = lax.broadcasted_iota(jnp.int32, back_ref.shape, 1)
     sub = lax.broadcasted_iota(jnp.int32, (SUB, LANES), 0)
-    back_ref[...] = jnp.where(at == (col & (SUB - 1)) * steps + (col >> 3), 1.0, 0.0).astype(BF16)
     fill_coming(coming_ref, states_ref, pick_ref, pole_ref, rows)
 
     def tile_step(n, carry):
         lane_at = pl.ds(pl.multiple_of(n * LANES, LANES), LANES)
         fill_chunks(chunk_ref, tokens_ref, n, None, (3,), steps, span)
-        for copy in loads(n):
-            copy.wait()
+
+        @pl.when(n > 0)
+        def _():
+            load_pack(n).wait()
+
         for way in range(2):
             for r, value in combine(way, n, steps, modes, pole_ref, pack_ref, coming_ref, cum_ref, lane_at):
                 if way == 0:
                     grad_ref[0, r] = chunk_ref[0, r + span] * value
-                    out_ref[at_step(r), lanes_of(3)] = query_ref[n, r] * value
+                    out_ref[3, r] = value
                 else:
                     grad_ref[1, r] = value * feat_ref[n, 1, r]
                     grad_ref[2, r] = value * feat_ref[n, 0, r]
@@ -538,24 +543,39 @@
             for i in range(3):
                 windows[i] = windows[i][-span:] + [grad_ref[i, r + span]]
                 terms = [taps[i][j] * (same[j - 1] * windows[i][j]) for j in range(1, span + 1)]
-                out_ref[at_step(r), lanes_of(i)] = total_of([taps[i][0] * windows[i][0]] + terms)
+                out_ref[i, r] = total_of([taps[i][0] * windows[i][0]] + terms)
+        gated_copy, grad_copy = results(n)
         for i in range(3):
-            for r in range(steps - HALO, steps):
-                last = out_ref[pl.ds(r * SUB + SUB - 1, 1), lanes_of(i)]
-                tail_ref[i, pl.ds(r - steps + HALO, 1), lane_at] = last
-        natural = jnp.dot(back_ref[...], out_ref[...].astype(BF16), preferred_element_type=F32).astype(BF16)
-        gated_ref[:, lane_at] = natural[:, 3 * LANES :]
-        for i in range(3):
-            grad_proj_ref[i, :, lane_at] = natural[:, i * LANES : (i + 1) * LANES]
+            natural = jnp.swapaxes(out_ref[i], 0, 1).reshape(SUB * steps, LANES)
+            tail_ref[i, :, lane_at] = natural[SUB * steps - HALO :]
+            grad_proj_ref[n, i] = natural.astype(BF16)
+        grad_copy.start()
+        load_query(n).wait()
+        gated_ref[n] = jnp.swapaxes(query_ref[n] * out_ref[3], 0, 1).reshape(SUB * steps, LANES).astype(BF16)
+        gated_copy.start()
         return carry
 
     lax.fori_loop(0, tiles, tile_step, 0)
+    for n in range(tiles):
+        for copy in results(n):
+            copy.wait()
     for j in range(1, span + 1):
         for r in range(span):
             tail_mask_ref[j - 1, pl.ds(r, 1), :] = same_ref[j - 1, steps + r, pl.ds(SUB - 1, 1), :]
 
 
-def tail_kernel(rows, span, partial_hbm, tail_ref, rim_ref, taps_ref, mask_ref, grad_proj_hbm, line_ref, sem):
+def spread_kernel(one_ref, two_ref, three_ref, own_ref, out_ref):
+    own, one, two, three = (ref[...].astype(F32) for ref in (own_ref, one_ref, two_ref, three_ref))
+    total = ((own + two) + (one + three)).astype(BF16)
+    for g in range(out_ref.shape[0]):
+        out_ref[g] = total
+
+
+def final_kernel(
+    rows, span, partial_hbm, parts_ref, tail_ref, rim_ref, taps_ref, mask_ref,
+    grad_proj_hbm, tap_hbm, res_hbm,
+    line_ref, tap_ref, res_ref, sem,
+):
     sub = lax.broadcasted_iota(jnp.int32, (SUB, LANES), 0)
     for n in range(rim_ref.shape[2] // LANES):
         at = lanes_of(n)
@@ -567,23 +587,18 @@
                 value = value + pltpu.roll(jnp.where(sub < j, added, 0.0), SUB - j, 0)
             whole = jnp.concatenate([tail_ref[i, pl.ds(0, HALO - SUB), at], value], axis=0)
             line_ref[i, :, at] = whole.astype(BF16)
-    copy = pltpu.make_async_copy(line_ref, grad_proj_hbm.at[:, pl.ds(rows - HALO, HALO), :], sem)
-    copy.start()
-    copy.wait()
-
-
-def spread_kernel(one_ref, two_ref, three_ref, own_ref, out_ref):
-    own, one, two, three = (ref[...].astype(F32) for ref in (own_ref, one_ref, two_ref, three_ref))
-    total = ((own + two) + (one + three)).astype(BF16)
-    for g in range(out_ref.shape[0]):
-        out_ref[g] = total
-
-
-def final_kernel(parts_ref, tap_ref, res_ref):
+    copies = [pltpu.make_async_copy(line_ref, grad_proj_hbm.at[:, pl.ds(rows - HALO, HALO), :], sem.at[0])]
+    copies[0].start()
     total = total_of(parts_ref[g].astype(F32) for g in range(parts_ref.shape[0]))
     for i in range(3):
         tap_ref[i] = total[i * SUB : i * SUB + tap_ref.shape[1]]
     res_ref[...] = total[3 * SUB :]
+    copies.append(pltpu.make_async_copy(tap_ref, tap_hbm, sem.at[1]))
+    copies.append(pltpu.make_async_copy(res_ref, res_hbm, sem.at[2]))
+    for copy in copies[1:]:
+        copy.start()
+    for copy in copies:
+        copy.wait()
 
 
 def per_device(projected, short_taps, pole_decay, residues, doc_lengths, cotangent):
@@ -628,7 +643,7 @@
     chunk_scratch = pltpu.VMEM((4, full_steps, SUB, LANES), F32)
     coming_scratch = pltpu.VMEM((tiles, 2, modes, LANES), F32)
 
-    left, proj, cot, taps_near, poles, weights, keeps, rim_masks, picks, order = call(
+    left, proj, cot, taps_near, poles, weights, keeps, rim_masks, picks = call(
         functools.partial(load_kernel, steps, span),
         "load",
         [
@@ -641,7 +656,6 @@
             ((full_steps + span, SUB, LANES), F32, pltpu.VMEM),
             ((taps + 1, SUB, LANES), F32, pltpu.VMEM),
             ((2, shards, chans // 2), F32, pltpu.VMEM),
-            ((rows, rows), BF16, pltpu.VMEM),
         ],
         [hbm] * 6,
         [pltpu.SMEM((docs,), jnp.int32), dma((5,)), dma((tiles, 2))],
@@ -658,17 +672,16 @@
             ((tiles, 4, SUB, LANES), F32, pltpu.VMEM),
             ((tiles, rows, 4 * LANES), BF16, pltpu.VMEM),
         ],
-        [vmem] * 6,
+        [vmem] * 5,
         [
             same_scratch,
             pltpu.VMEM((2, steps, SUB, LANES), F32),
-            pltpu.VMEM((rows, 4 * LANES), BF16),
-            pltpu.VMEM((rows, 4 * LANES), F32),
+            pltpu.VMEM((4, steps, SUB, LANES), F32),
             pltpu.VMEM((2, steps, SUB, LANES), F32),
         ],
         12,
         40_000_000,
-    )(*in_vmem(proj, cot, taps_near, poles, keeps, order))
+    )(*in_vmem(proj, cot, taps_near, poles, keeps))
 
     outgoing, left = call(
         functools.partial(rims_kernel, rows, span, modes),
@@ -752,26 +765,16 @@
     )(*(around(sums, hop) for hop in (1, 2, 3)), sums)
     groups = [[f * near + n for f in range(far)] for n in range(near)]
     gathered = lax.all_to_all(parts, "ctx", 0, 0, tiled=True, axis_index_groups=groups)
-    grad_tap, grad_res = call(
-        final_kernel,
-        "final",
-        [((3, taps, chans), F32, free), ((modes, chans), F32, free)],
-        [vmem],
-        [],
-        8,
-        100_000,
-    )(gathered)
-
     gated, grad_proj, tail, tail_mask = call(
         functools.partial(outputs_kernel, rows, steps, span, modes),
         "outputs",
         [
-            ((rows, chans), BF16, free),
-            ((3, rows, chans), BF16, free),
+            ((rows, chans), BF16, pltpu.HBM),
+            ((3, rows, chans), BF16, pltpu.HBM),
             ((3, HALO, chans), F32, pltpu.VMEM),
             ((span, SUB, LANES), F32, pltpu.VMEM),
         ],
-        [vmem] * 7 + [hbm] * 2,
+        [vmem] * 8 + [hbm] * 2,
         [
             pltpu.VMEM(pack_shape, F32),
             pltpu.VMEM(query_shape, F32),
@@ -780,8 +783,11 @@
             pltpu.VMEM((1, full_steps, SUB, LANES), F32),
             coming_scratch,
             pltpu.VMEM((3, full_steps, SUB, LANES), F32),
-            pltpu.VMEM((rows, rows), BF16),
-            pltpu.VMEM((rows, 4 * LANES), F32),
+            pltpu.VMEM((4, steps, SUB, LANES), F32),
+            pltpu.VMEM((tiles, rows, LANES), BF16),
+            pltpu.VMEM((tiles, 3, rows, LANES), BF16),
+            dma((tiles,)),
+            dma((tiles,)),
             dma((tiles, 2)),
         ],
         16,
@@ -789,19 +795,28 @@
     )(
         *in_vmem(tokens, taps_near, poles, keeps, picks),
         states,
-        *in_vmem(feats),
+        *in_vmem(feats, pack_first),
         *in_hbm(pack, query),
     )
-    (grad_proj,) = call(
-        functools.partial(tail_kernel, rows, span),
-        "tail",
-        [((3, rows, chans), BF16, pltpu.HBM)],
-        [hbm] + [vmem] * 4,
-        [pltpu.VMEM((3, HALO, chans), BF16), dma],
+    grad_proj, grad_tap, grad_res = call(
+        functools.partial(final_kernel, rows, span),
+        "final",
+        [
+            ((3, rows, chans), BF16, pltpu.HBM),
+            ((3, taps, chans), F32, pltpu.HBM),
+            ((modes, chans), F32, pltpu.HBM),
+        ],
+        [hbm] + [vmem] * 5,
+        [
+            pltpu.VMEM((3, HALO, chans), BF16),
+            pltpu.VMEM((3, taps, chans), F32),
+            pltpu.VMEM((modes, chans), F32),
+            dma((3,)),
+        ],
         4,
         500_000,
         aliases={0: 0},
-    )(*in_hbm(grad_proj), *in_vmem(tail), behind, *in_vmem(taps_near, tail_mask))
+    )(*in_hbm(grad_proj), gathered, *in_vmem(tail), behind, *in_vmem(taps_near, tail_mask))
     return (gated, grad_proj, grad_tap, grad_res)
 
 

time: 58.6 us -> 58.6 us (level)
  Pallas kernels: 18.8 us -> 16.5 us
  waiting for transfers between devices: 15.8 us -> 17.7 us
    pallas_call x1, Pallas kernels: 4.91 us -> 3.52 us  [per_device(): call(functools.partial(outputs_kernel, rows, steps, span, modes), 'output...]
    ppermute x2, waiting for transfers between devices: 0.01 us -> 1.16 us  [shift(): return lax.ppermute(block, 'ctx', route)]
    all_to_all x1, waiting for transfers between devices: 3.46 us -> 4.4 us  [per_device(): lax.all_to_all(parts, 'ctx', 0, 0, tiled=True, axis_index_groups=groups)]
    pallas_call x2 -> x1, Pallas kernels: 1.34 us -> 0.73 us  [per_device(): call(functools.partial(final_kernel, rows, span), 'final', [((3, rows, ch...]
  transfers between devices with their start and end apart: 7 -> 7, of which waited for: 5 -> 6; matrix products, arithmetic and copies ran while one was open for 0% -> 0% of each run, Pallas kernels for 21% -> 17%
where the time goes in v4:
time: 58.6 us; the launch traced here: 58.2 us
  starting transfers between devices  23.3 us (40%)
  waiting for transfers between devices  17.7 us (30%)
  Pallas kernels  16.5 us (28%)
  between operations  0.71 us (1%)
    all_to_all x1, starting transfers between devices, per_device(): lax.all_to_all(outgoing, 'ctx', split_axis=0, concat_axis=0, tiled=True)  12.3 us
    all_to_all x1, waiting for transfers between devices, per_device(): lax.all_to_all(outgoing, 'ctx', split_axis=0, concat_axis=0, tiled=True)  7.92 us
    ppermute x2, starting transfers between devices, shift(): return lax.ppermute(block, 'ctx', route)  4.77 us
    all_to_all x1, waiting for transfers between devices, per_device(): lax.all_to_all(parts, 'ctx', 0, 0, tiled=True, axis_index_groups=groups)  4.4 us
    ppermute x3, waiting for transfers between devices, around(): lax.ppermute(block, 'ctx', [(i, i // near * near + (i + hop) % near) for...  4.27 us
    pallas_call x1, Pallas kernels, per_device(): call(functools.partial(local_kernel, steps, span, modes), 'local', [((til...  4.13 us
    pallas_call x1, Pallas kernels, per_device(): call(functools.partial(outputs_kernel, rows, steps, span, modes), 'output...  3.52 us
    all_to_all x1, starting transfers between devices, per_device(): lax.all_to_all(parts, 'ctx', 0, 0, tiled=True, axis_index_groups=groups)  3.41 us
  transfers between devices with their start and end apart: 7, of which 6 were waited for; matrix products, arithmetic and copies ran while one was open for 0% of the time, Pallas kernels for 17%

profile of v4, /device:TPU:2, one launch (start us, length us, event | category | flops | bytes accessed | tf_op | source)
XLA Modules:
  0.0 58.2 jit_solution(5958036644409159309)
XLA Ops:
  0.6 1.4 %load.1 = (bf16[3,16,512]{2,1,0:T(8,128)(2,1)S(1)}, bf16[4,3,256,128]{3,2,1,0:T(8,128)(2,1)S(1)}, bf16[4,256,128]{2,1,0:T(8,128)(2,1)S(1)}, f32[3,7,512]{2,1,0:T...) custom-call(s32[16]{0:T(128)} %lens_hbm.1, ...), custom_call_target="tpu_custom_call" | custom-call | flops 1000000 | bytes 4194304 | tf_op jit(solution)/shard_map/load/pallas_call | solution.py:646
  2.1 3.5 %collective-permute-start = (bf16[3,16,512]{2,1,0:T(8,128)(2,1)S(1)}, bf16[3,16,512]{2,1,0:T(8,128)(2,1)S(1)}, u32[]{:S(2)}, u32[]{:S(2)}) collective-permute-start(bf16[3,16,512]{2,1,0:T(8,128)(2,1)S(1)} %get-tuple-element.42), channel_id=1, source_target_pairs={{0,8},{8,16},{16,24},{24,32},{32,40},{40,48},{48,56},{56,64},{64,7... | collective-permute-start | bytes 147464 | tf_op jit(solution)/shard_map/ppermute | solution.py:23
  5.6 2.3 %edges.1 = (f32[2,8,512]{2,1,0:T(8,128)S(1)}, f32[4,4,8,128]{3,2,1,0:T(8,128)S(1)}, bf16[4,256,512]{2,1,0:T(8,128)(2,1)S(1)}) custom-call(bf16[4,3,256,128]{3,2,1,0:T(8,128)(2,1)S(1)} %get-tuple-element.32.proj_ref, bf16[4,256,128]{2,1,0:T(8,128)(2,1)S(1)} %get-tuple-element.33.cot_ref, f32[3,7,512]{2,1,0:T(8,128)S(1)} %get-tuple-element.34.taps_ref, ...), custom_call_target="tpu_custom_call" | custom-call | flops 40000000 | bytes 4194304 | tf_op jit(solution)/shard_map/edges/pallas_call | solution.py:667
  7.9 0.0 collective-permute-done.left_ref
  7.9 1.0 %rims.1 = (bf16[32,16,256]{2,1,0:T(8,128)(2,1)}, f32[3,8,512]{2,1,0:T(8,128)S(1)}) custom-call(f32[2,8,512]{2,1,0:T(8,128)S(1)} %get-tuple-element.39.edge_ref, f32[4,4,8,128]{3,2,1,0:T(8,128)S(1)} %get-tuple-element.40.rim_ref, f32[3,7,512]{2,1,0:T(8,128)S(1)} %get-tuple-element.34.taps_ref, f32[8,512]{1,0:T(8,128)S(1)} %get-tuple-element.35.pole_ref, ...), custom_call_target="tpu_custom_call" | custom-call | flops 1000000 | bytes 4194304 | tf_op jit(solution)/shard_map/rims/pallas_call | solution.py:686
  8.9 12.3 %all-to-all-start = ((bf16[32,16,256]{2,1,0:T(8,128)(2,1)}), bf16[32,16,256]{2,1,0:T(8,128)(2,1)S(1)}, u32[]{:S(2)}, u32[]{:S(2)}) async-start(bf16[32,16,256]{2,1,0:T(8,128)(2,1)} %get-tuple-element.43), calls=%async_computation | async-start | bytes 524288 | tf_op jit(solution)/shard_map/all_to_all | solution.py:703
  21.2 4.1 %local.1 = (f32[4,2,32,8,128]{4,3,2,1,0:T(8,128)S(1)}, f32[2,8,512]{2,1,0:T(8,128)S(1)}, f32[96,8,128]{2,1,0:T(8,128)S(1)}, f32[4,96,8,128]{3,2,1,0:T(8,128)}, f32[4,32,8,128]{3,2,1,0:T(8,128)}) custom-call(bf16[4,256,512]{2,1,0:T(8,128)(2,1)S(1)} %get-tuple-element.37.tokens_ref, f32[3,8,512]{2,1,0:T(8,128)S(1)} %get-tuple-element.44.left_ref, ...), custom_call_target="tpu_custom_call" | custom-call | flops 60000000 | bytes 4194304 | tf_op jit(solution)/shard_map/local/pallas_call | solution.py:705
  25.4 7.9 %all-to-all-done.states_ref = bf16[32,16,256]{2,1,0:T(8,128)(2,1)S(1)} async-done(((bf16[32,16,256]{2,1,0:T(8,128)(2,1)}), bf16[32,16,256]{2,1,0:T(8,128)(2,1)S(1)}, u32[]{:S(2)}, u32[]{:S(2)}) %all-to-all-start) | async-done | bytes 262176 | tf_op jit(solution)/shard_map/all_to_all | solution.py:703
  33.3 2.6 %sums.1 = (bf16[32,512]{1,0:T(8,128)(2,1)S(1)}, bf16[3,16,512]{2,1,0:T(8,128)(2,1)S(1)}) custom-call(bf16[4,256,512]{2,1,0:T(8,128)(2,1)S(1)} %get-tuple-element.37.tokens_ref, f32[3,8,512]{2,1,0:T(8,128)S(1)} %get-tuple-element.44.left_ref, f32[8,512]{1,0:T(8,128)S(1)} %get-tuple-element.35.pole_ref, f32[44,8,128]{2,1,0:T(8,128)S(1)} %get-tuple-element.36.keep_ref, ...), custom_call_target="tpu_custom_call" | custom-call | flops 30000000 | bytes 4194304 | tf_op jit(solution)/shard_map/sums/pallas_call | solution.py:728
  35.9 1.2 %collective-permute-start.3 = (bf16[32,512]{1,0:T(8,128)(2,1)S(1)}, bf16[32,512]{1,0:T(8,128)(2,1)S(1)}, u32[]{:S(2)}, u32[]{:S(2)}) collective-permute-start(bf16[32,512]{1,0:T(8,128)(2,1)S(1)} %get-tuple-element.53.own_ref), channel_id=1, source_target_pairs={{0,24},{8,0},{16,8},{24,16},{32,56},{40,32},{48,40},{56,48},{64,88... | collective-permute-start | bytes 98312 | tf_op jit(solution)/shard_map/ppermute | solution.py:759
  37.1 0.7 %collective-permute-start.2 = (bf16[32,512]{1,0:T(8,128)(2,1)S(1)}, bf16[32,512]{1,0:T(8,128)(2,1)S(1)}, u32[]{:S(2)}, u32[]{:S(2)}) collective-permute-start(bf16[32,512]{1,0:T(8,128)(2,1)S(1)} %get-tuple-element.53.own_ref), channel_id=1, source_target_pairs={{0,16},{8,24},{16,0},{24,8},{32,48},{40,56},{48,32},{56,40},{64,80... | collective-permute-start | bytes 98312 | tf_op jit(solution)/shard_map/ppermute | solution.py:759
  37.8 0.9 %collective-permute-start.1 = (bf16[32,512]{1,0:T(8,128)(2,1)S(1)}, bf16[32,512]{1,0:T(8,128)(2,1)S(1)}, u32[]{:S(2)}, u32[]{:S(2)}) collective-permute-start(bf16[32,512]{1,0:T(8,128)(2,1)S(1)} %get-tuple-element.53.own_ref), channel_id=1, source_target_pairs={{0,8},{8,16},{16,24},{24,0},{32,40},{40,48},{48,56},{56,32},{64,72... | collective-permute-start | bytes 98312 | tf_op jit(solution)/shard_map/ppermute | solution.py:759
  38.7 1.2 %collective-permute-done.3.three_ref = bf16[32,512]{1,0:T(8,128)(2,1)S(1)} collective-permute-done((bf16[32,512]{1,0:T(8,128)(2,1)S(1)}, bf16[32,512]{1,0:T(8,128)(2,1)S(1)}, u32[]{:S(2)}, u32[]{:S(2)}) %collective-permute-start.3) | collective-permute-done | bytes 32800 | tf_op jit(solution)/shard_map/ppermute | solution.py:759
  39.9 2.6 %collective-permute-done.2.two_ref = bf16[32,512]{1,0:T(8,128)(2,1)S(1)} collective-permute-done((bf16[32,512]{1,0:T(8,128)(2,1)S(1)}, bf16[32,512]{1,0:T(8,128)(2,1)S(1)}, u32[]{:S(2)}, u32[]{:S(2)}) %collective-permute-start.2) | collective-permute-done | bytes 32800 | tf_op jit(solution)/shard_map/ppermute | solution.py:759
  42.5 0.5 collective-permute-done.1.one_ref
  43.0 0.7 %spread.1 = bf16[8,32,512]{2,1,0:T(8,128)(2,1)} custom-call(bf16[32,512]{1,0:T(8,128)(2,1)S(1)} %collective-permute-done.1.one_ref, bf16[32,512]{1,0:T(8,128)(2,1)S(1)} %collective-permute-done.2.two_ref, bf16[32,512]{1,0:T(8,128)(2,1)S(1)} %collective-permute-done.3.three_ref, bf16[32,512]{1,0:T(8,128)(2,1)S(1)} %get-tuple-element.53.own_ref), custom_call_target="tpu_custom_call" | custom-call | flops 100000 | bytes 4194304 | tf_op jit(solution)/shard_map/spread/pallas_call | solution.py:763
  43.7 3.4 %all-to-all-start.1 = ((bf16[8,32,512]{2,1,0:T(8,128)(2,1)}), bf16[8,32,512]{2,1,0:T(8,128)(2,1)S(1)}, u32[]{:S(2)}, u32[]{:S(2)}) async-start(bf16[8,32,512]{2,1,0:T(8,128)(2,1)} %spread.1), calls=%async_computation.1 | async-start | bytes 524288 | tf_op jit(solution)/shard_map/all_to_all | solution.py:767
  47.1 1.3 %collective-permute-start.4 = (bf16[3,16,512]{2,1,0:T(8,128)(2,1)S(1)}, bf16[3,16,512]{2,1,0:T(8,128)(2,1)S(1)}, u32[]{:S(2)}, u32[]{:S(2)}) collective-permute-start(bf16[3,16,512]{2,1,0:T(8,128)(2,1)S(1)} %get-tuple-element.55), channel_id=1, source_target_pairs={{8,0},{16,8},{24,16},{32,24},{40,32},{48,40},{56,48},{64,56},{72,6... | collective-permute-start | bytes 147464 | tf_op jit(solution)/shard_map/ppermute | solution.py:23
  48.4 3.5 %outputs.1 = (bf16[256,512]{1,0:T(8,128)(2,1)}, bf16[3,256,512]{2,1,0:T(8,128)(2,1)}, f32[3,16,512]{2,1,0:T(8,128)S(1)}, f32[6,8,128]{2,1,0:T(8,128)S(1)}) custom-call(bf16[4,256,512]{2,1,0:T(8,128)(2,1)S(1)} %get-tuple-element.37.tokens_ref, f32[3,7,512]{2,1,0:T(8,128)S(1)} %get-tuple-element.34.taps_ref, f32[8,512]{1,0:T(8,128)S(1)} %get-tuple-element.35.pole_ref, ...), custom_call_target="tpu_custom_call" | custom-call | flops 40000000 | bytes 4194304 | tf_op jit(solution)/shard_map/outputs/pallas_call | solution.py:768
  51.9 1.2 %collective-permute-done.4.rim_ref = bf16[3,16,512]{2,1,0:T(8,128)(2,1)S(1)} collective-permute-done((bf16[3,16,512]{2,1,0:T(8,128)(2,1)S(1)}, bf16[3,16,512]{2,1,0:T(8,128)(2,1)S(1)}, u32[]{:S(2)}, u32[]{:S(2)}) %collective-permute-start.4) | collective-permute-done | bytes 49184 | tf_op jit(solution)/shard_map/ppermute | solution.py:23
  53.1 4.4 %all-to-all-done.1.parts_ref = bf16[8,32,512]{2,1,0:T(8,128)(2,1)S(1)} async-done(((bf16[8,32,512]{2,1,0:T(8,128)(2,1)}), bf16[8,32,512]{2,1,0:T(8,128)(2,1)S(1)}, u32[]{:S(2)}, u32[]{:S(2)}) %all-to-all-start.1) | async-done | bytes 262176 | tf_op jit(solution)/shard_map/all_to_all | solution.py:767
  57.5 0.7 %final.1 = (bf16[3,256,512]{2,1,0:T(8,128)(2,1)}, f32[3,7,512]{2,1,0:T(8,128)}, f32[8,512]{1,0:T(8,128)}) custom-call(bf16[3,256,512]{2,1,0:T(8,128)(2,1)} %get-tuple-element.51.partial_hbm, bf16[8,32,512]{2,1,0:T(8,128)(2,1)S(1)} %all-to-all-done.1.parts_ref, f32[3,16,512]{2,1,0:T(8,128)S(1)} %get-tuple-element.54.tail_ref, ...), custom_call_target="tpu_custom_call", output_to_operand_aliasing={{0}: (0, {})} | custom-call | flops 500000 | bytes 4194304 | tf_op jit(solution)/shard_map/final/pallas_call | solution.py:801
Async XLA Ops:
  2.1 5.8 %collective-permute-start = (bf16[3,16,512]{2,1,0:T(8,128)(2,1)S(1)}, bf16[3,16,512]{2,1,0:T(8,128)(2,1)S(1)}, u32[]{:S(2)}, u32[]{:S(2)}) collective-permute-start(bf16[3,16,512]{2,1,0:T(8,128)(2,1)S(1)} %get-tuple-element.42), channel_id=1, source_target_pairs={{0,8},{8,16},{16,24},{24,32},{32,40},{40,48},{48,56},{56,64},{64,7... | collective-permute-start | bytes 147464 | tf_op jit(solution)/shard_map/ppermute | solution.py:23
  8.9 24.4 %all-to-all-start = ((bf16[32,16,256]{2,1,0:T(8,128)(2,1)}), bf16[32,16,256]{2,1,0:T(8,128)(2,1)S(1)}, u32[]{:S(2)}, u32[]{:S(2)}) async-start(bf16[32,16,256]{2,1,0:T(8,128)(2,1)} %get-tuple-element.43), calls=%async_computation | async-start | bytes 524288 | tf_op jit(solution)/shard_map/all_to_all | solution.py:703
  35.9 4.0 %collective-permute-start.3 = (bf16[32,512]{1,0:T(8,128)(2,1)S(1)}, bf16[32,512]{1,0:T(8,128)(2,1)S(1)}, u32[]{:S(2)}, u32[]{:S(2)}) collective-permute-start(bf16[32,512]{1,0:T(8,128)(2,1)S(1)} %get-tuple-element.53.own_ref), channel_id=1, source_target_pairs={{0,24},{8,0},{16,8},{24,16},{32,56},{40,32},{48,40},{56,48},{64,88... | collective-permute-start | bytes 98312 | tf_op jit(solution)/shard_map/ppermute | solution.py:759
  37.1 5.4 %collective-permute-start.2 = (bf16[32,512]{1,0:T(8,128)(2,1)S(1)}, bf16[32,512]{1,0:T(8,128)(2,1)S(1)}, u32[]{:S(2)}, u32[]{:S(2)}) collective-permute-start(bf16[32,512]{1,0:T(8,128)(2,1)S(1)} %get-tuple-element.53.own_ref), channel_id=1, source_target_pairs={{0,16},{8,24},{16,0},{24,8},{32,48},{40,56},{48,32},{56,40},{64,80... | collective-permute-start | bytes 98312 | tf_op jit(solution)/shard_map/ppermute | solution.py:759
  37.8 5.1 %collective-permute-start.1 = (bf16[32,512]{1,0:T(8,128)(2,1)S(1)}, bf16[32,512]{1,0:T(8,128)(2,1)S(1)}, u32[]{:S(2)}, u32[]{:S(2)}) collective-permute-start(bf16[32,512]{1,0:T(8,128)(2,1)S(1)} %get-tuple-element.53.own_ref), channel_id=1, source_target_pairs={{0,8},{8,16},{16,24},{24,0},{32,40},{40,48},{48,56},{56,32},{64,72... | collective-permute-start | bytes 98312 | tf_op jit(solution)/shard_map/ppermute | solution.py:759
  43.7 13.8 %all-to-all-start.1 = ((bf16[8,32,512]{2,1,0:T(8,128)(2,1)}), bf16[8,32,512]{2,1,0:T(8,128)(2,1)S(1)}, u32[]{:S(2)}, u32[]{:S(2)}) async-start(bf16[8,32,512]{2,1,0:T(8,128)(2,1)} %spread.1), calls=%async_computation.1 | async-start | bytes 524288 | tf_op jit(solution)/shard_map/all_to_all | solution.py:767
  47.1 6.0 %collective-permute-start.4 = (bf16[3,16,512]{2,1,0:T(8,128)(2,1)S(1)}, bf16[3,16,512]{2,1,0:T(8,128)(2,1)S(1)}, u32[]{:S(2)}, u32[]{:S(2)}) collective-permute-start(bf16[3,16,512]{2,1,0:T(8,128)(2,1)S(1)} %get-tuple-element.55), channel_id=1, source_target_pairs={{8,0},{16,8},{24,16},{32,24},{40,32},{48,40},{56,48},{64,56},{72,6... | collective-permute-start | bytes 147464 | tf_op jit(solution)/shard_map/ppermute | solution.py:23

commit v5 on v4

--- a/solution.py
+++ b/solution.py
@@ -416,8 +416,8 @@
 def sums_kernel(
     rows, steps, span, modes,
     tokens_ref, left_ref, pole_ref, keep_ref, pick_ref, states_ref, feat_ref, res_ref, pack_first_ref, pack_hbm,
-    out_ref, rim_ref,
-    pack_ref, same_ref, cum_ref, chunk_ref, coming_ref, grad_ref, sums_ref, line_ref, tile_sem,
+    out_hbm, rim_ref,
+    pack_ref, same_ref, cum_ref, chunk_ref, coming_ref, grad_ref, sums_ref, line_ref, total_ref, tile_sem, out_sem,
 ):
     tiles = feat_ref.shape[0]
     shards = states_ref.shape[0]
@@ -479,7 +479,12 @@
     pole = pole_ref[...]
     back = jnp.concatenate([coming_ref[n, 1] for n in range(tiles)], axis=1)
     res = (res_ref[0] + res_ref[1] * back) * jnp.sqrt(1.0 - pole * pole)
-    out_ref[...] = (jnp.concatenate([taps, res], axis=0) * scale).astype(BF16)
+    total_ref[...] = (jnp.concatenate([taps, res], axis=0) * scale).astype(BF16)
+    copies = [pltpu.make_async_copy(total_ref, out_hbm.at[g], out_sem.at[g]) for g in range(out_hbm.shape[0])]
+    for copy in copies:
+        copy.start()
+    for copy in copies:
+        copy.wait()
 
 
 def outputs_kernel(
@@ -564,15 +569,13 @@
             tail_mask_ref[j - 1, pl.ds(r, 1), :] = same_ref[j - 1, steps + r, pl.ds(SUB - 1, 1), :]
 
 
-def spread_kernel(one_ref, two_ref, three_ref, own_ref, out_ref):
-    own, one, two, three = (ref[...].astype(F32) for ref in (own_ref, one_ref, two_ref, three_ref))
-    total = ((own + two) + (one + three)).astype(BF16)
-    for g in range(out_ref.shape[0]):
-        out_ref[g] = total
+def far_kernel(parts_ref, after_ref, out_ref):
+    del after_ref
+    out_ref[...] = total_of(parts_ref[g].astype(F32) for g in range(parts_ref.shape[0])).astype(BF16)
 
 
 def final_kernel(
-    rows, span, partial_hbm, parts_ref, tail_ref, rim_ref, taps_ref, mask_ref,
+    rows, span, partial_hbm, own_ref, one_ref, two_ref, three_ref, tail_ref, rim_ref, taps_ref, mask_ref,
     grad_proj_hbm, tap_hbm, res_hbm,
     line_ref, tap_ref, res_ref, sem,
 ):
@@ -589,7 +592,8 @@
             line_ref[i, :, at] = whole.astype(BF16)
     copies = [pltpu.make_async_copy(line_ref, grad_proj_hbm.at[:, pl.ds(rows - HALO, HALO), :], sem.at[0])]
     copies[0].start()
-    total = total_of(parts_ref[g].astype(F32) for g in range(parts_ref.shape[0]))
+    own, one, two, three = (ref[...].astype(F32) for ref in (own_ref, one_ref, two_ref, three_ref))
+    total = (own + two) + (one + three)
     for i in range(3):
         tap_ref[i] = total[i * SUB : i * SUB + tap_ref.shape[1]]
     res_ref[...] = total[3 * SUB :]
@@ -611,6 +615,8 @@
     steps = rows // SUB
     tiles = chans // LANES
     full_steps = steps + span
+    near = 4
+    far = shards // near
     pack_shape = (tiles, 2 * steps + 4 * modes, SUB, LANES)
     query_shape = (tiles, steps, SUB, LANES)
 
@@ -728,7 +734,7 @@
     sums, ahead = call(
         functools.partial(sums_kernel, rows, steps, span, modes),
         "sums",
-        [((SUM_ROWS, chans), BF16, free), ((3, HALO, chans), BF16, free)],
+        [((far, SUM_ROWS, chans), BF16, pltpu.HBM), ((3, HALO, chans), BF16, free)],
         [vmem] * 9 + [hbm],
         [
             pltpu.VMEM(pack_shape, F32),
@@ -739,7 +745,9 @@
             pltpu.VMEM((3, steps, SUB, LANES), F32),
             pltpu.VMEM((3 * SUB * SUB, chans), F32),
             pltpu.VMEM((3, HALO, chans), F32),
+            pltpu.VMEM((SUM_ROWS, chans), BF16),
             dma((tiles,)),
+            dma((far,)),
         ],
         12,
         30_000_000,
@@ -752,19 +760,14 @@
 
     behind = shift(ahead, -1)
 
-    near = 4
-    far = shards // near
 
     def around(block, hop):
         return lax.ppermute(
             block, "ctx", [(i, i // near * near + (i + hop) % near) for i in range(shards)]
         )
 
-    (parts,) = call(
-        spread_kernel, "spread", [((far, SUM_ROWS, chans), BF16, pltpu.VMEM)], [vmem] * 4, [], 4, 100_000
-    )(*(around(sums, hop) for hop in (1, 2, 3)), sums)
     groups = [[f * near + n for f in range(far)] for n in range(near)]
-    gathered = lax.all_to_all(parts, "ctx", 0, 0, tiled=True, axis_index_groups=groups)
+    gathered = lax.all_to_all(sums, "ctx", 0, 0, tiled=True, axis_index_groups=groups)
     gated, grad_proj, tail, tail_mask = call(
         functools.partial(outputs_kernel, rows, steps, span, modes),
         "outputs",
@@ -798,6 +801,11 @@
         *in_vmem(feats, pack_first),
         *in_hbm(pack, query),
     )
+    (sums,) = call(far_kernel, "far", [((SUM_ROWS, chans), BF16, free)], [vmem] * 2, [], 4, 100_000)(
+        gathered, *in_vmem(tail_mask)
+    )
+    near_sums = [sums] + [around(sums, hop) for hop in (1, 2, 3)]
+
     grad_proj, grad_tap, grad_res = call(
         functools.partial(final_kernel, rows, span),
         "final",
@@ -806,7 +814,7 @@
             ((3, taps, chans), F32, pltpu.HBM),
             ((modes, chans), F32, pltpu.HBM),
         ],
-        [hbm] + [vmem] * 5,
+        [hbm] + [vmem] * 8,
         [
             pltpu.VMEM((3, HALO, chans), BF16),
             pltpu.VMEM((3, taps, chans), F32),
@@ -816,7 +824,7 @@
         4,
         500_000,
         aliases={0: 0},
-    )(*in_hbm(grad_proj), gathered, *in_vmem(tail), behind, *in_vmem(taps_near, tail_mask))
+    )(*in_hbm(grad_proj), *near_sums, *in_vmem(tail), behind, *in_vmem(taps_near, tail_mask))
     return (gated, grad_proj, grad_tap, grad_res)
 
 

time: 58.6 us -> 58.2 us (level)
  waiting for transfers between devices: 17.7 us -> 16 us
  starting transfers between devices: 23.3 us -> 24.5 us
    ppermute x3, waiting for transfers between devices: 4.27 us -> 2.56 us  [around(): lax.ppermute(block, 'ctx', [(i, i // near * near + (i + hop) % near) for...]
    ppermute x3, starting transfers between devices: 2.8 us -> 4 us  [around(): lax.ppermute(block, 'ctx', [(i, i // near * near + (i + hop) % near) for...]
    all_to_all x1, waiting for transfers between devices: 4.4 us -> 5.56 us  [per_device(): lax.all_to_all(sums, 'ctx', 0, 0, tiled=True, axis_index_groups=groups)]
    ppermute x2, waiting for transfers between devices: 1.16 us -> 0.01 us  [shift(): return lax.ppermute(block, 'ctx', route)]
    pallas_call x1, Pallas kernels: 2.62 us -> 3.39 us  [per_device(): call(functools.partial(sums_kernel, rows, steps, span, modes), 'sums', [(...]
    pallas_call x1, Pallas kernels: 0.73 us -> 0.04 us  [per_device(): call(far_kernel, 'far', [((SUM_ROWS, chans), BF16, free)], [vmem] * 2, []...]
  transfers between devices with their start and end apart: 7 -> 7, of which waited for: 6 -> 5; matrix products, arithmetic and copies ran while one was open for 0% -> 0% of each run, Pallas kernels for 17% -> 17%
where the time goes in v5:
time: 58.2 us; the launch traced here: 57.8 us
  starting transfers between devices  24.5 us (42%)
  Pallas kernels  16.5 us (28%)
  waiting for transfers between devices  16 us (27%)
  between operations  0.72 us (1%)
    all_to_all x1, starting transfers between devices, per_device(): lax.all_to_all(outgoing, 'ctx', split_axis=0, concat_axis=0, tiled=True)  12.3 us
    all_to_all x1, waiting for transfers between devices, per_device(): lax.all_to_all(outgoing, 'ctx', split_axis=0, concat_axis=0, tiled=True)  7.92 us
    all_to_all x1, waiting for transfers between devices, per_device(): lax.all_to_all(sums, 'ctx', 0, 0, tiled=True, axis_index_groups=groups)  5.56 us
    ppermute x2, starting transfers between devices, shift(): return lax.ppermute(block, 'ctx', route)  4.77 us
    pallas_call x1, Pallas kernels, per_device(): call(functools.partial(local_kernel, steps, span, modes), 'local', [((til...  4.13 us
    ppermute x3, starting transfers between devices, around(): lax.ppermute(block, 'ctx', [(i, i // near * near + (i + hop) % near) for...  4 us
    pallas_call x1, Pallas kernels, per_device(): call(functools.partial(outputs_kernel, rows, steps, span, modes), 'output...  3.52 us
    all_to_all x1, starting transfers between devices, per_device(): lax.all_to_all(sums, 'ctx', 0, 0, tiled=True, axis_index_groups=groups)  3.42 us
  transfers between devices with their start and end apart: 7, of which 5 were waited for; matrix products, arithmetic and copies ran while one was open for 0% of the time, Pallas kernels for 17%

profile of v5, /device:TPU:2, one launch (start us, length us, event | category | flops | bytes accessed | tf_op | source)
XLA Modules:
  0.0 57.8 jit_solution(4987577304949147092)
XLA Ops:
  0.6 1.4 %load.1 = (bf16[3,16,512]{2,1,0:T(8,128)(2,1)S(1)}, bf16[4,3,256,128]{3,2,1,0:T(8,128)(2,1)S(1)}, bf16[4,256,128]{2,1,0:T(8,128)(2,1)S(1)}, f32[3,7,512]{2,1,0:T...) custom-call(s32[16]{0:T(128)} %lens_hbm.1, ...), custom_call_target="tpu_custom_call" | custom-call | flops 1000000 | bytes 4194304 | tf_op jit(solution)/shard_map/load/pallas_call | solution.py:652
  2.1 3.5 %collective-permute-start = (bf16[3,16,512]{2,1,0:T(8,128)(2,1)S(1)}, bf16[3,16,512]{2,1,0:T(8,128)(2,1)S(1)}, u32[]{:S(2)}, u32[]{:S(2)}) collective-permute-start(bf16[3,16,512]{2,1,0:T(8,128)(2,1)S(1)} %get-tuple-element.42), channel_id=1, source_target_pairs={{0,8},{8,16},{16,24},{24,32},{32,40},{40,48},{48,56},{56,64},{64,7... | collective-permute-start | bytes 147464 | tf_op jit(solution)/shard_map/ppermute | solution.py:23
  5.6 2.3 %edges.1 = (f32[2,8,512]{2,1,0:T(8,128)S(1)}, f32[4,4,8,128]{3,2,1,0:T(8,128)S(1)}, bf16[4,256,512]{2,1,0:T(8,128)(2,1)S(1)}) custom-call(bf16[4,3,256,128]{3,2,1,0:T(8,128)(2,1)S(1)} %get-tuple-element.32.proj_ref, bf16[4,256,128]{2,1,0:T(8,128)(2,1)S(1)} %get-tuple-element.33.cot_ref, f32[3,7,512]{2,1,0:T(8,128)S(1)} %get-tuple-element.34.taps_ref, ...), custom_call_target="tpu_custom_call" | custom-call | flops 40000000 | bytes 4194304 | tf_op jit(solution)/shard_map/edges/pallas_call | solution.py:673
  7.9 0.0 collective-permute-done.left_ref
  7.9 1.0 %rims.1 = (bf16[32,16,256]{2,1,0:T(8,128)(2,1)}, f32[3,8,512]{2,1,0:T(8,128)S(1)}) custom-call(f32[2,8,512]{2,1,0:T(8,128)S(1)} %get-tuple-element.39.edge_ref, f32[4,4,8,128]{3,2,1,0:T(8,128)S(1)} %get-tuple-element.40.rim_ref, f32[3,7,512]{2,1,0:T(8,128)S(1)} %get-tuple-element.34.taps_ref, f32[8,512]{1,0:T(8,128)S(1)} %get-tuple-element.35.pole_ref, ...), custom_call_target="tpu_custom_call" | custom-call | flops 1000000 | bytes 4194304 | tf_op jit(solution)/shard_map/rims/pallas_call | solution.py:692
  8.9 12.3 %all-to-all-start = ((bf16[32,16,256]{2,1,0:T(8,128)(2,1)}), bf16[32,16,256]{2,1,0:T(8,128)(2,1)S(1)}, u32[]{:S(2)}, u32[]{:S(2)}) async-start(bf16[32,16,256]{2,1,0:T(8,128)(2,1)} %get-tuple-element.43), calls=%async_computation | async-start | bytes 524288 | tf_op jit(solution)/shard_map/all_to_all | solution.py:709
  21.2 4.1 %local.1 = (f32[4,2,32,8,128]{4,3,2,1,0:T(8,128)S(1)}, f32[2,8,512]{2,1,0:T(8,128)S(1)}, f32[96,8,128]{2,1,0:T(8,128)S(1)}, f32[4,96,8,128]{3,2,1,0:T(8,128)}, f32[4,32,8,128]{3,2,1,0:T(8,128)}) custom-call(bf16[4,256,512]{2,1,0:T(8,128)(2,1)S(1)} %get-tuple-element.37.tokens_ref, f32[3,8,512]{2,1,0:T(8,128)S(1)} %get-tuple-element.44.left_ref, ...), custom_call_target="tpu_custom_call" | custom-call | flops 60000000 | bytes 4194304 | tf_op jit(solution)/shard_map/local/pallas_call | solution.py:711
  25.4 7.9 %all-to-all-done.states_ref = bf16[32,16,256]{2,1,0:T(8,128)(2,1)S(1)} async-done(((bf16[32,16,256]{2,1,0:T(8,128)(2,1)}), bf16[32,16,256]{2,1,0:T(8,128)(2,1)S(1)}, u32[]{:S(2)}, u32[]{:S(2)}) %all-to-all-start) | async-done | bytes 262176 | tf_op jit(solution)/shard_map/all_to_all | solution.py:709
  33.3 3.4 %sums.1 = (bf16[8,32,512]{2,1,0:T(8,128)(2,1)}, bf16[3,16,512]{2,1,0:T(8,128)(2,1)S(1)}) custom-call(bf16[4,256,512]{2,1,0:T(8,128)(2,1)S(1)} %get-tuple-element.37.tokens_ref, f32[3,8,512]{2,1,0:T(8,128)S(1)} %get-tuple-element.44.left_ref, f32[8,512]{1,0:T(8,128)S(1)} %get-tuple-element.35.pole_ref, f32[44,8,128]{2,1,0:T(8,128)S(1)} %get-tuple-element.36.keep_ref, ...), custom_call_target="tpu_custom_call" | custom-call | flops 30000000 | bytes 4194304 | tf_op jit(solution)/shard_map/sums/pallas_call | solution.py:734
  36.7 3.4 %all-to-all-start.1 = ((bf16[8,32,512]{2,1,0:T(8,128)(2,1)}), bf16[8,32,512]{2,1,0:T(8,128)(2,1)S(1)}, u32[]{:S(2)}, u32[]{:S(2)}) async-start(bf16[8,32,512]{2,1,0:T(8,128)(2,1)} %get-tuple-element.53), calls=%async_computation.1 | async-start | bytes 524288 | tf_op jit(solution)/shard_map/all_to_all | solution.py:770
  40.1 1.3 %collective-permute-start.4 = (bf16[3,16,512]{2,1,0:T(8,128)(2,1)S(1)}, bf16[3,16,512]{2,1,0:T(8,128)(2,1)S(1)}, u32[]{:S(2)}, u32[]{:S(2)}) collective-permute-start(bf16[3,16,512]{2,1,0:T(8,128)(2,1)S(1)} %get-tuple-element.56), channel_id=1, source_target_pairs={{8,0},{16,8},{24,16},{32,24},{40,32},{48,40},{56,48},{64,56},{72,6... | collective-permute-start | bytes 147464 | tf_op jit(solution)/shard_map/ppermute | solution.py:23
  41.4 3.5 %outputs.1 = (bf16[256,512]{1,0:T(8,128)(2,1)}, bf16[3,256,512]{2,1,0:T(8,128)(2,1)}, f32[3,16,512]{2,1,0:T(8,128)S(1)}, f32[6,8,128]{2,1,0:T(8,128)S(1)}) custom-call(bf16[4,256,512]{2,1,0:T(8,128)(2,1)S(1)} %get-tuple-element.37.tokens_ref, f32[3,7,512]{2,1,0:T(8,128)S(1)} %get-tuple-element.34.taps_ref, f32[8,512]{1,0:T(8,128)S(1)} %get-tuple-element.35.pole_ref, ...), custom_call_target="tpu_custom_call" | custom-call | flops 40000000 | bytes 4194304 | tf_op jit(solution)/shard_map/outputs/pallas_call | solution.py:771
  44.9 5.6 %all-to-all-done.1.parts_ref = bf16[8,32,512]{2,1,0:T(8,128)(2,1)S(1)} async-done(((bf16[8,32,512]{2,1,0:T(8,128)(2,1)}), bf16[8,32,512]{2,1,0:T(8,128)(2,1)S(1)}, u32[]{:S(2)}, u32[]{:S(2)}) %all-to-all-start.1) | async-done | bytes 262176 | tf_op jit(solution)/shard_map/all_to_all | solution.py:770
  50.5 0.1 collective-permute-start.1
  50.6 2.6 %collective-permute-start.2 = (bf16[32,512]{1,0:T(8,128)(2,1)S(1)}, bf16[32,512]{1,0:T(8,128)(2,1)S(1)}, u32[]{:S(2)}, u32[]{:S(2)}) collective-permute-start(bf16[32,512]{1,0:T(8,128)(2,1)S(1)} %far.1.own_ref), channel_id=1, source_target_pairs={{0,16},{8,24},{16,0},{24,8},{32,48},{40,56},{48,32},{56,40},{64,80... | collective-permute-start | bytes 98312 | tf_op jit(solution)/shard_map/ppermute | solution.py:765
  53.2 1.3 %collective-permute-start.3 = (bf16[32,512]{1,0:T(8,128)(2,1)S(1)}, bf16[32,512]{1,0:T(8,128)(2,1)S(1)}, u32[]{:S(2)}, u32[]{:S(2)}) collective-permute-start(bf16[32,512]{1,0:T(8,128)(2,1)S(1)} %far.1.own_ref), channel_id=1, source_target_pairs={{0,24},{8,0},{16,8},{24,16},{32,56},{40,32},{48,40},{56,48},{64,88... | collective-permute-start | bytes 98312 | tf_op jit(solution)/shard_map/ppermute | solution.py:765
  54.5 0.0 collective-permute-done.4.rim_ref
  54.5 1.2 %collective-permute-done.1.one_ref = bf16[32,512]{1,0:T(8,128)(2,1)S(1)} collective-permute-done((bf16[32,512]{1,0:T(8,128)(2,1)S(1)}, bf16[32,512]{1,0:T(8,128)(2,1)S(1)}, u32[]{:S(2)}, u32[]{:S(2)}) %collective-permute-start.1) | collective-permute-done | bytes 32800 | tf_op jit(solution)/shard_map/ppermute | solution.py:765
  55.7 0.4 collective-permute-done.2.two_ref
  56.1 1.0 %collective-permute-done.3.three_ref = bf16[32,512]{1,0:T(8,128)(2,1)S(1)} collective-permute-done((bf16[32,512]{1,0:T(8,128)(2,1)S(1)}, bf16[32,512]{1,0:T(8,128)(2,1)S(1)}, u32[]{:S(2)}, u32[]{:S(2)}) %collective-permute-start.3) | collective-permute-done | bytes 32800 | tf_op jit(solution)/shard_map/ppermute | solution.py:765
  57.1 0.7 %final.1 = (bf16[3,256,512]{2,1,0:T(8,128)(2,1)}, f32[3,7,512]{2,1,0:T(8,128)}, f32[8,512]{1,0:T(8,128)}) custom-call(bf16[3,256,512]{2,1,0:T(8,128)(2,1)} %get-tuple-element.51.partial_hbm, bf16[32,512]{1,0:T(8,128)(2,1)S(1)} %far.1.own_ref, bf16[32,512]{1,0:T(8,128)(2,1)S(1)} %collective-permute-done.1.one_ref, ...), custom_call_target="tpu_custom_call", output_to_operand_aliasing={{0}: (0, {})} | custom-call | flops 500000 | bytes 4194304 | tf_op jit(solution)/shard_map/final/pallas_call | solution.py:809
  (1 shorter events, 0.0 us)
Async XLA Ops:
  2.1 5.8 %collective-permute-start = (bf16[3,16,512]{2,1,0:T(8,128)(2,1)S(1)}, bf16[3,16,512]{2,1,0:T(8,128)(2,1)S(1)}, u32[]{:S(2)}, u32[]{:S(2)}) collective-permute-start(bf16[3,16,512]{2,1,0:T(8,128)(2,1)S(1)} %get-tuple-element.42), channel_id=1, source_target_pairs={{0,8},{8,16},{16,24},{24,32},{32,40},{40,48},{48,56},{56,64},{64,7... | collective-permute-start | bytes 147464 | tf_op jit(solution)/shard_map/ppermute | solution.py:23
  8.9 24.4 %all-to-all-start = ((bf16[32,16,256]{2,1,0:T(8,128)(2,1)}), bf16[32,16,256]{2,1,0:T(8,128)(2,1)S(1)}, u32[]{:S(2)}, u32[]{:S(2)}) async-start(bf16[32,16,256]{2,1,0:T(8,128)(2,1)} %get-tuple-element.43), calls=%async_computation | async-start | bytes 524288 | tf_op jit(solution)/shard_map/all_to_all | solution.py:709
  36.7 13.8 %all-to-all-start.1 = ((bf16[8,32,512]{2,1,0:T(8,128)(2,1)}), bf16[8,32,512]{2,1,0:T(8,128)(2,1)S(1)}, u32[]{:S(2)}, u32[]{:S(2)}) async-start(bf16[8,32,512]{2,1,0:T(8,128)(2,1)} %get-tuple-element.53), calls=%async_computation.1 | async-start | bytes 524288 | tf_op jit(solution)/shard_map/all_to_all | solution.py:770
  40.1 14.4 %collective-permute-start.4 = (bf16[3,16,512]{2,1,0:T(8,128)(2,1)S(1)}, bf16[3,16,512]{2,1,0:T(8,128)(2,1)S(1)}, u32[]{:S(2)}, u32[]{:S(2)}) collective-permute-start(bf16[3,16,512]{2,1,0:T(8,128)(2,1)S(1)} %get-tuple-element.56), channel_id=1, source_target_pairs={{8,0},{16,8},{24,16},{32,24},{40,32},{48,40},{56,48},{64,56},{72,6... | collective-permute-start | bytes 147464 | tf_op jit(solution)/shard_map/ppermute | solution.py:23
  50.5 5.2 %collective-permute-start.1 = (bf16[32,512]{1,0:T(8,128)(2,1)S(1)}, bf16[32,512]{1,0:T(8,128)(2,1)S(1)}, u32[]{:S(2)}, u32[]{:S(2)}) collective-permute-start(bf16[32,512]{1,0:T(8,128)(2,1)S(1)} %far.1.own_ref), channel_id=1, source_target_pairs={{0,8},{8,16},{16,24},{24,0},{32,40},{40,48},{48,56},{56,32},{64,72... | collective-permute-start | bytes 98312 | tf_op jit(solution)/shard_map/ppermute | solution.py:765
  50.6 5.5 %collective-permute-start.2 = (bf16[32,512]{1,0:T(8,128)(2,1)S(1)}, bf16[32,512]{1,0:T(8,128)(2,1)S(1)}, u32[]{:S(2)}, u32[]{:S(2)}) collective-permute-start(bf16[32,512]{1,0:T(8,128)(2,1)S(1)} %far.1.own_ref), channel_id=1, source_target_pairs={{0,16},{8,24},{16,0},{24,8},{32,48},{40,56},{48,32},{56,40},{64,80... | collective-permute-start | bytes 98312 | tf_op jit(solution)/shard_map/ppermute | solution.py:765
  53.2 3.9 %collective-permute-start.3 = (bf16[32,512]{1,0:T(8,128)(2,1)S(1)}, bf16[32,512]{1,0:T(8,128)(2,1)S(1)}, u32[]{:S(2)}, u32[]{:S(2)}) collective-permute-start(bf16[32,512]{1,0:T(8,128)(2,1)S(1)} %far.1.own_ref), channel_id=1, source_target_pairs={{0,24},{8,0},{16,8},{24,16},{32,56},{40,32},{48,40},{56,48},{64,88... | collective-permute-start | bytes 98312 | tf_op jit(solution)/shard_map/ppermute | solution.py:765
